TPU v7x, 32 devices: a whole 2x2x4 slice. The times are simulated.
32 devices in a mesh: row: 4 (over y, x), col: 8 (over z, core).
Axes of the slice: x: 2, y: 2, z: 4, core: 2. Of those that a mesh axis runs over, the one named last changes fastest.
Arguments:
- tokens: bfloat16 [1024, 8192], P('row', 'col'), may hold values from -6 to 6
- w_in: bfloat16 [8192, 3, 8192], P('row', None, 'col'), may hold values from -0.0625 to 0.0625
- filt_in: float32 [7, 3, 8192], P(None, None, 'col'), may hold values from -2.4 to 2.4
- filt_mix: float32 [7, 8192], P(None, 'col'), may hold values from -2.4 to 2.4
Outputs:
- gated: bfloat16 [1024, 8192], P('row', 'col')
All inputs are finite; a program needn't handle non-finite values.
Results may differ from a plain program's by a relative error of at most 0.0064.
Values may be sent and summed in bfloat16 or wider, within the bound.
No kernel may reach another device: no remote copies, remote signals or barrier semaphores. Data moves between devices by JAX's collectives and lax.ppermute only.
A program may use at most 128 MiB of HBM per device.

v0:
```python
import jax
import jax.numpy as jnp
from jax import lax
from jax.sharding import PartitionSpec as P


def passed_along(block, axis, distance):
    devices = range(lax.axis_size(axis))
    route = [(i - distance, i) for i in devices if i - distance in devices]
    return lax.ppermute(block, axis, route)


def taps(ext, filt, count):
    total = filt[0] * ext[6 : 6 + count]
    for shift_s in range(1, 7):
        total = total + filt[shift_s] * ext[6 - shift_s : 6 - shift_s + count]
    return total


def per_device(tokens, w_in, filt_in, filt_mix):
    rows = tokens.shape[0]
    cols = w_in.shape[2]
    strip = lax.all_gather(tokens, "col", axis=1, tiled=True)
    piece = lax.all_gather(w_in, "row", axis=0, tiled=True)
    flat_piece = piece.reshape(piece.shape[0], 3 * cols)
    summed = jnp.dot(strip, flat_piece, preferred_element_type=jnp.float32)
    proj = summed.astype(jnp.bfloat16).reshape(rows, 3, cols)
    starts_seq = lax.axis_index("row") == 0
    keep_f = jnp.where(starts_seq, 0.0, 1.0).astype(jnp.float32)
    rim = passed_along(proj[rows - 6 :], "row", 1)
    ext = jnp.concatenate([rim.astype(jnp.float32) * keep_f, proj.astype(jnp.float32)], axis=0)
    conv = taps(ext, filt_in, rows)
    prod = conv[:, 1] * conv[:, 2]
    prod_rim = passed_along(prod[rows - 6 :], "row", 1)
    ext_prod = jnp.concatenate([prod_rim * keep_f, prod], axis=0)
    mix = taps(ext_prod, filt_mix, rows)
    query = conv[:, 0]
    return (query * mix).astype(jnp.bfloat16)


def solution(mesh):
    return jax.shard_map(
        per_device,
        mesh=mesh,
        in_specs=(P("row", "col"), P("row", None, "col"), P(None, None, "col"), P(None, "col")),
        out_specs=P("row", "col"),
        check_vma=False,
    )
```

profile of v0, /device:TPU:0, one launch (start us, length us, event | category | flops | bytes accessed | tf_op | source)
XLA Modules:
  0.0 563.6 jit_solution(2509420352518564781)
XLA Ops:
  6.5 0.0 all-gather.3.cloned.1.call-start
  6.5 0.7 all-gather.3.cloned.1.call-update
  7.3 0.0 all-gather.5.cloned.1.call-start
  7.3 17.0 %copy.18 = bf16[2048,3,1024]{0,2,1:T(8,128)(2,1)} copy(bf16[2048,3,1024]{2,0,1:T(8,128)(2,1)} %param.5) | data formatting | bytes 25165824 | tf_op args[1]
  24.3 0.0 all-gather.5.cloned.1.call-update
  24.3 0.9 copy-done.1
  25.2 0.1 fusion.36
  25.3 33.5 %all-gather.3.cloned.1.call-done = bf16[256,8192]{1,0:T(8,128)(2,1)} async-done(((bf16[256,1024]{1,0:T(8,128)(2,1)}), bf16[256,8192]{1,0:T(8,128)(2,1)}) %all-gather.3.cloned.1.call-update) | async-done | bytes 4194320 | tf_op jit(solution)/shard_map/all_gather | solution.py:23
  58.8 437.6 %all-gather.5.cloned.1.call-done = bf16[8192,3,1024]{0,2,1:T(8,128)(2,1)} async-done(((bf16[2048,3,1024]{0,2,1:T(8,128)(2,1)}), bf16[8192,3,1024]{0,2,1:T(8,128)(2,1)}) %all-gather.5.cloned.1.call-update) | async-done | bytes 50331664 | tf_op jit(solution)/shard_map/all_gather | solution.py:24
  496.5 21.1 %convolution_convert_fusion = bf16[256,3072]{1,0:T(8,128)(2,1)S(1)} fusion(bf16[256,8192]{1,0:T(8,128)(2,1)} %all-gather.3.cloned.1.call-done, bf16[8192,3072]{0,1:T(8,128)(2,1)} %bitcast.45), kind=kOutput, calls=%fused_computation.10 | convolution fusion | flops 12885688320 | bytes 56098816 | tf_op jit(solution)/shard_map/dot_general | solution.py:26
  517.6 0.0 copy-start
  517.6 3.4 collective-permute-start
  521.0 0.0 copy-done.2
  521.1 1.7 copy.19
  522.8 0.0 collective-permute-done
  522.8 1.7 copy.21
  524.5 12.9 %fusion.3 = f32[256,3,1024]{0,2,1:T(8,128)S(1)} fusion(f32[256,3,1024]{0,2,1:T(8,128)S(1)} %bitcast.35, f32[6,3,1024]{0,2,1:T(8,128)} %copy.21, f32[3,1024]{1,0:T(4,128)S(1)} %get-tuple-element.19, f32[3,1024]{1,0:T(4,128)S(1)} %get-tuple-element.20, f32[3,1024]{1,0:T(4,128)S(1)} %get-tuple-element.21, f32[3,1024]{1,0:T(4,128)S(1)} %get-tuple-element.22, ...), kind=kLoop, calls=%fused_computation.19 | loop fusion | flops 14942208 | bytes 6451200 | tf_op jit(solution)/shard_map/add | solution.py:16
  537.4 0.1 slice_multiply_fusion
  537.6 0.2 slice_bitcast_fusion.1
  537.8 4.2 collective-permute-start.1
  542.0 0.1 fusion.40
  542.1 9.9 %collective-permute-done.1 = f32[6,1024]{0,1:T(8,128)S(1)} collective-permute-done((f32[6,1024]{0,1:T(8,128)S(1)}, f32[6,1024]{0,1:T(8,128)S(1)}, u32[]{:S(2)}, u32[]{:S(2)}) %collective-permute-start.1) | collective-permute-done | bytes 24608 | tf_op jit(solution)/shard_map/ppermute | solution.py:10
  552.1 3.7 fusion.22
  555.7 1.0 copy.22
  (11 shorter events, 0.1 us)
Async XLA Ops:
  6.5 52.3 %all-gather.3.cloned.1.call-start = ((), (), s32[]{:S(2)}) async-start(), calls=%async_computation | async-start | bytes 4718592 | tf_op jit(solution)/shard_map/all_gather | solution.py:23
  7.3 489.2 %all-gather.5.cloned.1.call-start = ((), (), s32[]{:S(2)}) async-start(), calls=%async_computation.1 | async-start | bytes 62914560 | tf_op jit(solution)/shard_map/all_gather | solution.py:24
  24.3 0.9 copy-start.1
  496.5 24.5 %copy-start.2 = (f32[7,1024]{1,0:T(8,128)S(1)}, f32[7,1024]{1,0:T(8,128)}, u32[]{:S(2)}) copy-start(f32[7,1024]{1,0:T(8,128)} %param.7) | copy-start | bytes 86020
  517.6 3.5 copy-start
  517.6 5.2 collective-permute-start
  537.8 14.3 %collective-permute-start.1 = (f32[6,1024]{0,1:T(8,128)S(1)}, f32[6,1024]{0,1:T(8,128)S(1)}, u32[]{:S(2)}, u32[]{:S(2)}) collective-permute-start(f32[6,1024]{0,1:T(8,128)S(1)} %slice_bitcast_fusion.1), channel_id=1, source_target_pairs={{0,8},{8,16},{16,24},{1,9},{9,17},{17,25},{2,10},{10,18},{18,26},{... | collective-permute-start | bytes 73736 | tf_op jit(solution)/shard_map/ppermute | solution.py:10
Sparse Core Ops, SparseCore 0:
  9.0 49.8 all-gather.2
  60.7 435.7 all-gather.4
where the time goes:
time: 566 us; the launch traced here: 564 us
  waiting for transfers between devices  482 us (85%)
  local copies, waits for them, and re-layouts  22.6 us (4%)
  matrix products  21.1 us (4%)
  other arithmetic  16.9 us (3%)
  between operations  13.6 us (2%)
  starting transfers between devices  7.61 us (1%)
    all_gather x1, waiting for transfers between devices, per_device(): piece = lax.all_gather(w_in, 'row', axis=0, tiled=True)  438 us
    all_gather x1, waiting for transfers between devices, per_device(): strip = lax.all_gather(tokens, 'col', axis=1, tiled=True)  33.5 us
    dot_general x1, matrix products, per_device(): summed = jnp.dot(strip, flat_piece, preferred_element_type=jnp.float32)  21.1 us
    unnamed x11, local copies, waits for them, and re-layouts  17.9 us
    add x1, other arithmetic, taps(): total = total + filt[shift_s] * ext[6 - shift_s:6 - shift_s + count]  12.9 us
  transfers between devices with their start and end apart: 4, of which 3 were waited for; matrix products, arithmetic and copies ran while one was open for 3% of the time, Pallas kernels for 0%

commit v1 on v0

v1 whole, which is shorter than its diff:
```python
import functools

import jax
import jax.numpy as jnp
from jax import lax
from jax.experimental import pallas as pl
from jax.experimental.pallas import tpu as pltpu
from jax.sharding import PartitionSpec as P

CORES = 2
RIM = 16
PARTS = 4
LANES = 128
VMEM = pl.BlockSpec(memory_space=pltpu.VMEM)
HBM = pl.BlockSpec(memory_space=pl.ANY)
BF16, F32 = jnp.bfloat16, jnp.float32


def params(mib=16):
    return pltpu.CompilerParams(vmem_limit_bytes=mib * 2**20)


def cost(flops, moved):
    return pl.CostEstimate(flops=flops, bytes_accessed=moved, transcendentals=0)


def side(n):
    x = 1
    while x * x < n:
        x *= 2
    return n // x, x


def shift_rows(block, shape, dy, dx):
    ys, xs = shape
    route = []
    for y in range(ys):
        for x in range(xs):
            route.append((((y + dy) % ys) * xs + (x + dx) % xs, y * xs + x))
    return lax.ppermute(block, "row", route)


def shift_planes(block, dz):
    cols = lax.axis_size("col")
    return lax.ppermute(block, "col", [((c + CORES * dz) % cols, c) for c in range(cols)])


def fetch_kernel(w_ref, o_ref, sem):
    half = o_ref.shape[2]
    core = lax.rem(lax.axis_index("col"), CORES)
    copies = []
    for g in range(3):
        for j in range(2):
            start = pl.multiple_of((core if j == 0 else 1 - core) * half, half)
            copies.append(pltpu.make_async_copy(w_ref.at[g, pl.ds(start, half)], o_ref.at[g, j], sem.at[2 * g + j]))
    for c in copies:
        c.start()
    for c in copies:
        c.wait()


def fetch(w_in):
    w = w_in.transpose(1, 0, 2)
    g, k, n = w.shape
    return pl.pallas_call(
        fetch_kernel,
        in_specs=[HBM],
        out_specs=VMEM,
        out_shape=pltpu.VMEM((g, 2, k // 2, n), BF16),
        scratch_shapes=[pltpu.SemaphoreType.DMA((2 * g,))],
        compiler_params=params(),
        name="fetch_w",
    )(w)


def pick_kernel(shape, *refs):
    ys, xs = shape
    zs = ys * xs
    ins, outs = refs[:zs], refs[zs:]
    me = lax.axis_index("row")
    y, x = me // xs, lax.rem(me, xs)
    z = lax.axis_index("col") // CORES
    for dy in range(ys):
        for dx in range(xs):
            target = lax.rem(y - dy + ys, ys) * xs + lax.rem(x - dx + xs, xs)
            want = lax.rem(target - z + zs, zs)
            for dz in range(zs):

                @pl.when(want == dz)
                def _():
                    outs[dy * xs + dx][...] = ins[dz][...]


def gather_tokens(piece, shape):
    ys, xs = shape
    zs = ys * xs
    strips = [piece] + [shift_planes(piece, dz) for dz in range(1, zs)]
    picked = pl.pallas_call(
        functools.partial(pick_kernel, shape),
        in_specs=[VMEM] * zs,
        out_specs=[VMEM] * zs,
        out_shape=[pltpu.VMEM(piece.shape, BF16)] * zs,
        compiler_params=params(),
        name="pick",
    )(*strips)
    return [picked[0]] + [shift_rows(picked[i], shape, i // xs, i % xs) for i in range(1, zs)]


def stack_kernel(order, *refs):
    ins, out = refs[:-1], refs[-1]
    h = ins[0].shape[0] // 2
    for at, (block, part) in enumerate(order):
        out[at * h : (at + 1) * h] = ins[block][part * h : (part + 1) * h]


def stack(blocks, shape):
    ys, xs = shape
    order = [(dy * xs + dx, 0) for dx in range(1, xs) for dy in range(ys)]
    order += [(dy * xs + dx, 1) for dy in range(1, ys) for dx in range(xs)]
    order += [(dy * xs, 0) for dy in range(ys)] + [(dx, 1) for dx in range(xs)]
    n, e = blocks[0].shape
    return pl.pallas_call(
        functools.partial(stack_kernel, order),
        in_specs=[VMEM] * len(blocks),
        out_specs=VMEM,
        out_shape=pltpu.VMEM((len(blocks) * n, e), BF16),
        compiler_params=params(),
        name="stack",
    )(*blocks)


def project_kernel(tn, mine, other, w_ref, *outs):
    n = w_ref.shape[3]
    for g in range(3):
        for j in range(n // tn):
            cols = slice(j * tn, (j + 1) * tn)
            acc = jnp.dot(mine[...], w_ref[g, 0, :, cols], preferred_element_type=F32)
            acc = acc + jnp.dot(other[...], w_ref[g, 1, :, cols], preferred_element_type=F32)
            at = 0
            for o in outs:
                o[:, g * n + j * tn : g * n + (j + 1) * tn] = acc[at : at + o.shape[0]].astype(o.dtype)
                at += o.shape[0]


def project(mine, other, w, h, shape):
    ys, xs = shape
    m, e = mine.shape
    cols = w.shape[3]
    sizes = [(ys * h, BF16)] * (xs - 1) + [(xs * h, BF16)] * (ys - 1) + [(ys * h, F32), (xs * h, F32)]
    outs = pl.pallas_call(
        functools.partial(project_kernel, min(cols, 256)),
        in_specs=[VMEM] * 3,
        out_specs=[VMEM] * len(sizes),
        out_shape=[pltpu.VMEM((s, 3 * cols), t) for s, t in sizes],
        compiler_params=params(),
        cost_estimate=cost(2 * m * 2 * e * 3 * cols, 2 * w.size),
        name="project",
    )(mine, other, w)
    return outs[: xs - 1], outs[xs - 1 : xs + ys - 2], outs[-2], outs[-1]


def middle_kernel(count_a, count_c, *refs):
    keep_a, got_a = refs[0], refs[1 : 1 + count_a]
    keep_c, got_c = refs[1 + count_a], refs[2 + count_a : 2 + count_a + count_c]
    outs = refs[2 + count_a + count_c :]
    h = outs[0].shape[0]
    for keep, got, mids in ((keep_a, got_a, outs[:count_c]), (keep_c, got_c, outs[count_c:])):
        for i, mid in enumerate(mids, 1):
            total = keep[i * h : (i + 1) * h]
            for g in got:
                total = total + g[i * h : (i + 1) * h].astype(F32)
            mid[...] = total.astype(BF16)


def exchange(outs, h, shape):
    ys, xs = shape
    sent_a, sent_c, keep_a, keep_c = outs
    got_a = [shift_rows(s, shape, 0, -dx) for dx, s in enumerate(sent_a, 1)]
    got_c = [shift_rows(s, shape, -dy, 0) for dy, s in enumerate(sent_c, 1)]
    n = keep_a.shape[1]
    mids = pl.pallas_call(
        functools.partial(middle_kernel, xs - 1, ys - 1),
        in_specs=[VMEM] * (2 + xs - 1 + ys - 1),
        out_specs=[VMEM] * (xs + ys - 2),
        out_shape=[pltpu.VMEM((h, n), BF16)] * (xs + ys - 2),
        compiler_params=params(),
        name="middle",
    )(keep_a, *got_a, keep_c, *got_c)
    last_a = [shift_rows(s, shape, -dy, 0) for dy, s in enumerate(mids[: ys - 1], 1)]
    last_c = [shift_rows(s, shape, 0, -dx) for dx, s in enumerate(mids[ys - 1 :], 1)]
    return [keep_a, *got_a, *last_a], [keep_c, *got_c, *last_c]


def finish_kernel(q, parts, n, count_a, count_c, *refs):
    refs = list(refs)
    terms = [refs[:count_a], refs[count_a : count_a + count_c]]
    del refs[: count_a + count_c]
    fin, fmix = refs.pop(0), refs.pop(0)
    follow = refs.pop(0) if q < parts - 1 else None
    rim = refs.pop(0) if q == 0 else None
    out = refs.pop(0)
    lead = refs.pop(0) if q > 0 else None
    tail = refs.pop(0) if q == parts - 1 else None
    ext, prod = refs
    h = n // 2
    for i, group in enumerate(terms):
        total = group[0][:h]
        for g in group[1:]:
            total = total + g[:h].astype(F32)
        ext[RIM + i * h : RIM + (i + 1) * h] = total
    if follow is not None:
        ext[RIM + n : RIM + n + RIM] = follow[...]
    if rim is not None:
        ext[:RIM] = rim[...].astype(F32)
    if lead is not None:
        lead[...] = ext[RIM : 2 * RIM]
    if tail is not None:
        tail[...] = ext[n : n + RIM].astype(BF16)
    cols = fmix.shape[1]
    first = RIM if q == 0 else 2 * RIM
    rows = out.shape[0]
    step = 48 if rows % 48 == 0 else (40 if rows % 40 == 0 else 16)
    step = min(step, rows)
    if rows % 64 == 0:
        step = 64

    def column(c, _):
        at = pl.multiple_of(c * LANES, LANES)

        def conv(g, start, count):
            where = pl.ds(pl.multiple_of(g * cols + at, LANES), LANES)
            total = fin[g, 0:1, pl.ds(at, LANES)] * ext[start : start + count, where]
            for s in range(1, 7):
                total = total + fin[g, s : s + 1, pl.ds(at, LANES)] * ext[start - s : start - s + count, where]
            return total

        for r in range(0, rows, step):
            base = first + r
            prod[: step + 8] = conv(1, base - 8, step + 8) * conv(2, base - 8, step + 8)
            mix = fmix[0:1, pl.ds(at, LANES)] * prod[8 : 8 + step]
            for s in range(1, 7):
                mix = mix + fmix[s : s + 1, pl.ds(at, LANES)] * prod[8 - s : 8 - s + step]
            out[r : r + step, pl.ds(at, LANES)] = (conv(0, base, step) * mix).astype(BF16)
        return 0

    lax.fori_loop(0, cols // LANES, column, 0)


def finish(q, parts, n, terms_a, terms_c, fin, fmix, follow, rim):
    width = terms_a[0].shape[1]
    cols = fmix.shape[1]
    rows = n + (RIM if q == 0 else 0) - (RIM if q == parts - 1 else 0)
    args = [*terms_a, *terms_c, fin, fmix]
    args += [follow] if q < parts - 1 else []
    args += [rim] if q == 0 else []
    shapes = [pltpu.VMEM((rows, cols), BF16)]
    shapes += [pltpu.VMEM((RIM, width), F32)] if q > 0 else []
    shapes += [pltpu.VMEM((RIM, width), BF16)] if q == parts - 1 else []
    return pl.pallas_call(
        functools.partial(finish_kernel, q, parts, n, len(terms_a), len(terms_c)),
        in_specs=[VMEM] * len(args),
        out_specs=[VMEM] * len(shapes),
        out_shape=shapes,
        scratch_shapes=[pltpu.VMEM((n + 2 * RIM, width), F32), pltpu.VMEM((80, LANES), F32)],
        compiler_params=params(),
        name="finish",
    )(*args)


def per_device(tokens, w_in, filt_in, filt_mix):
    rows = tokens.shape[0]
    cols = lax.axis_size("col")
    count = lax.axis_size("row")
    shape = side(count)
    n = rows // PARTS
    w = fetch(w_in)
    fin = filt_in.transpose(1, 0, 2)
    swap = [(c, c ^ 1) for c in range(cols)]
    outs, follow, rim = [], None, None
    for q in reversed(range(PARTS)):
        blocks = gather_tokens(tokens[q * n : (q + 1) * n], shape)
        mine = stack(blocks, shape)
        other = lax.ppermute(mine, "col", swap)
        sums = project(mine, other, w, n // 2, shape)
        terms_a, terms_c = exchange(sums, n // 2, shape)
        got = list(finish(q, PARTS, n, terms_a, terms_c, fin, filt_mix, follow, rim))
        outs.insert(0, got.pop(0))
        if q > 0:
            follow = got.pop(0)
        if q == PARTS - 1:
            rim = lax.ppermute(got.pop(0), "row", [(i, i + 1) for i in range(count - 1)])
    return jnp.concatenate(outs, axis=0)


def solution(mesh):
    return jax.shard_map(
        per_device,
        mesh=mesh,
        in_specs=(P("row", "col"), P("row", None, "col"), P(None, None, "col"), P(None, "col")),
        out_specs=P("row", "col"),
        check_vma=False,
    )
```

time: 566 us -> 134 us (0.24)
  the two profiles are of different devices: /device:TPU:0 before, /device:TPU:20 now
where the time goes in v1:
time: 134 us
  waiting for transfers between devices  60.3 us (45%)
  starting transfers between devices  46.4 us (35%)
  Pallas kernels  20.1 us (15%)
  local copies, waits for them, and re-layouts  5.72 us (4%)
    ppermute x28, waiting for transfers between devices, shift_rows(): return lax.ppermute(block, 'row', route)  32 us
    ppermute x28, starting transfers between devices, shift_rows(): return lax.ppermute(block, 'row', route)  30.7 us
    ppermute x12, waiting for transfers between devices, shift_planes(): lax.ppermute(block, 'col', [((c + CORES * dz) % cols, c) for c in range(c...  26.3 us
    pallas_call x4, Pallas kernels, project(): pl.pallas_call(functools.partial(project_kernel, min(cols, 256)), in_spec...  13.6 us
    ppermute x12, starting transfers between devices, shift_planes(): lax.ppermute(block, 'col', [((c + CORES * dz) % cols, c) for c in range(c...  12.8 us
    unnamed x6, local copies, waits for them, and re-layouts  4.59 us
    pallas_call x4, Pallas kernels, finish(): pl.pallas_call(functools.partial(finish_kernel, q, parts, n, len(terms_a)...  4.47 us
  transfers between devices with their start and end apart: 45, of which 17 were waited for; matrix products, arithmetic and copies ran while one was open for 0% of the time, Pallas kernels for 14%

profile of v1, /device:TPU:20, one launch (start us, length us, event | category | flops | bytes accessed | tf_op | source)
XLA Modules:
  0.0 133.7 jit_solution(8088752859854737054)
XLA Ops:
  1.6 3.5 %collective-permute-start.34 = (bf16[64,1024]{1,0:T(8,128)(2,1)S(1)}, bf16[64,1024]{1,0:T(8,128)(2,1)S(1)}, u32[]{:S(2)}, u32[]{:S(2)}) collective-permute-start(bf16[64,1024]{1,0:T(8,128)(2,1)S(1)} %get-tuple-element.101.refs_0_), channel_id=1, source_target_pairs={{4,0},{5,1},{6,2},{7,3},{0,4},{1,5},{2,6},{3,7},{12,8},{13,9},{14,... | collective-permute-start | bytes 393224 | tf_op jit(solution)/shard_map/ppermute | solution.py:45
  5.1 2.0 %collective-permute-start.22 = (bf16[64,1024]{1,0:T(8,128)(2,1)S(1)}, bf16[64,1024]{1,0:T(8,128)(2,1)S(1)}, u32[]{:S(2)}, u32[]{:S(2)}) collective-permute-start(bf16[64,1024]{1,0:T(8,128)(2,1)S(1)} %get-tuple-element.102.refs_0_), channel_id=1, source_target_pairs={{2,0},{3,1},{4,2},{5,3},{6,4},{7,5},{0,6},{1,7},{10,8},{11,9},{12,... | collective-permute-start | bytes 393224 | tf_op jit(solution)/shard_map/ppermute | solution.py:45
  9.0 5.2 %collective-permute-done.34.refs_2_ = bf16[64,1024]{1,0:T(8,128)(2,1)S(1)} collective-permute-done((bf16[64,1024]{1,0:T(8,128)(2,1)S(1)}, bf16[64,1024]{1,0:T(8,128)(2,1)S(1)}, u32[]{:S(2)}, u32[]{:S(2)}) %collective-permute-start.34) | collective-permute-done | bytes 131104 | tf_op jit(solution)/shard_map/ppermute | solution.py:45
  14.2 8.3 %collective-permute-done.35.refs_3_ = bf16[64,1024]{1,0:T(8,128)(2,1)S(1)} collective-permute-done((bf16[64,1024]{1,0:T(8,128)(2,1)S(1)}, bf16[64,1024]{1,0:T(8,128)(2,1)S(1)}, u32[]{:S(2)}, u32[]{:S(2)}) %collective-permute-start.35) | collective-permute-done | bytes 131104 | tf_op jit(solution)/shard_map/ppermute | solution.py:45
  28.9 2.1 %collective-permute-done.37.refs_2_ = bf16[64,1024]{1,0:T(8,128)(2,1)S(1)} collective-permute-done((bf16[64,1024]{1,0:T(8,128)(2,1)S(1)}, bf16[64,1024]{1,0:T(8,128)(2,1)S(1)}, u32[]{:S(2)}, u32[]{:S(2)}) %collective-permute-start.37) | collective-permute-done | bytes 131104 | tf_op jit(solution)/shard_map/ppermute | solution.py:40
  31.0 2.0 %collective-permute-start = (bf16[64,1024]{1,0:T(8,128)(2,1)S(1)}, bf16[64,1024]{1,0:T(8,128)(2,1)S(1)}, u32[]{:S(2)}, u32[]{:S(2)}) collective-permute-start(bf16[64,1024]{1,0:T(8,128)(2,1)S(1)} %get-tuple-element.99.refs_0_), channel_id=1, source_target_pairs={{2,0},{3,1},{4,2},{5,3},{6,4},{7,5},{0,6},{1,7},{10,8},{11,9},{12,... | collective-permute-start | bytes 393224 | tf_op jit(solution)/shard_map/ppermute | solution.py:45
  33.0 5.3 %collective-permute-done.24.refs_3_ = bf16[64,1024]{1,0:T(8,128)(2,1)S(1)} collective-permute-done((bf16[64,1024]{1,0:T(8,128)(2,1)S(1)}, bf16[64,1024]{1,0:T(8,128)(2,1)S(1)}, u32[]{:S(2)}, u32[]{:S(2)}) %collective-permute-start.24) | collective-permute-done | bytes 131104 | tf_op jit(solution)/shard_map/ppermute | solution.py:45
  38.5 2.5 %collective-permute-done.12.refs_2_ = bf16[64,1024]{1,0:T(8,128)(2,1)S(1)} collective-permute-done((bf16[64,1024]{1,0:T(8,128)(2,1)S(1)}, bf16[64,1024]{1,0:T(8,128)(2,1)S(1)}, u32[]{:S(2)}, u32[]{:S(2)}) %collective-permute-start.12) | collective-permute-done | bytes 131104 | tf_op jit(solution)/shard_map/ppermute | solution.py:45
  42.5 4.9 %collective-permute-done.13.refs_3_ = bf16[64,1024]{1,0:T(8,128)(2,1)S(1)} collective-permute-done((bf16[64,1024]{1,0:T(8,128)(2,1)S(1)}, bf16[64,1024]{1,0:T(8,128)(2,1)S(1)}, u32[]{:S(2)}, u32[]{:S(2)}) %collective-permute-start.13) | collective-permute-done | bytes 131104 | tf_op jit(solution)/shard_map/ppermute | solution.py:45
  47.9 2.5 %collective-permute-start.27 = (bf16[64,1024]{1,0:T(8,128)(2,1)S(1)}, bf16[64,1024]{1,0:T(8,128)(2,1)S(1)}, u32[]{:S(2)}, u32[]{:S(2)}) collective-permute-start(bf16[64,1024]{1,0:T(8,128)(2,1)S(1)} %get-tuple-element.75), channel_id=1, source_target_pairs={{24,0},{16,8},{8,16},{0,24},{25,1},{17,9},{9,17},{1,25},{26,2},{18... | collective-permute-start | bytes 393224 | tf_op jit(solution)/shard_map/ppermute | solution.py:40
  53.0 3.2 %collective-permute-done.26.refs_2_ = bf16[64,1024]{1,0:T(8,128)(2,1)S(1)} collective-permute-done((bf16[64,1024]{1,0:T(8,128)(2,1)S(1)}, bf16[64,1024]{1,0:T(8,128)(2,1)S(1)}, u32[]{:S(2)}, u32[]{:S(2)}) %collective-permute-start.26) | collective-permute-done | bytes 131104 | tf_op jit(solution)/shard_map/ppermute | solution.py:40
  56.2 2.8 %collective-permute-start.16 = (bf16[64,1024]{1,0:T(8,128)(2,1)S(1)}, bf16[64,1024]{1,0:T(8,128)(2,1)S(1)}, u32[]{:S(2)}, u32[]{:S(2)}) collective-permute-start(bf16[64,1024]{1,0:T(8,128)(2,1)S(1)} %get-tuple-element.65), channel_id=1, source_target_pairs={{24,0},{16,8},{8,16},{0,24},{25,1},{17,9},{9,17},{1,25},{26,2},{18... | collective-permute-start | bytes 393224 | tf_op jit(solution)/shard_map/ppermute | solution.py:40
  60.2 2.3 %collective-permute-done.15.refs_2_ = bf16[64,1024]{1,0:T(8,128)(2,1)S(1)} collective-permute-done((bf16[64,1024]{1,0:T(8,128)(2,1)S(1)}, bf16[64,1024]{1,0:T(8,128)(2,1)S(1)}, u32[]{:S(2)}, u32[]{:S(2)}) %collective-permute-start.15) | collective-permute-done | bytes 131104 | tf_op jit(solution)/shard_map/ppermute | solution.py:40
  62.6 3.1 %collective-permute-start.5 = (bf16[64,1024]{1,0:T(8,128)(2,1)S(1)}, bf16[64,1024]{1,0:T(8,128)(2,1)S(1)}, u32[]{:S(2)}, u32[]{:S(2)}) collective-permute-start(bf16[64,1024]{1,0:T(8,128)(2,1)S(1)} %get-tuple-element.55), channel_id=1, source_target_pairs={{24,0},{16,8},{8,16},{0,24},{25,1},{17,9},{9,17},{1,25},{26,2},{18... | collective-permute-start | bytes 393224 | tf_op jit(solution)/shard_map/ppermute | solution.py:40
  65.7 4.6 %copy-done = bf16[2048,3,1024]{2,0,1:T(8,128)(2,1)S(1)} copy-done((bf16[2048,3,1024]{2,0,1:T(8,128)(2,1)S(1)}, bf16[2048,3,1024]{2,0,1:T(8,128)(2,1)}, u32[]{:S(2)}) %copy-start) | copy-done | bytes 12582936
  71.9 3.4 %project.7 = (bf16[64,3072]{1,0:T(8,128)(2,1)S(1)}, bf16[64,3072]{1,0:T(8,128)(2,1)S(1)}, f32[64,3072]{1,0:T(8,128)S(1)}, f32[64,3072]{1,0:T(8,128)S(1)}) custom-call(bf16[256,1024]{1,0:T(8,128)(2,1)S(1)} %stack.7.mine, bf16[256,1024]{1,0:T(8,128)(2,1)S(1)} %collective-permute-done.39.other, bf16[3,2,1024,1024]{3,2,1,0:T(8,128)(2,1)S(1)} %fetch_w.1.w_ref), custom_call_target="tpu_custom_call" | custom-call | flops 3221225472 | bytes 12582912 | tf_op jit(solution)/shard_map/project/pallas_call | solution.py:150
  76.3 3.4 %project.6 = (bf16[64,3072]{1,0:T(8,128)(2,1)S(1)}, bf16[64,3072]{1,0:T(8,128)(2,1)S(1)}, f32[64,3072]{1,0:T(8,128)S(1)}, f32[64,3072]{1,0:T(8,128)S(1)}) custom-call(bf16[256,1024]{1,0:T(8,128)(2,1)S(1)} %stack.6.mine, bf16[256,1024]{1,0:T(8,128)(2,1)S(1)} %collective-permute-done.28.other, bf16[3,2,1024,1024]{3,2,1,0:T(8,128)(2,1)S(1)} %fetch_w.1.w_ref), custom_call_target="tpu_custom_call" | custom-call | flops 3221225472 | bytes 12582912 | tf_op jit(solution)/shard_map/project/pallas_call | solution.py:150
  82.9 3.4 %project.5 = (bf16[64,3072]{1,0:T(8,128)(2,1)S(1)}, bf16[64,3072]{1,0:T(8,128)(2,1)S(1)}, f32[64,3072]{1,0:T(8,128)S(1)}, f32[64,3072]{1,0:T(8,128)S(1)}) custom-call(bf16[256,1024]{1,0:T(8,128)(2,1)S(1)} %stack.5.mine, bf16[256,1024]{1,0:T(8,128)(2,1)S(1)} %collective-permute-done.17.other, bf16[3,2,1024,1024]{3,2,1,0:T(8,128)(2,1)S(1)} %fetch_w.1.w_ref), custom_call_target="tpu_custom_call" | custom-call | flops 3221225472 | bytes 12582912 | tf_op jit(solution)/shard_map/project/pallas_call | solution.py:150
  88.2 3.4 %project.4 = (bf16[64,3072]{1,0:T(8,128)(2,1)S(1)}, bf16[64,3072]{1,0:T(8,128)(2,1)S(1)}, f32[64,3072]{1,0:T(8,128)S(1)}, f32[64,3072]{1,0:T(8,128)S(1)}) custom-call(bf16[256,1024]{1,0:T(8,128)(2,1)S(1)} %stack.4.mine, bf16[256,1024]{1,0:T(8,128)(2,1)S(1)} %collective-permute-done.6.other, bf16[3,2,1024,1024]{3,2,1,0:T(8,128)(2,1)S(1)} %fetch_w.1.w_ref), custom_call_target="tpu_custom_call" | custom-call | flops 3221225472 | bytes 12582912 | tf_op jit(solution)/shard_map/project/pallas_call | solution.py:150
  92.7 3.1 %collective-permute-done.29.refs_1_ = bf16[64,3072]{1,0:T(8,128)(2,1)S(1)} collective-permute-done((bf16[64,3072]{1,0:T(8,128)(2,1)S(1)}, bf16[64,3072]{1,0:T(8,128)(2,1)S(1)}, u32[]{:S(2)}, u32[]{:S(2)}) %collective-permute-start.29) | collective-permute-done | bytes 393248 | tf_op jit(solution)/shard_map/ppermute | solution.py:40
  98.1 6.2 %collective-permute-done.18.refs_1_ = bf16[64,3072]{1,0:T(8,128)(2,1)S(1)} collective-permute-done((bf16[64,3072]{1,0:T(8,128)(2,1)S(1)}, bf16[64,3072]{1,0:T(8,128)(2,1)S(1)}, u32[]{:S(2)}, u32[]{:S(2)}) %collective-permute-start.18) | collective-permute-done | bytes 393248 | tf_op jit(solution)/shard_map/ppermute | solution.py:40
  105.1 7.6 %collective-permute-done.7.refs_1_ = bf16[64,3072]{1,0:T(8,128)(2,1)S(1)} collective-permute-done((bf16[64,3072]{1,0:T(8,128)(2,1)S(1)}, bf16[64,3072]{1,0:T(8,128)(2,1)S(1)}, u32[]{:S(2)}, u32[]{:S(2)}) %collective-permute-start.7) | collective-permute-done | bytes 393248 | tf_op jit(solution)/shard_map/ppermute | solution.py:40
  113.7 3.6 %collective-permute-done.42.refs_2_ = bf16[32,3072]{1,0:T(8,128)(2,1)S(1)} collective-permute-done((bf16[32,3072]{1,0:T(8,128)(2,1)S(1)}, bf16[32,3072]{1,0:T(8,128)(2,1)S(1)}, u32[]{:S(2)}, u32[]{:S(2)}) %collective-permute-start.42) | collective-permute-done | bytes 196640 | tf_op jit(solution)/shard_map/ppermute | solution.py:40
  124.1 2.3 %collective-permute-start.44 = (bf16[16,3072]{1,0:T(8,128)(2,1)S(1)}, bf16[16,3072]{1,0:T(8,128)(2,1)S(1)}, u32[]{:S(2)}, u32[]{:S(2)}) collective-permute-start(bf16[16,3072]{1,0:T(8,128)(2,1)S(1)} %get-tuple-element.95), channel_id=1, source_target_pairs={{0,8},{8,16},{16,24},{1,9},{9,17},{17,25},{2,10},{10,18},{18,26},{... | collective-permute-start | bytes 294920 | tf_op jit(solution)/shard_map/ppermute | solution.py:291
  (95 shorter events, 42.6 us)
Async XLA Ops:
  1.6 12.6 %collective-permute-start.34 = (bf16[64,1024]{1,0:T(8,128)(2,1)S(1)}, bf16[64,1024]{1,0:T(8,128)(2,1)S(1)}, u32[]{:S(2)}, u32[]{:S(2)}) collective-permute-start(bf16[64,1024]{1,0:T(8,128)(2,1)S(1)} %get-tuple-element.101.refs_0_), channel_id=1, source_target_pairs={{4,0},{5,1},{6,2},{7,3},{0,4},{1,5},{2,6},{3,7},{12,8},{13,9},{14,... | collective-permute-start | bytes 393224 | tf_op jit(solution)/shard_map/ppermute | solution.py:45
  5.1 17.4 %collective-permute-start.35 = (bf16[64,1024]{1,0:T(8,128)(2,1)S(1)}, bf16[64,1024]{1,0:T(8,128)(2,1)S(1)}, u32[]{:S(2)}, u32[]{:S(2)}) collective-permute-start(bf16[64,1024]{1,0:T(8,128)(2,1)S(1)} %get-tuple-element.101.refs_0_), channel_id=1, source_target_pairs={{6,0},{7,1},{0,2},{1,3},{2,4},{3,5},{4,6},{5,7},{14,8},{15,9},{8,1... | collective-permute-start | bytes 393224 | tf_op jit(solution)/shard_map/ppermute | solution.py:45
  5.1 21.1 %collective-permute-start.22 = (bf16[64,1024]{1,0:T(8,128)(2,1)S(1)}, bf16[64,1024]{1,0:T(8,128)(2,1)S(1)}, u32[]{:S(2)}, u32[]{:S(2)}) collective-permute-start(bf16[64,1024]{1,0:T(8,128)(2,1)S(1)} %get-tuple-element.102.refs_0_), channel_id=1, source_target_pairs={{2,0},{3,1},{4,2},{5,3},{6,4},{7,5},{0,6},{1,7},{10,8},{11,9},{12,... | collective-permute-start | bytes 393224 | tf_op jit(solution)/shard_map/ppermute | solution.py:45
  7.1 19.1 %collective-permute-start.23 = (bf16[64,1024]{1,0:T(8,128)(2,1)S(1)}, bf16[64,1024]{1,0:T(8,128)(2,1)S(1)}, u32[]{:S(2)}, u32[]{:S(2)}) collective-permute-start(bf16[64,1024]{1,0:T(8,128)(2,1)S(1)} %get-tuple-element.102.refs_0_), channel_id=1, source_target_pairs={{4,0},{5,1},{6,2},{7,3},{0,4},{1,5},{2,6},{3,7},{12,8},{13,9},{14,... | collective-permute-start | bytes 393224 | tf_op jit(solution)/shard_map/ppermute | solution.py:45
  26.2 12.1 %collective-permute-start.24 = (bf16[64,1024]{1,0:T(8,128)(2,1)S(1)}, bf16[64,1024]{1,0:T(8,128)(2,1)S(1)}, u32[]{:S(2)}, u32[]{:S(2)}) collective-permute-start(bf16[64,1024]{1,0:T(8,128)(2,1)S(1)} %get-tuple-element.102.refs_0_), channel_id=1, source_target_pairs={{6,0},{7,1},{0,2},{1,3},{2,4},{3,5},{4,6},{5,7},{14,8},{15,9},{8,1... | collective-permute-start | bytes 393224 | tf_op jit(solution)/shard_map/ppermute | solution.py:45
  26.2 12.1 %collective-permute-start.11 = (bf16[64,1024]{1,0:T(8,128)(2,1)S(1)}, bf16[64,1024]{1,0:T(8,128)(2,1)S(1)}, u32[]{:S(2)}, u32[]{:S(2)}) collective-permute-start(bf16[64,1024]{1,0:T(8,128)(2,1)S(1)} %get-tuple-element.100.refs_0_), channel_id=1, source_target_pairs={{2,0},{3,1},{4,2},{5,3},{6,4},{7,5},{0,6},{1,7},{10,8},{11,9},{12,... | collective-permute-start | bytes 393224 | tf_op jit(solution)/shard_map/ppermute | solution.py:45
  28.9 12.1 %collective-permute-start.12 = (bf16[64,1024]{1,0:T(8,128)(2,1)S(1)}, bf16[64,1024]{1,0:T(8,128)(2,1)S(1)}, u32[]{:S(2)}, u32[]{:S(2)}) collective-permute-start(bf16[64,1024]{1,0:T(8,128)(2,1)S(1)} %get-tuple-element.100.refs_0_), channel_id=1, source_target_pairs={{4,0},{5,1},{6,2},{7,3},{0,4},{1,5},{2,6},{3,7},{12,8},{13,9},{14,... | collective-permute-start | bytes 393224 | tf_op jit(solution)/shard_map/ppermute | solution.py:45
  31.0 16.4 %collective-permute-start.13 = (bf16[64,1024]{1,0:T(8,128)(2,1)S(1)}, bf16[64,1024]{1,0:T(8,128)(2,1)S(1)}, u32[]{:S(2)}, u32[]{:S(2)}) collective-permute-start(bf16[64,1024]{1,0:T(8,128)(2,1)S(1)} %get-tuple-element.100.refs_0_), channel_id=1, source_target_pairs={{6,0},{7,1},{0,2},{1,3},{2,4},{3,5},{4,6},{5,7},{14,8},{15,9},{8,1... | collective-permute-start | bytes 393224 | tf_op jit(solution)/shard_map/ppermute | solution.py:45
  31.0 16.9 %collective-permute-start = (bf16[64,1024]{1,0:T(8,128)(2,1)S(1)}, bf16[64,1024]{1,0:T(8,128)(2,1)S(1)}, u32[]{:S(2)}, u32[]{:S(2)}) collective-permute-start(bf16[64,1024]{1,0:T(8,128)(2,1)S(1)} %get-tuple-element.99.refs_0_), channel_id=1, source_target_pairs={{2,0},{3,1},{4,2},{5,3},{6,4},{7,5},{0,6},{1,7},{10,8},{11,9},{12,... | collective-permute-start | bytes 393224 | tf_op jit(solution)/shard_map/ppermute | solution.py:45
  38.3 33.6 %collective-permute-start.39 = (bf16[256,1024]{1,0:T(8,128)(2,1)S(1)}, bf16[256,1024]{1,0:T(8,128)(2,1)S(1)}, u32[]{:S(2)}, u32[]{:S(2)}) collective-permute-start(bf16[256,1024]{1,0:T(8,128)(2,1)S(1)} %stack.7.mine), channel_id=1, source_target_pairs={{0,1},{1,0},{2,3},{3,2},{4,5},{5,4},{6,7},{7,6},{8,9},{9,8},{10,11... | collective-permute-start | bytes 1572872 | tf_op jit(solution)/shard_map/ppermute | solution.py:283
  59.1 17.2 %collective-permute-start.28 = (bf16[256,1024]{1,0:T(8,128)(2,1)S(1)}, bf16[256,1024]{1,0:T(8,128)(2,1)S(1)}, u32[]{:S(2)}, u32[]{:S(2)}) collective-permute-start(bf16[256,1024]{1,0:T(8,128)(2,1)S(1)} %stack.6.mine), channel_id=1, source_target_pairs={{0,1},{1,0},{2,3},{3,2},{4,5},{5,4},{6,7},{7,6},{8,9},{9,8},{10,11... | collective-permute-start | bytes 1572872 | tf_op jit(solution)/shard_map/ppermute | solution.py:283
  71.4 15.0 %collective-permute-start.6 = (bf16[256,1024]{1,0:T(8,128)(2,1)S(1)}, bf16[256,1024]{1,0:T(8,128)(2,1)S(1)}, u32[]{:S(2)}, u32[]{:S(2)}) collective-permute-start(bf16[256,1024]{1,0:T(8,128)(2,1)S(1)} %stack.4.mine), channel_id=1, source_target_pairs={{0,1},{1,0},{2,3},{3,2},{4,5},{5,4},{6,7},{7,6},{8,9},{9,8},{10,11... | collective-permute-start | bytes 1572872 | tf_op jit(solution)/shard_map/ppermute | solution.py:283
  75.3 12.0 %collective-permute-start.40 = (bf16[64,3072]{1,0:T(8,128)(2,1)S(1)}, bf16[64,3072]{1,0:T(8,128)(2,1)S(1)}, u32[]{:S(2)}, u32[]{:S(2)}) collective-permute-start(bf16[64,3072]{1,0:T(8,128)(2,1)S(1)} %get-tuple-element.87), channel_id=1, source_target_pairs={{8,0},{0,8},{24,16},{16,24},{9,1},{1,9},{25,17},{17,25},{10,2},{2,... | collective-permute-start | bytes 1179656 | tf_op jit(solution)/shard_map/ppermute | solution.py:40
  75.8 15.8 %collective-permute-start.41 = (bf16[64,3072]{1,0:T(8,128)(2,1)S(1)}, bf16[64,3072]{1,0:T(8,128)(2,1)S(1)}, u32[]{:S(2)}, u32[]{:S(2)}) collective-permute-start(bf16[64,3072]{1,0:T(8,128)(2,1)S(1)} %get-tuple-element.89), channel_id=1, source_target_pairs={{16,0},{24,8},{0,16},{8,24},{17,1},{25,9},{1,17},{9,25},{18,2},{26... | collective-permute-start | bytes 1179656 | tf_op jit(solution)/shard_map/ppermute | solution.py:40
  79.7 16.1 %collective-permute-start.29 = (bf16[64,3072]{1,0:T(8,128)(2,1)S(1)}, bf16[64,3072]{1,0:T(8,128)(2,1)S(1)}, u32[]{:S(2)}, u32[]{:S(2)}) collective-permute-start(bf16[64,3072]{1,0:T(8,128)(2,1)S(1)} %get-tuple-element.77), channel_id=1, source_target_pairs={{8,0},{0,8},{24,16},{16,24},{9,1},{1,9},{25,17},{17,25},{10,2},{2,... | collective-permute-start | bytes 1179656 | tf_op jit(solution)/shard_map/ppermute | solution.py:40
  81.7 15.0 %collective-permute-start.30 = (bf16[64,3072]{1,0:T(8,128)(2,1)S(1)}, bf16[64,3072]{1,0:T(8,128)(2,1)S(1)}, u32[]{:S(2)}, u32[]{:S(2)}) collective-permute-start(bf16[64,3072]{1,0:T(8,128)(2,1)S(1)} %get-tuple-element.79), channel_id=1, source_target_pairs={{16,0},{24,8},{0,16},{8,24},{17,1},{25,9},{1,17},{9,25},{18,2},{26... | collective-permute-start | bytes 1179656 | tf_op jit(solution)/shard_map/ppermute | solution.py:40
  86.4 17.8 %collective-permute-start.18 = (bf16[64,3072]{1,0:T(8,128)(2,1)S(1)}, bf16[64,3072]{1,0:T(8,128)(2,1)S(1)}, u32[]{:S(2)}, u32[]{:S(2)}) collective-permute-start(bf16[64,3072]{1,0:T(8,128)(2,1)S(1)} %get-tuple-element.67), channel_id=1, source_target_pairs={{8,0},{0,8},{24,16},{16,24},{9,1},{1,9},{25,17},{17,25},{10,2},{2,... | collective-permute-start | bytes 1179656 | tf_op jit(solution)/shard_map/ppermute | solution.py:40
  87.4 17.2 %collective-permute-start.19 = (bf16[64,3072]{1,0:T(8,128)(2,1)S(1)}, bf16[64,3072]{1,0:T(8,128)(2,1)S(1)}, u32[]{:S(2)}, u32[]{:S(2)}) collective-permute-start(bf16[64,3072]{1,0:T(8,128)(2,1)S(1)} %get-tuple-element.69), channel_id=1, source_target_pairs={{16,0},{24,8},{0,16},{8,24},{17,1},{25,9},{1,17},{9,25},{18,2},{26... | collective-permute-start | bytes 1179656 | tf_op jit(solution)/shard_map/ppermute | solution.py:40
  91.6 21.1 %collective-permute-start.7 = (bf16[64,3072]{1,0:T(8,128)(2,1)S(1)}, bf16[64,3072]{1,0:T(8,128)(2,1)S(1)}, u32[]{:S(2)}, u32[]{:S(2)}) collective-permute-start(bf16[64,3072]{1,0:T(8,128)(2,1)S(1)} %get-tuple-element.57), channel_id=1, source_target_pairs={{8,0},{0,8},{24,16},{16,24},{9,1},{1,9},{25,17},{17,25},{10,2},{2,... | collective-permute-start | bytes 1179656 | tf_op jit(solution)/shard_map/ppermute | solution.py:40
  95.8 17.3 %collective-permute-start.8 = (bf16[64,3072]{1,0:T(8,128)(2,1)S(1)}, bf16[64,3072]{1,0:T(8,128)(2,1)S(1)}, u32[]{:S(2)}, u32[]{:S(2)}) collective-permute-start(bf16[64,3072]{1,0:T(8,128)(2,1)S(1)} %get-tuple-element.59), channel_id=1, source_target_pairs={{16,0},{24,8},{0,16},{8,24},{17,1},{25,9},{1,17},{9,25},{18,2},{26... | collective-permute-start | bytes 1179656 | tf_op jit(solution)/shard_map/ppermute | solution.py:40
  96.7 20.6 %collective-permute-start.42 = (bf16[32,3072]{1,0:T(8,128)(2,1)S(1)}, bf16[32,3072]{1,0:T(8,128)(2,1)S(1)}, u32[]{:S(2)}, u32[]{:S(2)}) collective-permute-start(bf16[32,3072]{1,0:T(8,128)(2,1)S(1)} %get-tuple-element.90), channel_id=1, source_target_pairs={{16,0},{24,8},{0,16},{8,24},{17,1},{25,9},{1,17},{9,25},{18,2},{26... | collective-permute-start | bytes 589832 | tf_op jit(solution)/shard_map/ppermute | solution.py:40
  104.2 14.7 %collective-permute-start.43 = (bf16[32,3072]{1,0:T(8,128)(2,1)S(1)}, bf16[32,3072]{1,0:T(8,128)(2,1)S(1)}, u32[]{:S(2)}, u32[]{:S(2)}) collective-permute-start(bf16[32,3072]{1,0:T(8,128)(2,1)S(1)} %get-tuple-element.91), channel_id=1, source_target_pairs={{8,0},{0,8},{24,16},{16,24},{9,1},{1,9},{25,17},{17,25},{10,2},{2,... | collective-permute-start | bytes 589832 | tf_op jit(solution)/shard_map/ppermute | solution.py:40
  104.6 16.9 %collective-permute-start.31 = (bf16[32,3072]{1,0:T(8,128)(2,1)S(1)}, bf16[32,3072]{1,0:T(8,128)(2,1)S(1)}, u32[]{:S(2)}, u32[]{:S(2)}) collective-permute-start(bf16[32,3072]{1,0:T(8,128)(2,1)S(1)} %get-tuple-element.80), channel_id=1, source_target_pairs={{16,0},{24,8},{0,16},{8,24},{17,1},{25,9},{1,17},{9,25},{18,2},{26... | collective-permute-start | bytes 589832 | tf_op jit(solution)/shard_map/ppermute | solution.py:40
  113.1 14.4 %collective-permute-start.20 = (bf16[32,3072]{1,0:T(8,128)(2,1)S(1)}, bf16[32,3072]{1,0:T(8,128)(2,1)S(1)}, u32[]{:S(2)}, u32[]{:S(2)}) collective-permute-start(bf16[32,3072]{1,0:T(8,128)(2,1)S(1)} %get-tuple-element.70), channel_id=1, source_target_pairs={{16,0},{24,8},{0,16},{8,24},{17,1},{25,9},{1,17},{9,25},{18,2},{26... | collective-permute-start | bytes 589832 | tf_op jit(solution)/shard_map/ppermute | solution.py:40
  (24 other events, 261.6 us)

commit v2 on v1

--- a/solution.py
+++ b/solution.py
@@ -20,8 +20,33 @@
     return pltpu.CompilerParams(vmem_limit_bytes=mib * 2**20)
 
 
-def cost(flops, moved):
-    return pl.CostEstimate(flops=flops, bytes_accessed=moved, transcendentals=0)
+QUICK = pl.CostEstimate(flops=1, bytes_accessed=1, transcendentals=0)
+
+
+class Order:
+    def __init__(self):
+        self.last = None
+
+    def call(self, kernel, args, shapes, name, scratch=(), specs=None):
+        specs = [VMEM] * len(args) if specs is None else specs
+        extra = [] if self.last is None else [self.last]
+        count = len(args)
+
+        def body(*refs):
+            kernel(*refs[:count], *refs[count + len(extra) :])
+
+        outs = pl.pallas_call(
+            body,
+            in_specs=specs + [HBM] * len(extra),
+            out_specs=[VMEM] * len(shapes),
+            out_shape=[pltpu.VMEM(s, t) for s, t in shapes],
+            scratch_shapes=list(scratch),
+            compiler_params=params(),
+            cost_estimate=QUICK,
+            name=name,
+        )(*args, *extra)
+        self.last = outs[-1]
+        return list(outs)
 
 
 def side(n):
@@ -59,18 +84,11 @@
         c.wait()
 
 
-def fetch(w_in):
-    w = w_in.transpose(1, 0, 2)
+def fetch(order, w_in):
+    w = pltpu.with_memory_space_constraint(w_in.transpose(1, 0, 2), pltpu.HBM)
     g, k, n = w.shape
-    return pl.pallas_call(
-        fetch_kernel,
-        in_specs=[HBM],
-        out_specs=VMEM,
-        out_shape=pltpu.VMEM((g, 2, k // 2, n), BF16),
-        scratch_shapes=[pltpu.SemaphoreType.DMA((2 * g,))],
-        compiler_params=params(),
-        name="fetch_w",
-    )(w)
+    scratch = [pltpu.SemaphoreType.DMA((2 * g,))]
+    return order.call(fetch_kernel, [w], [((g, 2, k // 2, n), BF16)], "fetch_w", scratch, specs=[HBM])[0]
 
 
 def pick_kernel(shape, *refs):
@@ -91,19 +109,15 @@
                     outs[dy * xs + dx][...] = ins[dz][...]
 
 
-def gather_tokens(piece, shape):
-    ys, xs = shape
-    zs = ys * xs
-    strips = [piece] + [shift_planes(piece, dz) for dz in range(1, zs)]
-    picked = pl.pallas_call(
-        functools.partial(pick_kernel, shape),
-        in_specs=[VMEM] * zs,
-        out_specs=[VMEM] * zs,
-        out_shape=[pltpu.VMEM(piece.shape, BF16)] * zs,
-        compiler_params=params(),
-        name="pick",
-    )(*strips)
-    return [picked[0]] + [shift_rows(picked[i], shape, i // xs, i % xs) for i in range(1, zs)]
+def gather_planes(piece, shape):
+    ys, xs = shape
+    return [piece] + [shift_planes(piece, dz) for dz in range(1, ys * xs)]
+
+
+def gather_rows(order, strips, shape):
+    xs = shape[1]
+    picked = order.call(functools.partial(pick_kernel, shape), strips, [(strips[0].shape, BF16)] * len(strips), "pick")
+    return [picked[0]] + [shift_rows(picked[i], shape, i // xs, i % xs) for i in range(1, len(picked))]
 
 
 def stack_kernel(order, *refs):
@@ -113,20 +127,13 @@
         out[at * h : (at + 1) * h] = ins[block][part * h : (part + 1) * h]
 
 
-def stack(blocks, shape):
-    ys, xs = shape
-    order = [(dy * xs + dx, 0) for dx in range(1, xs) for dy in range(ys)]
-    order += [(dy * xs + dx, 1) for dy in range(1, ys) for dx in range(xs)]
-    order += [(dy * xs, 0) for dy in range(ys)] + [(dx, 1) for dx in range(xs)]
+def stack(order, blocks, shape):
+    ys, xs = shape
+    parts = [(dy * xs + dx, 0) for dx in range(1, xs) for dy in range(ys)]
+    parts += [(dy * xs + dx, 1) for dy in range(1, ys) for dx in range(xs)]
+    parts += [(dy * xs, 0) for dy in range(ys)] + [(dx, 1) for dx in range(xs)]
     n, e = blocks[0].shape
-    return pl.pallas_call(
-        functools.partial(stack_kernel, order),
-        in_specs=[VMEM] * len(blocks),
-        out_specs=VMEM,
-        out_shape=pltpu.VMEM((len(blocks) * n, e), BF16),
-        compiler_params=params(),
-        name="stack",
-    )(*blocks)
+    return order.call(functools.partial(stack_kernel, parts), blocks, [((len(blocks) * n, e), BF16)], "stack")[0]
 
 
 def project_kernel(tn, mine, other, w_ref, *outs):
@@ -142,21 +149,21 @@
                 at += o.shape[0]
 
 
-def project(mine, other, w, h, shape):
+def project(order, mine, other, w, h, shape):
     ys, xs = shape
     m, e = mine.shape
     cols = w.shape[3]
-    sizes = [(ys * h, BF16)] * (xs - 1) + [(xs * h, BF16)] * (ys - 1) + [(ys * h, F32), (xs * h, F32)]
-    outs = pl.pallas_call(
+    shapes = [((ys * h, 3 * cols), BF16)] * (xs - 1) + [((xs * h, 3 * cols), BF16)] * (ys - 1)
+    shapes += [((ys * h, 3 * cols), F32), ((xs * h, 3 * cols), F32)]
+    outs = order.call(
         functools.partial(project_kernel, min(cols, 256)),
-        in_specs=[VMEM] * 3,
-        out_specs=[VMEM] * len(sizes),
-        out_shape=[pltpu.VMEM((s, 3 * cols), t) for s, t in sizes],
-        compiler_params=params(),
-        cost_estimate=cost(2 * m * 2 * e * 3 * cols, 2 * w.size),
-        name="project",
-    )(mine, other, w)
-    return outs[: xs - 1], outs[xs - 1 : xs + ys - 2], outs[-2], outs[-1]
+        [mine, other, w],
+        shapes,
+        "project",
+    )
+    got_a = [shift_rows(s, shape, 0, -dx) for dx, s in enumerate(outs[: xs - 1], 1)]
+    got_c = [shift_rows(s, shape, -dy, 0) for dy, s in enumerate(outs[xs - 1 : -2], 1)]
+    return [outs[-2], *got_a], [outs[-1], *got_c]
 
 
 def middle_kernel(count_a, count_c, *refs):
@@ -172,23 +179,16 @@
             mid[...] = total.astype(BF16)
 
 
-def exchange(outs, h, shape):
-    ys, xs = shape
-    sent_a, sent_c, keep_a, keep_c = outs
-    got_a = [shift_rows(s, shape, 0, -dx) for dx, s in enumerate(sent_a, 1)]
-    got_c = [shift_rows(s, shape, -dy, 0) for dy, s in enumerate(sent_c, 1)]
-    n = keep_a.shape[1]
-    mids = pl.pallas_call(
-        functools.partial(middle_kernel, xs - 1, ys - 1),
-        in_specs=[VMEM] * (2 + xs - 1 + ys - 1),
-        out_specs=[VMEM] * (xs + ys - 2),
-        out_shape=[pltpu.VMEM((h, n), BF16)] * (xs + ys - 2),
-        compiler_params=params(),
-        name="middle",
-    )(keep_a, *got_a, keep_c, *got_c)
+def middle(order, terms, h, shape):
+    ys, xs = shape
+    first, second = terms
+    n = first[0].shape[1]
+    mids = order.call(
+        functools.partial(middle_kernel, xs - 1, ys - 1), [*first, *second], [((h, n), BF16)] * (xs + ys - 2), "middle"
+    )
     last_a = [shift_rows(s, shape, -dy, 0) for dy, s in enumerate(mids[: ys - 1], 1)]
     last_c = [shift_rows(s, shape, 0, -dx) for dx, s in enumerate(mids[ys - 1 :], 1)]
-    return [keep_a, *got_a, *last_a], [keep_c, *got_c, *last_c]
+    return [*first, *last_a], [*second, *last_c]
 
 
 def finish_kernel(q, parts, n, count_a, count_c, *refs):
@@ -246,25 +246,22 @@
     lax.fori_loop(0, cols // LANES, column, 0)
 
 
-def finish(q, parts, n, terms_a, terms_c, fin, fmix, follow, rim):
-    width = terms_a[0].shape[1]
+def finish(order, q, parts, n, terms, fin, fmix, follow, rim):
+    width = terms[0][0].shape[1]
     cols = fmix.shape[1]
     rows = n + (RIM if q == 0 else 0) - (RIM if q == parts - 1 else 0)
-    args = [*terms_a, *terms_c, fin, fmix]
+    args = [*terms[0], *terms[1], fin, fmix]
     args += [follow] if q < parts - 1 else []
     args += [rim] if q == 0 else []
-    shapes = [pltpu.VMEM((rows, cols), BF16)]
-    shapes += [pltpu.VMEM((RIM, width), F32)] if q > 0 else []
-    shapes += [pltpu.VMEM((RIM, width), BF16)] if q == parts - 1 else []
-    return pl.pallas_call(
-        functools.partial(finish_kernel, q, parts, n, len(terms_a), len(terms_c)),
-        in_specs=[VMEM] * len(args),
-        out_specs=[VMEM] * len(shapes),
-        out_shape=shapes,
-        scratch_shapes=[pltpu.VMEM((n + 2 * RIM, width), F32), pltpu.VMEM((80, LANES), F32)],
-        compiler_params=params(),
-        name="finish",
-    )(*args)
+    shapes = [((rows, cols), BF16)]
+    shapes += [((RIM, width), F32)] if q > 0 else []
+    shapes += [((RIM, width), BF16)] if q == parts - 1 else []
+    kernel = functools.partial(finish_kernel, q, parts, n, len(terms[0]), len(terms[1]))
+    scratch = [pltpu.VMEM((n + 2 * RIM, width), F32), pltpu.VMEM((80, LANES), F32)]
+    return order.call(kernel, args, shapes, "finish", scratch)
+
+
+PLAN = "P0 W K0 P1 J0 K1 P2 J1 M0 K2 P3 J2 M1 K3 F0 J3 M2 F1 M3 F2 F3"
 
 
 def per_device(tokens, w_in, filt_in, filt_mix):
@@ -273,23 +270,35 @@
     count = lax.axis_size("row")
     shape = side(count)
     n = rows // PARTS
-    w = fetch(w_in)
+    order = Order()
     fin = filt_in.transpose(1, 0, 2)
     swap = [(c, c ^ 1) for c in range(cols)]
-    outs, follow, rim = [], None, None
-    for q in reversed(range(PARTS)):
-        blocks = gather_tokens(tokens[q * n : (q + 1) * n], shape)
-        mine = stack(blocks, shape)
-        other = lax.ppermute(mine, "col", swap)
-        sums = project(mine, other, w, n // 2, shape)
-        terms_a, terms_c = exchange(sums, n // 2, shape)
-        got = list(finish(q, PARTS, n, terms_a, terms_c, fin, filt_mix, follow, rim))
-        outs.insert(0, got.pop(0))
-        if q > 0:
-            follow = got.pop(0)
-        if q == PARTS - 1:
-            rim = lax.ppermute(got.pop(0), "row", [(i, i + 1) for i in range(count - 1)])
-    return jnp.concatenate(outs, axis=0)
+    pieces = [tokens[(PARTS - 1 - i) * n : (PARTS - i) * n] for i in range(PARTS)]
+    strips = [gather_planes(piece, shape) for piece in pieces]
+    blocks, mine, other, terms, outs = {}, {}, {}, {}, {}
+    follow, rim = None, None
+    for step in PLAN.split():
+        kind, i = step[0], int(step[1:] or 0)
+        if kind == "W":
+            w = fetch(order, w_in)
+        elif kind == "P":
+            blocks[i] = gather_rows(order, strips[i], shape)
+        elif kind == "K":
+            mine[i] = stack(order, blocks[i], shape)
+            other[i] = lax.ppermute(mine[i], "col", swap)
+        elif kind == "J":
+            terms[i] = project(order, mine[i], other[i], w, n // 2, shape)
+        elif kind == "M":
+            terms[i] = middle(order, terms[i], n // 2, shape)
+        else:
+            q = PARTS - 1 - i
+            got = finish(order, q, PARTS, n, terms[i], fin, filt_mix, follow, rim)
+            outs[q] = got.pop(0)
+            if q > 0:
+                follow = got.pop(0)
+            if i == 0:
+                rim = lax.ppermute(got.pop(0), "row", [(r, r + 1) for r in range(count - 1)])
+    return jnp.concatenate([outs[q] for q in range(PARTS)], axis=0)
 
 
 def solution(mesh):

time: 134 us -> 141 us (1.052)
  the two profiles are of different devices: /device:TPU:20 before, /device:TPU:0 now
where the time goes in v2:
time: 141 us
  waiting for transfers between devices  57.7 us (41%)
  starting transfers between devices  57.2 us (41%)
  Pallas kernels  23.8 us (17%)
    ppermute x12, waiting for transfers between devices, shift_planes(): lax.ppermute(block, 'col', [((c + CORES * dz) % cols, c) for c in range(c...  33.3 us
    ppermute x28, starting transfers between devices, shift_rows(): return lax.ppermute(block, 'row', route)  31.1 us
    pallas_call x21, Pallas kernels, call(): pl.pallas_call(body, in_specs=specs + [HBM] * len(extra), out_specs=[VMEM...  23.8 us
    ppermute x28, waiting for transfers between devices, shift_rows(): return lax.ppermute(block, 'row', route)  23.7 us
    ppermute x12, starting transfers between devices, shift_planes(): lax.ppermute(block, 'col', [((c + CORES * dz) % cols, c) for c in range(c...  22.9 us
    ppermute x1, starting transfers between devices, per_device(): lax.ppermute(got.pop(0), 'row', [(r, r + 1) for r in range(count - 1)])  2.92 us
  transfers between devices with their start and end apart: 45, of which 22 were waited for; matrix products, arithmetic and copies ran while one was open for 0% of the time, Pallas kernels for 16%

profile of v2, /device:TPU:0, one launch (start us, length us, event | category | flops | bytes accessed | tf_op | source)
XLA Modules:
  0.0 141.0 jit_solution(12571242665187163218)
XLA Ops:
  1.1 3.1 %collective-permute-start.11 = (bf16[64,1024]{1,0:T(8,128)(2,1)S(1)}, bf16[64,1024]{1,0:T(8,128)(2,1)S(1)}, u32[]{:S(2)}, u32[]{:S(2)}) collective-permute-start(bf16[64,1024]{1,0:T(8,128)(2,1)S(1)} %get-tuple-element.101.refs_0_), channel_id=1, source_target_pairs={{6,0},{7,1},{0,2},{1,3},{2,4},{3,5},{4,6},{5,7},{14,8},{15,9},{8,1... | collective-permute-start | bytes 393224 | tf_op jit(solution)/shard_map/ppermute | solution.py:70
  4.2 2.6 %collective-permute-start.10 = (bf16[64,1024]{1,0:T(8,128)(2,1)S(1)}, bf16[64,1024]{1,0:T(8,128)(2,1)S(1)}, u32[]{:S(2)}, u32[]{:S(2)}) collective-permute-start(bf16[64,1024]{1,0:T(8,128)(2,1)S(1)} %get-tuple-element.101.refs_0_), channel_id=1, source_target_pairs={{4,0},{5,1},{6,2},{7,3},{0,4},{1,5},{2,6},{3,7},{12,8},{13,9},{14,... | collective-permute-start | bytes 393224 | tf_op jit(solution)/shard_map/ppermute | solution.py:70
  8.1 2.5 %collective-permute-done.11.refs_3_ = bf16[64,1024]{1,0:T(8,128)(2,1)S(1)} collective-permute-done((bf16[64,1024]{1,0:T(8,128)(2,1)S(1)}, bf16[64,1024]{1,0:T(8,128)(2,1)S(1)}, u32[]{:S(2)}, u32[]{:S(2)}) %collective-permute-start.11) | collective-permute-done | bytes 131104 | tf_op jit(solution)/shard_map/ppermute | solution.py:70
  10.7 4.8 %collective-permute-done.10.refs_2_ = bf16[64,1024]{1,0:T(8,128)(2,1)S(1)} collective-permute-done((bf16[64,1024]{1,0:T(8,128)(2,1)S(1)}, bf16[64,1024]{1,0:T(8,128)(2,1)S(1)}, u32[]{:S(2)}, u32[]{:S(2)}) %collective-permute-start.10) | collective-permute-done | bytes 131104 | tf_op jit(solution)/shard_map/ppermute | solution.py:70
  19.1 4.7 %fetch_w.1.refs_4_.refs_2_ = bf16[3,2,1024,1024]{3,2,1,0:T(8,128)(2,1)S(1)} custom-call(bf16[3,2048,1024]{2,1,0:T(8,128)(2,1)} %bitcast.6, bf16[64,1024]{1,0:T(8,128)(2,1)S(1)} %get-tuple-element.55.refs_1_), custom_call_target="tpu_custom_call" | custom-call | flops 1 | bytes 1 | tf_op jit(solution)/shard_map/fetch_w/pallas_call | solution.py:38
  25.1 3.4 %collective-permute-start.8 = (bf16[64,1024]{1,0:T(8,128)(2,1)S(1)}, bf16[64,1024]{1,0:T(8,128)(2,1)S(1)}, u32[]{:S(2)}, u32[]{:S(2)}) collective-permute-start(bf16[64,1024]{1,0:T(8,128)(2,1)S(1)} %get-tuple-element.102.refs_0_), channel_id=1, source_target_pairs={{6,0},{7,1},{0,2},{1,3},{2,4},{3,5},{4,6},{5,7},{14,8},{15,9},{8,1... | collective-permute-start | bytes 393224 | tf_op jit(solution)/shard_map/ppermute | solution.py:70
  31.0 2.8 %collective-permute-done.8.refs_3_ = bf16[64,1024]{1,0:T(8,128)(2,1)S(1)} collective-permute-done((bf16[64,1024]{1,0:T(8,128)(2,1)S(1)}, bf16[64,1024]{1,0:T(8,128)(2,1)S(1)}, u32[]{:S(2)}, u32[]{:S(2)}) %collective-permute-start.8) | collective-permute-done | bytes 131104 | tf_op jit(solution)/shard_map/ppermute | solution.py:70
  33.7 5.3 %collective-permute-done.7.refs_2_ = bf16[64,1024]{1,0:T(8,128)(2,1)S(1)} collective-permute-done((bf16[64,1024]{1,0:T(8,128)(2,1)S(1)}, bf16[64,1024]{1,0:T(8,128)(2,1)S(1)}, u32[]{:S(2)}, u32[]{:S(2)}) %collective-permute-start.7) | collective-permute-done | bytes 131104 | tf_op jit(solution)/shard_map/ppermute | solution.py:70
  42.8 3.4 %project.4 = (bf16[64,3072]{1,0:T(8,128)(2,1)S(1)}, bf16[64,3072]{1,0:T(8,128)(2,1)S(1)}, f32[64,3072]{1,0:T(8,128)S(1)}, f32[64,3072]{1,0:T(8,128)S(1)}) custom-call(bf16[256,1024]{1,0:T(8,128)(2,1)S(1)} %stack.4.refs_4_.refs_0_, bf16[256,1024]{1,0:T(8,128)(2,1)S(1)} %collective-permute-done.18.refs_1_, ...), custom_call_target="tpu_custom_call" | custom-call | flops 1 | bytes 1 | tf_op jit(solution)/shard_map/project/pallas_call | solution.py:38
  48.0 3.4 %collective-permute-start.5 = (bf16[64,1024]{1,0:T(8,128)(2,1)S(1)}, bf16[64,1024]{1,0:T(8,128)(2,1)S(1)}, u32[]{:S(2)}, u32[]{:S(2)}) collective-permute-start(bf16[64,1024]{1,0:T(8,128)(2,1)S(1)} %get-tuple-element.100.refs_0_), channel_id=1, source_target_pairs={{6,0},{7,1},{0,2},{1,3},{2,4},{3,5},{4,6},{5,7},{14,8},{15,9},{8,1... | collective-permute-start | bytes 393224 | tf_op jit(solution)/shard_map/ppermute | solution.py:70
  53.7 1.9 %collective-permute-start.4 = (bf16[64,1024]{1,0:T(8,128)(2,1)S(1)}, bf16[64,1024]{1,0:T(8,128)(2,1)S(1)}, u32[]{:S(2)}, u32[]{:S(2)}) collective-permute-start(bf16[64,1024]{1,0:T(8,128)(2,1)S(1)} %get-tuple-element.100.refs_0_), channel_id=1, source_target_pairs={{4,0},{5,1},{6,2},{7,3},{0,4},{1,5},{2,6},{3,7},{12,8},{13,9},{14,... | collective-permute-start | bytes 393224 | tf_op jit(solution)/shard_map/ppermute | solution.py:70
  57.2 2.7 %collective-permute-start.3 = (bf16[64,1024]{1,0:T(8,128)(2,1)S(1)}, bf16[64,1024]{1,0:T(8,128)(2,1)S(1)}, u32[]{:S(2)}, u32[]{:S(2)}) collective-permute-start(bf16[64,1024]{1,0:T(8,128)(2,1)S(1)} %get-tuple-element.100.refs_0_), channel_id=1, source_target_pairs={{2,0},{3,1},{4,2},{5,3},{6,4},{7,5},{0,6},{1,7},{10,8},{11,9},{12,... | collective-permute-start | bytes 393224 | tf_op jit(solution)/shard_map/ppermute | solution.py:70
  59.9 2.8 %collective-permute-done.4.refs_2_ = bf16[64,1024]{1,0:T(8,128)(2,1)S(1)} collective-permute-done((bf16[64,1024]{1,0:T(8,128)(2,1)S(1)}, bf16[64,1024]{1,0:T(8,128)(2,1)S(1)}, u32[]{:S(2)}, u32[]{:S(2)}) %collective-permute-start.4) | collective-permute-done | bytes 131104 | tf_op jit(solution)/shard_map/ppermute | solution.py:70
  62.6 2.2 %collective-permute-done.3.refs_1_ = bf16[64,1024]{1,0:T(8,128)(2,1)S(1)} collective-permute-done((bf16[64,1024]{1,0:T(8,128)(2,1)S(1)}, bf16[64,1024]{1,0:T(8,128)(2,1)S(1)}, u32[]{:S(2)}, u32[]{:S(2)}) %collective-permute-start.3) | collective-permute-done | bytes 131104 | tf_op jit(solution)/shard_map/ppermute | solution.py:70
  68.5 3.4 %project.5 = (bf16[64,3072]{1,0:T(8,128)(2,1)S(1)}, bf16[64,3072]{1,0:T(8,128)(2,1)S(1)}, f32[64,3072]{1,0:T(8,128)S(1)}, f32[64,3072]{1,0:T(8,128)S(1)}) custom-call(bf16[256,1024]{1,0:T(8,128)(2,1)S(1)} %stack.5.refs_4_.refs_0_, bf16[256,1024]{1,0:T(8,128)(2,1)S(1)} %collective-permute-done.24.refs_1_, ...), custom_call_target="tpu_custom_call" | custom-call | flops 1 | bytes 1 | tf_op jit(solution)/shard_map/project/pallas_call | solution.py:38
  77.8 4.2 %collective-permute-done.2.refs_3_ = bf16[64,1024]{1,0:T(8,128)(2,1)S(1)} collective-permute-done((bf16[64,1024]{1,0:T(8,128)(2,1)S(1)}, bf16[64,1024]{1,0:T(8,128)(2,1)S(1)}, u32[]{:S(2)}, u32[]{:S(2)}) %collective-permute-start.2) | collective-permute-done | bytes 131104 | tf_op jit(solution)/shard_map/ppermute | solution.py:70
  82.0 5.2 %collective-permute-done.1.refs_2_ = bf16[64,1024]{1,0:T(8,128)(2,1)S(1)} collective-permute-done((bf16[64,1024]{1,0:T(8,128)(2,1)S(1)}, bf16[64,1024]{1,0:T(8,128)(2,1)S(1)}, u32[]{:S(2)}, u32[]{:S(2)}) %collective-permute-start.1) | collective-permute-done | bytes 131104 | tf_op jit(solution)/shard_map/ppermute | solution.py:70
  87.2 2.0 %collective-permute-done.refs_1_ = bf16[64,1024]{1,0:T(8,128)(2,1)S(1)} collective-permute-done((bf16[64,1024]{1,0:T(8,128)(2,1)S(1)}, bf16[64,1024]{1,0:T(8,128)(2,1)S(1)}, u32[]{:S(2)}, u32[]{:S(2)}) %collective-permute-start) | collective-permute-done | bytes 131104 | tf_op jit(solution)/shard_map/ppermute | solution.py:70
  93.1 3.4 %project.6 = (bf16[64,3072]{1,0:T(8,128)(2,1)S(1)}, bf16[64,3072]{1,0:T(8,128)(2,1)S(1)}, f32[64,3072]{1,0:T(8,128)S(1)}, f32[64,3072]{1,0:T(8,128)S(1)}) custom-call(bf16[256,1024]{1,0:T(8,128)(2,1)S(1)} %stack.6.refs_4_.refs_0_, bf16[256,1024]{1,0:T(8,128)(2,1)S(1)} %collective-permute-done.30.refs_1_, ...), custom_call_target="tpu_custom_call" | custom-call | flops 1 | bytes 1 | tf_op jit(solution)/shard_map/project/pallas_call | solution.py:38
  96.6 1.7 %collective-permute-done.26.refs_2_ = bf16[64,1024]{1,0:T(8,128)(2,1)S(1)} collective-permute-done((bf16[64,1024]{1,0:T(8,128)(2,1)S(1)}, bf16[64,1024]{1,0:T(8,128)(2,1)S(1)}, u32[]{:S(2)}, u32[]{:S(2)}) %collective-permute-start.26) | collective-permute-done | bytes 131104 | tf_op jit(solution)/shard_map/ppermute | solution.py:65
  102.5 3.6 %collective-permute-done.32.refs_2_ = bf16[32,3072]{1,0:T(8,128)(2,1)S(1)} collective-permute-done((bf16[32,3072]{1,0:T(8,128)(2,1)S(1)}, bf16[32,3072]{1,0:T(8,128)(2,1)S(1)}, u32[]{:S(2)}, u32[]{:S(2)}) %collective-permute-start.32) | collective-permute-done | bytes 196640 | tf_op jit(solution)/shard_map/ppermute | solution.py:65
  108.1 3.4 %project.7 = (bf16[64,3072]{1,0:T(8,128)(2,1)S(1)}, bf16[64,3072]{1,0:T(8,128)(2,1)S(1)}, f32[64,3072]{1,0:T(8,128)S(1)}, f32[64,3072]{1,0:T(8,128)S(1)}) custom-call(bf16[256,1024]{1,0:T(8,128)(2,1)S(1)} %stack.7.refs_8_.refs_0_, bf16[256,1024]{1,0:T(8,128)(2,1)S(1)} %collective-permute-done.31.refs_1_, ...), custom_call_target="tpu_custom_call" | custom-call | flops 1 | bytes 1 | tf_op jit(solution)/shard_map/project/pallas_call | solution.py:38
  117.8 11.1 %collective-permute-done.36.refs_2_ = bf16[32,3072]{1,0:T(8,128)(2,1)S(1)} collective-permute-done((bf16[32,3072]{1,0:T(8,128)(2,1)S(1)}, bf16[32,3072]{1,0:T(8,128)(2,1)S(1)}, u32[]{:S(2)}, u32[]{:S(2)}) %collective-permute-start.36) | collective-permute-done | bytes 196640 | tf_op jit(solution)/shard_map/ppermute | solution.py:65
  133.2 2.9 %collective-permute-start.44 = (bf16[16,3072]{1,0:T(8,128)(2,1)S(1)}, bf16[16,3072]{1,0:T(8,128)(2,1)S(1)}, u32[]{:S(2)}, u32[]{:S(2)}) collective-permute-start(bf16[16,3072]{1,0:T(8,128)(2,1)S(1)} %get-tuple-element.80.refs_3_), channel_id=1, source_target_pairs={{0,8},{8,16},{16,24},{1,9},{9,17},{17,25},{2,10},{10,18},{18,26},{... | collective-permute-start | bytes 294920 | tf_op jit(solution)/shard_map/ppermute | solution.py:300
  (93 shorter events, 54.1 us)
Async XLA Ops:
  1.1 9.5 %collective-permute-start.11 = (bf16[64,1024]{1,0:T(8,128)(2,1)S(1)}, bf16[64,1024]{1,0:T(8,128)(2,1)S(1)}, u32[]{:S(2)}, u32[]{:S(2)}) collective-permute-start(bf16[64,1024]{1,0:T(8,128)(2,1)S(1)} %get-tuple-element.101.refs_0_), channel_id=1, source_target_pairs={{6,0},{7,1},{0,2},{1,3},{2,4},{3,5},{4,6},{5,7},{14,8},{15,9},{8,1... | collective-permute-start | bytes 393224 | tf_op jit(solution)/shard_map/ppermute | solution.py:70
  4.2 11.2 %collective-permute-start.10 = (bf16[64,1024]{1,0:T(8,128)(2,1)S(1)}, bf16[64,1024]{1,0:T(8,128)(2,1)S(1)}, u32[]{:S(2)}, u32[]{:S(2)}) collective-permute-start(bf16[64,1024]{1,0:T(8,128)(2,1)S(1)} %get-tuple-element.101.refs_0_), channel_id=1, source_target_pairs={{4,0},{5,1},{6,2},{7,3},{0,4},{1,5},{2,6},{3,7},{12,8},{13,9},{14,... | collective-permute-start | bytes 393224 | tf_op jit(solution)/shard_map/ppermute | solution.py:70
  6.8 8.6 %collective-permute-start.9 = (bf16[64,1024]{1,0:T(8,128)(2,1)S(1)}, bf16[64,1024]{1,0:T(8,128)(2,1)S(1)}, u32[]{:S(2)}, u32[]{:S(2)}) collective-permute-start(bf16[64,1024]{1,0:T(8,128)(2,1)S(1)} %get-tuple-element.101.refs_0_), channel_id=1, source_target_pairs={{2,0},{3,1},{4,2},{5,3},{6,4},{7,5},{0,6},{1,7},{10,8},{11,9},{12,... | collective-permute-start | bytes 393224 | tf_op jit(solution)/shard_map/ppermute | solution.py:70
  25.0 17.8 %collective-permute-start.18 = (bf16[256,1024]{1,0:T(8,128)(2,1)S(1)}, bf16[256,1024]{1,0:T(8,128)(2,1)S(1)}, u32[]{:S(2)}, u32[]{:S(2)}) collective-permute-start(bf16[256,1024]{1,0:T(8,128)(2,1)S(1)} %stack.4.refs_4_.refs_0_), channel_id=1, source_target_pairs={{0,1},{1,0},{2,3},{3,2},{4,5},{5,4},{6,7},{7,6},{8,9},{9,8},{10,11... | collective-permute-start | bytes 1572872 | tf_op jit(solution)/shard_map/ppermute | solution.py:288
  25.1 8.6 %collective-permute-start.8 = (bf16[64,1024]{1,0:T(8,128)(2,1)S(1)}, bf16[64,1024]{1,0:T(8,128)(2,1)S(1)}, u32[]{:S(2)}, u32[]{:S(2)}) collective-permute-start(bf16[64,1024]{1,0:T(8,128)(2,1)S(1)} %get-tuple-element.102.refs_0_), channel_id=1, source_target_pairs={{6,0},{7,1},{0,2},{1,3},{2,4},{3,5},{4,6},{5,7},{14,8},{15,9},{8,1... | collective-permute-start | bytes 393224 | tf_op jit(solution)/shard_map/ppermute | solution.py:70
  28.5 10.6 %collective-permute-start.7 = (bf16[64,1024]{1,0:T(8,128)(2,1)S(1)}, bf16[64,1024]{1,0:T(8,128)(2,1)S(1)}, u32[]{:S(2)}, u32[]{:S(2)}) collective-permute-start(bf16[64,1024]{1,0:T(8,128)(2,1)S(1)} %get-tuple-element.102.refs_0_), channel_id=1, source_target_pairs={{4,0},{5,1},{6,2},{7,3},{0,4},{1,5},{2,6},{3,7},{12,8},{13,9},{14,... | collective-permute-start | bytes 393224 | tf_op jit(solution)/shard_map/ppermute | solution.py:70
  29.9 9.2 %collective-permute-start.6 = (bf16[64,1024]{1,0:T(8,128)(2,1)S(1)}, bf16[64,1024]{1,0:T(8,128)(2,1)S(1)}, u32[]{:S(2)}, u32[]{:S(2)}) collective-permute-start(bf16[64,1024]{1,0:T(8,128)(2,1)S(1)} %get-tuple-element.102.refs_0_), channel_id=1, source_target_pairs={{2,0},{3,1},{4,2},{5,3},{6,4},{7,5},{0,6},{1,7},{10,8},{11,9},{12,... | collective-permute-start | bytes 393224 | tf_op jit(solution)/shard_map/ppermute | solution.py:70
  47.9 19.4 %collective-permute-start.24 = (bf16[256,1024]{1,0:T(8,128)(2,1)S(1)}, bf16[256,1024]{1,0:T(8,128)(2,1)S(1)}, u32[]{:S(2)}, u32[]{:S(2)}) collective-permute-start(bf16[256,1024]{1,0:T(8,128)(2,1)S(1)} %stack.5.refs_4_.refs_0_), channel_id=1, source_target_pairs={{0,1},{1,0},{2,3},{3,2},{4,5},{5,4},{6,7},{7,6},{8,9},{9,8},{10,11... | collective-permute-start | bytes 1572872 | tf_op jit(solution)/shard_map/ppermute | solution.py:288
  48.0 9.1 %collective-permute-start.5 = (bf16[64,1024]{1,0:T(8,128)(2,1)S(1)}, bf16[64,1024]{1,0:T(8,128)(2,1)S(1)}, u32[]{:S(2)}, u32[]{:S(2)}) collective-permute-start(bf16[64,1024]{1,0:T(8,128)(2,1)S(1)} %get-tuple-element.100.refs_0_), channel_id=1, source_target_pairs={{6,0},{7,1},{0,2},{1,3},{2,4},{3,5},{4,6},{5,7},{14,8},{15,9},{8,1... | collective-permute-start | bytes 393224 | tf_op jit(solution)/shard_map/ppermute | solution.py:70
  51.4 20.5 %collective-permute-start.22 = (bf16[64,3072]{1,0:T(8,128)(2,1)S(1)}, bf16[64,3072]{1,0:T(8,128)(2,1)S(1)}, u32[]{:S(2)}, u32[]{:S(2)}) collective-permute-start(bf16[64,3072]{1,0:T(8,128)(2,1)S(1)} %get-tuple-element.66), channel_id=1, source_target_pairs={{8,0},{0,8},{24,16},{16,24},{9,1},{1,9},{25,17},{17,25},{10,2},{2,... | collective-permute-start | bytes 1179656 | tf_op jit(solution)/shard_map/ppermute | solution.py:65
  52.7 19.2 %collective-permute-start.23 = (bf16[64,3072]{1,0:T(8,128)(2,1)S(1)}, bf16[64,3072]{1,0:T(8,128)(2,1)S(1)}, u32[]{:S(2)}, u32[]{:S(2)}) collective-permute-start(bf16[64,3072]{1,0:T(8,128)(2,1)S(1)} %get-tuple-element.67), channel_id=1, source_target_pairs={{16,0},{24,8},{0,16},{8,24},{17,1},{25,9},{1,17},{9,25},{18,2},{26... | collective-permute-start | bytes 1179656 | tf_op jit(solution)/shard_map/ppermute | solution.py:65
  53.7 8.9 %collective-permute-start.4 = (bf16[64,1024]{1,0:T(8,128)(2,1)S(1)}, bf16[64,1024]{1,0:T(8,128)(2,1)S(1)}, u32[]{:S(2)}, u32[]{:S(2)}) collective-permute-start(bf16[64,1024]{1,0:T(8,128)(2,1)S(1)} %get-tuple-element.100.refs_0_), channel_id=1, source_target_pairs={{4,0},{5,1},{6,2},{7,3},{0,4},{1,5},{2,6},{3,7},{12,8},{13,9},{14,... | collective-permute-start | bytes 393224 | tf_op jit(solution)/shard_map/ppermute | solution.py:70
  73.7 18.0 %collective-permute-start.30 = (bf16[256,1024]{1,0:T(8,128)(2,1)S(1)}, bf16[256,1024]{1,0:T(8,128)(2,1)S(1)}, u32[]{:S(2)}, u32[]{:S(2)}) collective-permute-start(bf16[256,1024]{1,0:T(8,128)(2,1)S(1)} %stack.6.refs_4_.refs_0_), channel_id=1, source_target_pairs={{0,1},{1,0},{2,3},{3,2},{4,5},{5,4},{6,7},{7,6},{8,9},{9,8},{10,11... | collective-permute-start | bytes 1572872 | tf_op jit(solution)/shard_map/ppermute | solution.py:288
  75.0 21.4 %collective-permute-start.28 = (bf16[64,3072]{1,0:T(8,128)(2,1)S(1)}, bf16[64,3072]{1,0:T(8,128)(2,1)S(1)}, u32[]{:S(2)}, u32[]{:S(2)}) collective-permute-start(bf16[64,3072]{1,0:T(8,128)(2,1)S(1)} %get-tuple-element.75), channel_id=1, source_target_pairs={{8,0},{0,8},{24,16},{16,24},{9,1},{1,9},{25,17},{17,25},{10,2},{2,... | collective-permute-start | bytes 1179656 | tf_op jit(solution)/shard_map/ppermute | solution.py:65
  76.2 20.2 %collective-permute-start.29 = (bf16[64,3072]{1,0:T(8,128)(2,1)S(1)}, bf16[64,3072]{1,0:T(8,128)(2,1)S(1)}, u32[]{:S(2)}, u32[]{:S(2)}) collective-permute-start(bf16[64,3072]{1,0:T(8,128)(2,1)S(1)} %get-tuple-element.76), channel_id=1, source_target_pairs={{16,0},{24,8},{0,16},{8,24},{17,1},{25,9},{1,17},{9,25},{18,2},{26... | collective-permute-start | bytes 1179656 | tf_op jit(solution)/shard_map/ppermute | solution.py:65
  77.1 10.1 %collective-permute-start.1 = (bf16[64,1024]{1,0:T(8,128)(2,1)S(1)}, bf16[64,1024]{1,0:T(8,128)(2,1)S(1)}, u32[]{:S(2)}, u32[]{:S(2)}) collective-permute-start(bf16[64,1024]{1,0:T(8,128)(2,1)S(1)} %get-tuple-element.99.refs_0_), channel_id=1, source_target_pairs={{4,0},{5,1},{6,2},{7,3},{0,4},{1,5},{2,6},{3,7},{12,8},{13,9},{14,... | collective-permute-start | bytes 393224 | tf_op jit(solution)/shard_map/ppermute | solution.py:70
  98.3 9.8 %collective-permute-start.31 = (bf16[256,1024]{1,0:T(8,128)(2,1)S(1)}, bf16[256,1024]{1,0:T(8,128)(2,1)S(1)}, u32[]{:S(2)}, u32[]{:S(2)}) collective-permute-start(bf16[256,1024]{1,0:T(8,128)(2,1)S(1)} %stack.7.refs_8_.refs_0_), channel_id=1, source_target_pairs={{0,1},{1,0},{2,3},{3,2},{4,5},{5,4},{6,7},{7,6},{8,9},{9,8},{10,11... | collective-permute-start | bytes 1572872 | tf_op jit(solution)/shard_map/ppermute | solution.py:288
  100.5 15.1 %collective-permute-start.38 = (bf16[64,3072]{1,0:T(8,128)(2,1)S(1)}, bf16[64,3072]{1,0:T(8,128)(2,1)S(1)}, u32[]{:S(2)}, u32[]{:S(2)}) collective-permute-start(bf16[64,3072]{1,0:T(8,128)(2,1)S(1)} %get-tuple-element.88), channel_id=1, source_target_pairs={{8,0},{0,8},{24,16},{16,24},{9,1},{1,9},{25,17},{17,25},{10,2},{2,... | collective-permute-start | bytes 1179656 | tf_op jit(solution)/shard_map/ppermute | solution.py:65
  101.5 15.2 %collective-permute-start.39 = (bf16[64,3072]{1,0:T(8,128)(2,1)S(1)}, bf16[64,3072]{1,0:T(8,128)(2,1)S(1)}, u32[]{:S(2)}, u32[]{:S(2)}) collective-permute-start(bf16[64,3072]{1,0:T(8,128)(2,1)S(1)} %get-tuple-element.89), channel_id=1, source_target_pairs={{16,0},{24,8},{0,16},{8,24},{17,1},{25,9},{1,17},{9,25},{18,2},{26... | collective-permute-start | bytes 1179656 | tf_op jit(solution)/shard_map/ppermute | solution.py:65
  111.5 19.5 %collective-permute-start.34 = (bf16[64,3072]{1,0:T(8,128)(2,1)S(1)}, bf16[64,3072]{1,0:T(8,128)(2,1)S(1)}, u32[]{:S(2)}, u32[]{:S(2)}) collective-permute-start(bf16[64,3072]{1,0:T(8,128)(2,1)S(1)} %get-tuple-element.82), channel_id=1, source_target_pairs={{8,0},{0,8},{24,16},{16,24},{9,1},{1,9},{25,17},{17,25},{10,2},{2,... | collective-permute-start | bytes 1179656 | tf_op jit(solution)/shard_map/ppermute | solution.py:65
  112.7 18.4 %collective-permute-start.35 = (bf16[64,3072]{1,0:T(8,128)(2,1)S(1)}, bf16[64,3072]{1,0:T(8,128)(2,1)S(1)}, u32[]{:S(2)}, u32[]{:S(2)}) collective-permute-start(bf16[64,3072]{1,0:T(8,128)(2,1)S(1)} %get-tuple-element.84), channel_id=1, source_target_pairs={{16,0},{24,8},{0,16},{8,24},{17,1},{25,9},{1,17},{9,25},{18,2},{26... | collective-permute-start | bytes 1179656 | tf_op jit(solution)/shard_map/ppermute | solution.py:65
  113.6 15.2 %collective-permute-start.36 = (bf16[32,3072]{1,0:T(8,128)(2,1)S(1)}, bf16[32,3072]{1,0:T(8,128)(2,1)S(1)}, u32[]{:S(2)}, u32[]{:S(2)}) collective-permute-start(bf16[32,3072]{1,0:T(8,128)(2,1)S(1)} %get-tuple-element.85), channel_id=1, source_target_pairs={{16,0},{24,8},{0,16},{8,24},{17,1},{25,9},{1,17},{9,25},{18,2},{26... | collective-permute-start | bytes 589832 | tf_op jit(solution)/shard_map/ppermute | solution.py:65
  115.6 14.3 %collective-permute-start.37 = (bf16[32,3072]{1,0:T(8,128)(2,1)S(1)}, bf16[32,3072]{1,0:T(8,128)(2,1)S(1)}, u32[]{:S(2)}, u32[]{:S(2)}) collective-permute-start(bf16[32,3072]{1,0:T(8,128)(2,1)S(1)} %get-tuple-element.78.refs_4_), channel_id=1, source_target_pairs={{8,0},{0,8},{24,16},{16,24},{9,1},{1,9},{25,17},{17,25},{10,2},{2,... | collective-permute-start | bytes 589832 | tf_op jit(solution)/shard_map/ppermute | solution.py:65
  116.8 19.3 %collective-permute-start.42 = (bf16[32,3072]{1,0:T(8,128)(2,1)S(1)}, bf16[32,3072]{1,0:T(8,128)(2,1)S(1)}, u32[]{:S(2)}, u32[]{:S(2)}) collective-permute-start(bf16[32,3072]{1,0:T(8,128)(2,1)S(1)} %get-tuple-element.94), channel_id=1, source_target_pairs={{16,0},{24,8},{0,16},{8,24},{17,1},{25,9},{1,17},{9,25},{18,2},{26... | collective-permute-start | bytes 589832 | tf_op jit(solution)/shard_map/ppermute | solution.py:65
  (23 other events, 221.5 us)

commit v3 on v2

v3 whole, which is shorter than its diff:
```python
import functools

import jax
import jax.numpy as jnp
from jax import lax
from jax.experimental import pallas as pl
from jax.experimental.pallas import tpu as pltpu
from jax.sharding import PartitionSpec as P

CORES = 2
RIM = 16
STEP = 72
LANES = 128
VMEM = pl.BlockSpec(memory_space=pltpu.VMEM)
HBM = pl.BlockSpec(memory_space=pl.ANY)
BF16, F32 = jnp.bfloat16, jnp.float32


def params(mib=16):
    return pltpu.CompilerParams(vmem_limit_bytes=mib * 2**20)


class Order:
    def __init__(self):
        self.last = None
        self.wait = []

    def call(self, kernel, args, shapes, name, scratch=(), specs=None, after=(), shown=0):
        specs = [VMEM] * len(args) if specs is None else specs
        extra = [*([] if self.last is None else [self.last]), *self.wait, *after]
        self.wait = []
        count = len(args)

        def body(*refs):
            kernel(*refs[:count], *refs[count + len(extra) :])

        outs = pl.pallas_call(
            body,
            in_specs=specs + [HBM] * len(extra),
            out_specs=[VMEM] * len(shapes),
            out_shape=[pltpu.VMEM(s, t) for s, t in shapes],
            scratch_shapes=list(scratch),
            compiler_params=params(),
            cost_estimate=pl.CostEstimate(flops=shown, bytes_accessed=0, transcendentals=0),
            name=name,
        )(*args, *extra)
        self.last = outs[-1]
        return list(outs)


def side(n):
    x = 1
    while x * x < n:
        x *= 2
    return n // x, x


def shift_rows(block, shape, dy, dx):
    ys, xs = shape
    route = []
    for y in range(ys):
        for x in range(xs):
            route.append((((y + dy) % ys) * xs + (x + dx) % xs, y * xs + x))
    return lax.ppermute(block, "row", route)


def widen_kernel(own, other, *outs):
    e = own.shape[1]
    core = lax.rem(lax.axis_index("col"), CORES)
    row = own.shape[0]
    for o in outs:
        row -= o.shape[0]
        for k in range(CORES):

            @pl.when(core == k)
            def _():
                o[:, k * e : (k + 1) * e] = own[row : row + o.shape[0]]
                o[:, (1 - k) * e : (2 - k) * e] = other[row : row + o.shape[0]]


def widen(order, own, other, sizes):
    shapes = [((n, CORES * own.shape[1]), BF16) for n in sizes]
    return order.call(widen_kernel, [own, other], shapes, "widen")


def gather(piece):
    count, cols = lax.axis_size("row"), lax.axis_size("col")
    planes = cols // CORES
    assert count == planes and count & (count - 1) == 0

    def place(row, plane, core):
        return row * cols + plane * CORES + core

    blocks = []
    for a in range(count // CORES):
        route = []
        for row in range(count):
            for plane in range(planes):
                for core in range(CORES):
                    route.append((place(row, plane, core), place(plane, row ^ (a * CORES + core), core)))
        blocks.append(lax.ppermute(piece, ("row", "col"), route))
    return blocks


def cut_kernel(sizes, count, *refs):
    outs = iter(refs[count:])
    for block in refs[:count]:
        end = block.shape[0]
        for n in sizes:
            next(outs)[...] = block[end - n : end]
            end -= n


def cut(order, blocks, sizes):
    e = blocks[0].shape[1]
    kernel = functools.partial(cut_kernel, sizes, len(blocks))
    outs = order.call(kernel, blocks, [((n, e), BF16) for _ in blocks for n in sizes], "cut")
    return [outs[i :: len(sizes)] for i in range(len(sizes))]


def stack_halves(shape, mine, other, out):
    ys, xs = shape
    h = out.shape[1]
    me = lax.axis_index("row")
    plane = lax.axis_index("col") // CORES
    core = lax.rem(lax.axis_index("col"), CORES)
    sent = (xs - 1) * ys + (ys - 1) * xs
    for a in range(len(mine)):
        for blocks, j in ((mine, a * CORES + core), (other, a * CORES + 1 - core)):
            row = lax.bitwise_xor(plane, j)
            dy = lax.rem(row // xs - me // xs + ys, ys)
            dx = lax.rem(lax.rem(row, xs) - lax.rem(me, xs) + xs, xs)
            out[jnp.where(dx > 0, (dx - 1) * ys + dy, sent + dy)] = blocks[a][:h]
            out[jnp.where(dy > 0, (xs - 1) * ys + (dy - 1) * xs + dx, sent + ys + dx)] = blocks[a][h:]


def fetch_kernel(w_ref, o_ref, sems):
    copies = [pltpu.make_async_copy(w_ref.at[g], o_ref.at[g], sems.at[g]) for g in range(3)]
    for c in copies:
        c.start()
    for c in copies:
        c.wait()


def fetch(order, w_in):
    w = pltpu.with_memory_space_constraint(w_in.transpose(1, 0, 2), pltpu.HBM)
    scratch = [pltpu.SemaphoreType.DMA((3,))]
    return order.call(fetch_kernel, [w], [(w.shape, BF16)], "fetch_w", scratch, specs=[HBM])[0]


def project_kernel(tn, shape, *refs):
    count = shape[0] * shape[1] // CORES
    mine, other, w_ref = refs[:count], refs[count : 2 * count], refs[2 * count]
    *outs, halves = refs[2 * count + 1 :]
    stack_halves(shape, mine, other, halves)
    parts, h, e = halves.shape
    cols = w_ref.shape[2]
    for g in range(3):
        for c in range(0, cols, tn):
            acc = jnp.dot(halves[...].reshape(parts * h, e), w_ref[g, :, c : c + tn], preferred_element_type=F32)
            at = 0
            for o in outs:
                o[:, g * cols + c : g * cols + c + tn] = acc[at : at + o.shape[0]].astype(o.dtype)
                at += o.shape[0]


def project(order, mine, other, w, shape):
    ys, xs = shape
    n, e = mine[0].shape
    h = n // 2
    cols = w.shape[2]
    counts = [ys] * (xs - 1) + [xs] * (ys - 1) + [ys, xs]
    shapes = [((k * h, 3 * cols), BF16 if i < xs + ys - 2 else F32) for i, k in enumerate(counts)]
    scratch = [pltpu.VMEM((2 * xs * ys, h, e), BF16)]
    kernel = functools.partial(project_kernel, min(cols, 256), shape)
    outs = order.call(kernel, [*mine, *other, w], shapes, "project", scratch)
    got_a = [shift_rows(s, shape, 0, -dx) for dx, s in enumerate(outs[: xs - 1], 1)]
    got_c = [shift_rows(s, shape, -dy, 0) for dy, s in enumerate(outs[xs - 1 : -2], 1)]
    return [outs[-2], *got_a], [outs[-1], *got_c]


def middle_kernel(count_a, count_c, *refs):
    keep_a, got_a = refs[0], refs[1 : 1 + count_a]
    keep_c, got_c = refs[1 + count_a], refs[2 + count_a : 2 + count_a + count_c]
    outs = refs[2 + count_a + count_c :]
    h = outs[0].shape[0]
    for keep, got, mids in ((keep_a, got_a, outs[:count_c]), (keep_c, got_c, outs[count_c:])):
        for i, mid in enumerate(mids, 1):
            total = keep[i * h : (i + 1) * h]
            for g in got:
                total = total + g[i * h : (i + 1) * h].astype(F32)
            mid[...] = total.astype(BF16)


def middle(order, terms, h, shape):
    ys, xs = shape
    first, second = terms
    n = first[0].shape[1]
    mids = order.call(
        functools.partial(middle_kernel, xs - 1, ys - 1), [*first, *second], [((h, n), BF16)] * (xs + ys - 2), "middle"
    )
    last_a = [shift_rows(s, shape, -dy, 0) for dy, s in enumerate(mids[: ys - 1], 1)]
    last_c = [shift_rows(s, shape, 0, -dx) for dx, s in enumerate(mids[ys - 1 :], 1)]
    return [*first, *last_a], [*second, *last_c]


def finish_kernel(top, bottom, n, count_a, count_c, *refs):
    refs = list(refs)
    terms = [refs[:count_a], refs[count_a : count_a + count_c]]
    del refs[: count_a + count_c]
    fin, fmix = refs.pop(0), refs.pop(0)
    follow = refs.pop(0) if not bottom else None
    rim = refs.pop(0) if top else None
    out = refs.pop(0)
    lead = refs.pop(0) if not top else None
    tail = refs.pop(0) if bottom else None
    ext, prod = refs
    h = n // 2
    for i, group in enumerate(terms):
        total = group[0][:h]
        for g in group[1:]:
            total = total + g[:h].astype(F32)
        ext[RIM + i * h : RIM + (i + 1) * h] = total
    if follow is not None:
        ext[RIM + n : RIM + n + RIM] = follow[...]
    if rim is not None:
        ext[:RIM] = rim[...].astype(F32)
    if lead is not None:
        lead[...] = ext[RIM : 2 * RIM]
    if tail is not None:
        tail[...] = ext[n : n + RIM].astype(BF16)
    cols = fmix.shape[1]
    first = RIM if top else 2 * RIM
    rows = out.shape[0]
    step = max(s for s in range(16, STEP + 1, 8) if rows % s == 0)

    def column(c, _):
        at = pl.multiple_of(c * LANES, LANES)

        def conv(g, start, count):
            where = pl.ds(pl.multiple_of(g * cols + at, LANES), LANES)
            total = fin[g, 0:1, pl.ds(at, LANES)] * ext[start : start + count, where]
            for s in range(1, 7):
                total = total + fin[g, s : s + 1, pl.ds(at, LANES)] * ext[start - s : start - s + count, where]
            return total

        for r in range(0, rows, step):
            base = first + r
            prod[: step + 8] = conv(1, base - 8, step + 8) * conv(2, base - 8, step + 8)
            mix = fmix[0:1, pl.ds(at, LANES)] * prod[8 : 8 + step]
            for s in range(1, 7):
                mix = mix + fmix[s : s + 1, pl.ds(at, LANES)] * prod[8 - s : 8 - s + step]
            out[r : r + step, pl.ds(at, LANES)] = (conv(0, base, step) * mix).astype(BF16)
        return 0

    lax.fori_loop(0, cols // LANES, column, 0)


def finish(order, top, bottom, n, terms, fin, fmix, follow, rim):
    width = terms[0][0].shape[1]
    cols = fmix.shape[1]
    rows = n + (RIM if top else 0) - (RIM if bottom else 0)
    args = [*terms[0], *terms[1], fin, fmix]
    args += [follow] if not bottom else []
    args += [rim] if top else []
    shapes = [((rows, cols), BF16)]
    shapes += [((RIM, width), F32)] if not top else []
    shapes += [((RIM, width), BF16)] if bottom else []
    kernel = functools.partial(finish_kernel, top, bottom, n, len(terms[0]), len(terms[1]))
    scratch = [pltpu.VMEM((n + 2 * RIM, width), F32), pltpu.VMEM((STEP + 8, LANES), F32)]
    return order.call(kernel, args, shapes, "finish", scratch, shown=50 * 10**9 if bottom else 0)


CHUNKS = ((3,), (3, 2))
PLAN = ("W", "K0", "C0", "J0", "K1", "C1", "C2", "M0", "J1", "F0", "J2", "M1", "M2", "F1", "F2")


def per_device(tokens, w_in, filt_in, filt_mix):
    rows = tokens.shape[0]
    cols = lax.axis_size("col")
    count = lax.axis_size("row")
    shape = side(count)
    order = Order()
    fin = filt_in.transpose(1, 0, 2)
    swap = [(c, c ^ 1) for c in range(cols)]
    parts = [[rows * k // 8 for k in chunk] for chunk in CHUNKS]
    sizes = sum(parts, [])
    last = len(sizes) - 1
    wide = widen(order, tokens, lax.ppermute(tokens, "col", swap), [sum(p) for p in parts])
    blocks = [gather(piece) for piece in wide]
    mine, other, terms, outs = [], {}, {}, {}
    follow, rim = None, None
    for step in PLAN:
        kind, i = step[0], int(step[1:] or 0)
        if kind == "W":
            w = fetch(order, w_in)
        elif kind == "K":
            mine += cut(order, blocks[i], parts[i])
        elif kind == "C":
            other[i] = [lax.ppermute(b, "col", swap) for b in mine[i]]
        elif kind == "J":
            terms[i] = project(order, mine[i], other[i], w, shape)
        elif kind == "M":
            terms[i] = middle(order, terms[i], sizes[i] // 2, shape)
        else:
            got = finish(order, i == last, i == 0, sizes[i], terms[i], fin, filt_mix, follow, rim)
            outs[i] = got.pop(0)
            if i < last:
                follow = got.pop(0)
            if i == 0:
                rim = lax.ppermute(got.pop(0), "row", [(r, r + 1) for r in range(count - 1)])
    return jnp.concatenate([outs[i] for i in reversed(range(len(sizes)))], axis=0)


def solution(mesh):
    return jax.shard_map(
        per_device,
        mesh=mesh,
        in_specs=(P("row", "col"), P("row", None, "col"), P(None, None, "col"), P(None, "col")),
        out_specs=P("row", "col"),
        check_vma=False,
    )
```

time: 141 us -> 114 us (0.81)
  starting transfers between devices: 57.2 us -> 37.5 us
  waiting for transfers between devices: 57.7 us -> 50.7 us
    ppermute x28 -> x12, starting transfers between devices: 31.1 us -> 9.73 us  [shift_rows(): return lax.ppermute(block, 'row', route)]
    ppermute x16 -> x11, waiting for transfers between devices: 33.3 us -> 20.2 us  [the longest x4 18.4 us: gather(): blocks.append(lax.ppermute(piece, ('row', 'col'), route))]
    ppermute x28 -> x12, waiting for transfers between devices: 23.7 us -> 29.3 us  [shift_rows(): return lax.ppermute(block, 'row', route)]
    ppermute x16 -> x11, starting transfers between devices: 23.2 us -> 25 us  [the longest x4 22.8 us: gather(): blocks.append(lax.ppermute(piece, ('row', 'col'), route))]
    pallas_call x21 -> x13, Pallas kernels: 23.8 us -> 23.5 us  [call(): pl.pallas_call(body, in_specs=specs + [HBM] * len(extra), out_specs=[VMEM...]
  transfers between devices with their start and end apart: 45 -> 24, of which waited for: 22 -> 11; matrix products, arithmetic and copies ran while one was open for 0% -> 0% of each run, Pallas kernels for 16% -> 19%
where the time goes in v3:
time: 114 us
  waiting for transfers between devices  50.7 us (44%)
  starting transfers between devices  37.5 us (33%)
  Pallas kernels  23.5 us (21%)
    ppermute x12, waiting for transfers between devices, shift_rows(): return lax.ppermute(block, 'row', route)  29.3 us
    pallas_call x13, Pallas kernels, call(): pl.pallas_call(body, in_specs=specs + [HBM] * len(extra), out_specs=[VMEM...  23.5 us
    ppermute x4, starting transfers between devices, gather(): blocks.append(lax.ppermute(piece, ('row', 'col'), route))  22.8 us
    ppermute x4, waiting for transfers between devices, gather(): blocks.append(lax.ppermute(piece, ('row', 'col'), route))  18.4 us
    ppermute x12, starting transfers between devices, shift_rows(): return lax.ppermute(block, 'row', route)  9.73 us
    ppermute x1, starting transfers between devices, per_device(): lax.ppermute(got.pop(0), 'row', [(r, r + 1) for r in range(count - 1)])  2.73 us
  transfers between devices with their start and end apart: 24, of which 11 were waited for; matrix products, arithmetic and copies ran while one was open for 0% of the time, Pallas kernels for 19%

profile of v3, /device:TPU:0, one launch (start us, length us, event | category | flops | bytes accessed | tf_op | source)
XLA Modules:
  0.0 113.7 jit_solution(17727560348206413082)
XLA Ops:
  0.5 1.7 %collective-permute-done.refs_1_ = bf16[256,1024]{1,0:T(8,128)(2,1)S(1)} collective-permute-done((bf16[256,1024]{1,0:T(8,128)(2,1)}, bf16[256,1024]{1,0:T(8,128)(2,1)S(1)}, u32[]{:S(2)}, u32[]{:S(2)}) %collective-permute-start) | collective-permute-done | bytes 524320 | tf_op jit(solution)/shard_map/ppermute | solution.py:289
  4.0 6.5 %collective-permute-start.4 = (bf16[96,2048]{1,0:T(8,128)(2,1)S(1)}, bf16[96,2048]{1,0:T(8,128)(2,1)S(1)}, u32[]{:S(2)}, u32[]{:S(2)}) collective-permute-start(bf16[96,2048]{1,0:T(8,128)(2,1)S(1)} %get-tuple-element.37), channel_id=1, source_target_pairs={{0,4},{1,7},{2,12},{3,15},{4,20},{5,23},{6,28},{7,31},{8,6},{9,5},... | collective-permute-start | bytes 1179656 | tf_op jit(solution)/shard_map/ppermute | solution.py:101
  10.5 4.7 %fetch_w.1.refs_2_.refs_4_ = bf16[3,2048,1024]{2,1,0:T(8,128)(2,1)S(1)} custom-call(bf16[3,2048,1024]{2,1,0:T(8,128)(2,1)} %bitcast.5, bf16[160,2048]{1,0:T(8,128)(2,1)S(1)} %get-tuple-element.36.refs_1_), custom_call_target="tpu_custom_call" | custom-call | tf_op jit(solution)/shard_map/fetch_w/pallas_call | solution.py:37
  15.2 5.4 %collective-permute-done.4.refs_1_ = bf16[96,2048]{1,0:T(8,128)(2,1)S(1)} collective-permute-done((bf16[96,2048]{1,0:T(8,128)(2,1)S(1)}, bf16[96,2048]{1,0:T(8,128)(2,1)S(1)}, u32[]{:S(2)}, u32[]{:S(2)}) %collective-permute-start.4) | collective-permute-done | bytes 393248 | tf_op jit(solution)/shard_map/ppermute | solution.py:101
  22.1 14.9 %collective-permute-start.2 = (bf16[160,2048]{1,0:T(8,128)(2,1)S(1)}, bf16[160,2048]{1,0:T(8,128)(2,1)S(1)}, u32[]{:S(2)}, u32[]{:S(2)}) collective-permute-start(bf16[160,2048]{1,0:T(8,128)(2,1)S(1)} %get-tuple-element.36.refs_1_), channel_id=1, source_target_pairs={{0,4},{1,7},{2,12},{3,15},{4,20},{5,23},{6,28},{7,31},{8,6},{9,5},... | collective-permute-start | bytes 1966088 | tf_op jit(solution)/shard_map/ppermute | solution.py:101
  37.0 5.2 %project.3 = (bf16[96,3072]{1,0:T(8,128)(2,1)S(1)}, bf16[96,3072]{1,0:T(8,128)(2,1)S(1)}, f32[96,3072]{1,0:T(8,128)S(1)}, f32[96,3072]{1,0:T(8,128)S(1)}) custom-call(bf16[96,2048]{1,0:T(8,128)(2,1)S(1)} %get-tuple-element.38.refs_0_, bf16[96,2048]{1,0:T(8,128)(2,1)S(1)} %get-tuple-element.39.refs_1_.refs_5_, ...), custom_call_target="tpu_custom_call" | custom-call | tf_op jit(solution)/shard_map/project/pallas_call | solution.py:37
  42.4 13.0 %collective-permute-done.2.refs_1_ = bf16[160,2048]{1,0:T(8,128)(2,1)S(1)} collective-permute-done((bf16[160,2048]{1,0:T(8,128)(2,1)S(1)}, bf16[160,2048]{1,0:T(8,128)(2,1)S(1)}, u32[]{:S(2)}, u32[]{:S(2)}) %collective-permute-start.2) | collective-permute-done | bytes 655392 | tf_op jit(solution)/shard_map/ppermute | solution.py:101
  56.0 11.1 %collective-permute-done.10.refs_3_.refs_4_ = bf16[96,3072]{1,0:T(8,128)(2,1)S(1)} collective-permute-done((bf16[96,3072]{1,0:T(8,128)(2,1)S(1)}, bf16[96,3072]{1,0:T(8,128)(2,1)S(1)}, u32[]{:S(2)}, u32[]{:S(2)}) %collective-permute-start.10) | collective-permute-done | bytes 589856 | tf_op jit(solution)/shard_map/ppermute | solution.py:64
  67.2 2.5 %collective-permute-start.11 = (bf16[48,3072]{1,0:T(8,128)(2,1)S(1)}, bf16[48,3072]{1,0:T(8,128)(2,1)S(1)}, u32[]{:S(2)}, u32[]{:S(2)}) collective-permute-start(bf16[48,3072]{1,0:T(8,128)(2,1)S(1)} %get-tuple-element.46), channel_id=1, source_target_pairs={{16,0},{24,8},{0,16},{8,24},{17,1},{25,9},{1,17},{9,25},{18,2},{26... | collective-permute-start | bytes 884744 | tf_op jit(solution)/shard_map/ppermute | solution.py:64
  70.5 5.2 %project.4 = (bf16[96,3072]{1,0:T(8,128)(2,1)S(1)}, bf16[96,3072]{1,0:T(8,128)(2,1)S(1)}, f32[96,3072]{1,0:T(8,128)S(1)}, f32[96,3072]{1,0:T(8,128)S(1)}) custom-call(bf16[96,2048]{1,0:T(8,128)(2,1)S(1)} %get-tuple-element.48.refs_0_, bf16[96,2048]{1,0:T(8,128)(2,1)S(1)} %get-tuple-element.49.refs_1_, bf16[96,2048]{1,0:T(8,128)(2,1)S(1)} %collective-permute-done.13.refs_2_, ...), custom_call_target="tpu_custom_call" | custom-call | tf_op jit(solution)/shard_map/project/pallas_call | solution.py:37
  75.6 1.9 %collective-permute-start.17 = (bf16[96,3072]{1,0:T(8,128)(2,1)S(1)}, bf16[96,3072]{1,0:T(8,128)(2,1)S(1)}, u32[]{:S(2)}, u32[]{:S(2)}) collective-permute-start(bf16[96,3072]{1,0:T(8,128)(2,1)S(1)} %get-tuple-element.57), channel_id=1, source_target_pairs={{8,0},{0,8},{24,16},{16,24},{9,1},{1,9},{25,17},{17,25},{10,2},{2,... | collective-permute-start | bytes 1769480 | tf_op jit(solution)/shard_map/ppermute | solution.py:64
  77.6 1.5 %finish.3 = (bf16[80,1024]{1,0:T(8,128)(2,1)S(1)}, f32[16,3072]{1,0:T(8,128)S(1)}, bf16[16,3072]{1,0:T(8,128)(2,1)S(1)}) custom-call(f32[96,3072]{1,0:T(8,128)S(1)} %get-tuple-element.43.refs_0_, bf16[96,3072]{1,0:T(8,128)(2,1)S(1)} %collective-permute-done.9.refs_1_, bf16[48,3072]{1,0:T(8,128)(2,1)S(1)} %collective-permute-done.11.refs_2_, ...), custom_call_target="tpu_custom_call" | custom-call | flops 49999998976 | tf_op jit(solution)/shard_map/finish/pallas_call | solution.py:37
  79.1 3.5 %project.5 = (bf16[64,3072]{1,0:T(8,128)(2,1)S(1)}, bf16[64,3072]{1,0:T(8,128)(2,1)S(1)}, f32[64,3072]{1,0:T(8,128)S(1)}, f32[64,3072]{1,0:T(8,128)S(1)}) custom-call(bf16[64,2048]{1,0:T(8,128)(2,1)S(1)} %get-tuple-element.41.refs_0_, bf16[64,2048]{1,0:T(8,128)(2,1)S(1)} %get-tuple-element.42.refs_4_.refs_1_, ...), custom_call_target="tpu_custom_call" | custom-call | tf_op jit(solution)/shard_map/project/pallas_call | solution.py:37
  84.8 7.0 %collective-permute-done.17.refs_1_ = bf16[96,3072]{1,0:T(8,128)(2,1)S(1)} collective-permute-done((bf16[96,3072]{1,0:T(8,128)(2,1)S(1)}, bf16[96,3072]{1,0:T(8,128)(2,1)S(1)}, u32[]{:S(2)}, u32[]{:S(2)}) %collective-permute-start.17) | collective-permute-done | bytes 589856 | tf_op jit(solution)/shard_map/ppermute | solution.py:64
  91.9 1.9 %collective-permute-done.18.refs_3_.refs_4_ = bf16[96,3072]{1,0:T(8,128)(2,1)S(1)} collective-permute-done((bf16[96,3072]{1,0:T(8,128)(2,1)S(1)}, bf16[96,3072]{1,0:T(8,128)(2,1)S(1)}, u32[]{:S(2)}, u32[]{:S(2)}) %collective-permute-start.18) | collective-permute-done | bytes 589856 | tf_op jit(solution)/shard_map/ppermute | solution.py:64
  94.0 1.2 %collective-permute-start.22 = (bf16[48,3072]{1,0:T(8,128)(2,1)S(1)}, bf16[48,3072]{1,0:T(8,128)(2,1)S(1)}, u32[]{:S(2)}, u32[]{:S(2)}) collective-permute-start(bf16[48,3072]{1,0:T(8,128)(2,1)S(1)} %get-tuple-element.59.refs_4_), channel_id=1, source_target_pairs={{8,0},{0,8},{24,16},{16,24},{9,1},{1,9},{25,17},{17,25},{10,2},{2,... | collective-permute-start | bytes 884744 | tf_op jit(solution)/shard_map/ppermute | solution.py:64
  95.2 5.1 %collective-permute-done.15.refs_1_ = bf16[64,3072]{1,0:T(8,128)(2,1)S(1)} collective-permute-done((bf16[64,3072]{1,0:T(8,128)(2,1)S(1)}, bf16[64,3072]{1,0:T(8,128)(2,1)S(1)}, u32[]{:S(2)}, u32[]{:S(2)}) %collective-permute-start.15) | collective-permute-done | bytes 393248 | tf_op jit(solution)/shard_map/ppermute | solution.py:64
  100.3 1.9 %collective-permute-done.16.refs_3_.refs_4_ = bf16[64,3072]{1,0:T(8,128)(2,1)S(1)} collective-permute-done((bf16[64,3072]{1,0:T(8,128)(2,1)S(1)}, bf16[64,3072]{1,0:T(8,128)(2,1)S(1)}, u32[]{:S(2)}, u32[]{:S(2)}) %collective-permute-start.16) | collective-permute-done | bytes 393248 | tf_op jit(solution)/shard_map/ppermute | solution.py:64
  102.4 1.2 %collective-permute-start.20 = (bf16[32,3072]{1,0:T(8,128)(2,1)S(1)}, bf16[32,3072]{1,0:T(8,128)(2,1)S(1)}, u32[]{:S(2)}, u32[]{:S(2)}) collective-permute-start(bf16[32,3072]{1,0:T(8,128)(2,1)S(1)} %get-tuple-element.61.refs_9_), channel_id=1, source_target_pairs={{8,0},{0,8},{24,16},{16,24},{9,1},{1,9},{25,17},{17,25},{10,2},{2,... | collective-permute-start | bytes 589832 | tf_op jit(solution)/shard_map/ppermute | solution.py:64
  103.6 2.7 %collective-permute-start.23 = (bf16[16,3072]{1,0:T(8,128)(2,1)S(1)}, bf16[16,3072]{1,0:T(8,128)(2,1)S(1)}, u32[]{:S(2)}, u32[]{:S(2)}) collective-permute-start(bf16[16,3072]{1,0:T(8,128)(2,1)S(1)} %get-tuple-element.51.refs_5_), channel_id=1, source_target_pairs={{0,8},{8,16},{16,24},{1,9},{9,17},{17,25},{2,10},{10,18},{18,26},{... | collective-permute-start | bytes 294920 | tf_op jit(solution)/shard_map/ppermute | solution.py:311
  106.3 2.2 %collective-permute-done.21.refs_2_ = bf16[48,3072]{1,0:T(8,128)(2,1)S(1)} collective-permute-done((bf16[48,3072]{1,0:T(8,128)(2,1)S(1)}, bf16[48,3072]{1,0:T(8,128)(2,1)S(1)}, u32[]{:S(2)}, u32[]{:S(2)}) %collective-permute-start.21) | collective-permute-done | bytes 294944 | tf_op jit(solution)/shard_map/ppermute | solution.py:64
  108.5 1.7 %finish.4 = (bf16[96,1024]{1,0:T(8,128)(2,1)S(1)}, f32[16,3072]{1,0:T(8,128)S(1)}) custom-call(f32[96,3072]{1,0:T(8,128)S(1)} %get-tuple-element.56.refs_0_, bf16[96,3072]{1,0:T(8,128)(2,1)S(1)} %collective-permute-done.17.refs_1_, bf16[48,3072]{1,0:T(8,128)(2,1)S(1)} %collective-permute-done.21.refs_2_, ...), custom_call_target="tpu_custom_call" | custom-call | tf_op jit(solution)/shard_map/finish/pallas_call | solution.py:37
  110.2 1.2 %collective-permute-done.23.refs_9_ = bf16[16,3072]{1,0:T(8,128)(2,1)S(1)} collective-permute-done((bf16[16,3072]{1,0:T(8,128)(2,1)S(1)}, bf16[16,3072]{1,0:T(8,128)(2,1)S(1)}, u32[]{:S(2)}, u32[]{:S(2)}) %collective-permute-start.23) | collective-permute-done | bytes 98336 | tf_op jit(solution)/shard_map/ppermute | solution.py:311
  111.5 1.3 %finish.5 = bf16[80,1024]{1,0:T(8,128)(2,1)S(1)} custom-call(f32[64,3072]{1,0:T(8,128)S(1)} %get-tuple-element.52.refs_0_, bf16[64,3072]{1,0:T(8,128)(2,1)S(1)} %collective-permute-done.15.refs_1_, bf16[32,3072]{1,0:T(8,128)(2,1)S(1)} %collective-permute-done.19.refs_2_, f32[64,3072]{1,0:T(8,128)S(1)} %get-tuple-element.54.refs_4_.refs_2_.refs_3_, ...), custom_call_target="tpu_custom_call" | custom-call | tf_op jit(solution)/shard_map/finish/pallas_call | solution.py:37
  (44 shorter events, 8.9 us)
Async XLA Ops:
  0.0 2.2 %collective-permute-start = (bf16[256,1024]{1,0:T(8,128)(2,1)}, bf16[256,1024]{1,0:T(8,128)(2,1)S(1)}, u32[]{:S(2)}, u32[]{:S(2)}) collective-permute-start(bf16[256,1024]{1,0:T(8,128)(2,1)} %refs_0_.1), channel_id=1, source_target_pairs={{0,1},{1,0},{2,3},{3,2},{4,5},{5,4},{6,7},{7,6},{8,9},{9,8},{10,11... | collective-permute-start | bytes 1572872 | tf_op jit(solution)/shard_map/ppermute | solution.py:289
  3.3 11.9 %collective-permute-start.3 = (bf16[96,2048]{1,0:T(8,128)(2,1)S(1)}, bf16[96,2048]{1,0:T(8,128)(2,1)S(1)}, u32[]{:S(2)}, u32[]{:S(2)}) collective-permute-start(bf16[96,2048]{1,0:T(8,128)(2,1)S(1)} %get-tuple-element.37), channel_id=1, source_target_pairs={{0,0},{1,3},{2,8},{3,11},{4,16},{5,19},{6,24},{7,27},{8,2},{9,1},{... | collective-permute-start | bytes 1179656 | tf_op jit(solution)/shard_map/ppermute | solution.py:101
  4.0 16.7 %collective-permute-start.4 = (bf16[96,2048]{1,0:T(8,128)(2,1)S(1)}, bf16[96,2048]{1,0:T(8,128)(2,1)S(1)}, u32[]{:S(2)}, u32[]{:S(2)}) collective-permute-start(bf16[96,2048]{1,0:T(8,128)(2,1)S(1)} %get-tuple-element.37), channel_id=1, source_target_pairs={{0,4},{1,7},{2,12},{3,15},{4,20},{5,23},{6,28},{7,31},{8,6},{9,5},... | collective-permute-start | bytes 1179656 | tf_op jit(solution)/shard_map/ppermute | solution.py:101
  20.7 16.3 %collective-permute-start.5 = (bf16[96,2048]{1,0:T(8,128)(2,1)S(1)}, bf16[96,2048]{1,0:T(8,128)(2,1)S(1)}, u32[]{:S(2)}, u32[]{:S(2)}) collective-permute-start(bf16[96,2048]{1,0:T(8,128)(2,1)S(1)} %get-tuple-element.38.refs_0_), channel_id=1, source_target_pairs={{0,1},{1,0},{2,3},{3,2},{4,5},{5,4},{6,7},{7,6},{8,9},{9,8},{10,11... | collective-permute-start | bytes 1179656 | tf_op jit(solution)/shard_map/ppermute | solution.py:300
  21.3 15.7 %collective-permute-start.6 = (bf16[96,2048]{1,0:T(8,128)(2,1)S(1)}, bf16[96,2048]{1,0:T(8,128)(2,1)S(1)}, u32[]{:S(2)}, u32[]{:S(2)}) collective-permute-start(bf16[96,2048]{1,0:T(8,128)(2,1)S(1)} %get-tuple-element.39.refs_1_.refs_5_), channel_id=1, source_target_pairs={{0,1},{1,0},{2,3},{3,2},{4,5},{5,4},{6,7},{7,6},{8,9},{9,8},{10,11... | collective-permute-start | bytes 1179656 | tf_op jit(solution)/shard_map/ppermute | solution.py:300
  21.4 20.9 %collective-permute-start.1 = (bf16[160,2048]{1,0:T(8,128)(2,1)S(1)}, bf16[160,2048]{1,0:T(8,128)(2,1)S(1)}, u32[]{:S(2)}, u32[]{:S(2)}) collective-permute-start(bf16[160,2048]{1,0:T(8,128)(2,1)S(1)} %get-tuple-element.36.refs_1_), channel_id=1, source_target_pairs={{0,0},{1,3},{2,8},{3,11},{4,16},{5,19},{6,24},{7,27},{8,2},{9,1},{... | collective-permute-start | bytes 1966088 | tf_op jit(solution)/shard_map/ppermute | solution.py:101
  22.1 33.2 %collective-permute-start.2 = (bf16[160,2048]{1,0:T(8,128)(2,1)S(1)}, bf16[160,2048]{1,0:T(8,128)(2,1)S(1)}, u32[]{:S(2)}, u32[]{:S(2)}) collective-permute-start(bf16[160,2048]{1,0:T(8,128)(2,1)S(1)} %get-tuple-element.36.refs_1_), channel_id=1, source_target_pairs={{0,4},{1,7},{2,12},{3,15},{4,20},{5,23},{6,28},{7,31},{8,6},{9,5},... | collective-permute-start | bytes 1966088 | tf_op jit(solution)/shard_map/ppermute | solution.py:101
  42.2 24.9 %collective-permute-start.10 = (bf16[96,3072]{1,0:T(8,128)(2,1)S(1)}, bf16[96,3072]{1,0:T(8,128)(2,1)S(1)}, u32[]{:S(2)}, u32[]{:S(2)}) collective-permute-start(bf16[96,3072]{1,0:T(8,128)(2,1)S(1)} %get-tuple-element.45), channel_id=1, source_target_pairs={{16,0},{24,8},{0,16},{8,24},{17,1},{25,9},{1,17},{9,25},{18,2},{26... | collective-permute-start | bytes 1769480 | tf_op jit(solution)/shard_map/ppermute | solution.py:64
  42.3 24.8 %collective-permute-start.9 = (bf16[96,3072]{1,0:T(8,128)(2,1)S(1)}, bf16[96,3072]{1,0:T(8,128)(2,1)S(1)}, u32[]{:S(2)}, u32[]{:S(2)}) collective-permute-start(bf16[96,3072]{1,0:T(8,128)(2,1)S(1)} %get-tuple-element.44), channel_id=1, source_target_pairs={{8,0},{0,8},{24,16},{16,24},{9,1},{1,9},{25,17},{17,25},{10,2},{2,... | collective-permute-start | bytes 1769480 | tf_op jit(solution)/shard_map/ppermute | solution.py:64
  55.4 14.5 %collective-permute-start.13 = (bf16[96,2048]{1,0:T(8,128)(2,1)S(1)}, bf16[96,2048]{1,0:T(8,128)(2,1)S(1)}, u32[]{:S(2)}, u32[]{:S(2)}) collective-permute-start(bf16[96,2048]{1,0:T(8,128)(2,1)S(1)} %get-tuple-element.48.refs_0_), channel_id=1, source_target_pairs={{0,1},{1,0},{2,3},{3,2},{4,5},{5,4},{6,7},{7,6},{8,9},{9,8},{10,11... | collective-permute-start | bytes 1179656 | tf_op jit(solution)/shard_map/ppermute | solution.py:300
  55.5 15.0 %collective-permute-start.14 = (bf16[96,2048]{1,0:T(8,128)(2,1)S(1)}, bf16[96,2048]{1,0:T(8,128)(2,1)S(1)}, u32[]{:S(2)}, u32[]{:S(2)}) collective-permute-start(bf16[96,2048]{1,0:T(8,128)(2,1)S(1)} %get-tuple-element.49.refs_1_), channel_id=1, source_target_pairs={{0,1},{1,0},{2,3},{3,2},{4,5},{5,4},{6,7},{7,6},{8,9},{9,8},{10,11... | collective-permute-start | bytes 1179656 | tf_op jit(solution)/shard_map/ppermute | solution.py:300
  67.2 10.3 %collective-permute-start.11 = (bf16[48,3072]{1,0:T(8,128)(2,1)S(1)}, bf16[48,3072]{1,0:T(8,128)(2,1)S(1)}, u32[]{:S(2)}, u32[]{:S(2)}) collective-permute-start(bf16[48,3072]{1,0:T(8,128)(2,1)S(1)} %get-tuple-element.46), channel_id=1, source_target_pairs={{16,0},{24,8},{0,16},{8,24},{17,1},{25,9},{1,17},{9,25},{18,2},{26... | collective-permute-start | bytes 884744 | tf_op jit(solution)/shard_map/ppermute | solution.py:64
  69.8 7.9 %collective-permute-start.12 = (bf16[48,3072]{1,0:T(8,128)(2,1)S(1)}, bf16[48,3072]{1,0:T(8,128)(2,1)S(1)}, u32[]{:S(2)}, u32[]{:S(2)}) collective-permute-start(bf16[48,3072]{1,0:T(8,128)(2,1)S(1)} %get-tuple-element.47.refs_5_), channel_id=1, source_target_pairs={{8,0},{0,8},{24,16},{16,24},{9,1},{1,9},{25,17},{17,25},{10,2},{2,... | collective-permute-start | bytes 884744 | tf_op jit(solution)/shard_map/ppermute | solution.py:64
  70.0 9.2 %collective-permute-start.8 = (bf16[64,2048]{1,0:T(8,128)(2,1)S(1)}, bf16[64,2048]{1,0:T(8,128)(2,1)S(1)}, u32[]{:S(2)}, u32[]{:S(2)}) collective-permute-start(bf16[64,2048]{1,0:T(8,128)(2,1)S(1)} %get-tuple-element.42.refs_4_.refs_1_), channel_id=1, source_target_pairs={{0,1},{1,0},{2,3},{3,2},{4,5},{5,4},{6,7},{7,6},{8,9},{9,8},{10,11... | collective-permute-start | bytes 786440 | tf_op jit(solution)/shard_map/ppermute | solution.py:300
  70.0 9.2 %collective-permute-start.7 = (bf16[64,2048]{1,0:T(8,128)(2,1)S(1)}, bf16[64,2048]{1,0:T(8,128)(2,1)S(1)}, u32[]{:S(2)}, u32[]{:S(2)}) collective-permute-start(bf16[64,2048]{1,0:T(8,128)(2,1)S(1)} %get-tuple-element.41.refs_0_), channel_id=1, source_target_pairs={{0,1},{1,0},{2,3},{3,2},{4,5},{5,4},{6,7},{7,6},{8,9},{9,8},{10,11... | collective-permute-start | bytes 786440 | tf_op jit(solution)/shard_map/ppermute | solution.py:300
  75.6 16.2 %collective-permute-start.17 = (bf16[96,3072]{1,0:T(8,128)(2,1)S(1)}, bf16[96,3072]{1,0:T(8,128)(2,1)S(1)}, u32[]{:S(2)}, u32[]{:S(2)}) collective-permute-start(bf16[96,3072]{1,0:T(8,128)(2,1)S(1)} %get-tuple-element.57), channel_id=1, source_target_pairs={{8,0},{0,8},{24,16},{16,24},{9,1},{1,9},{25,17},{17,25},{10,2},{2,... | collective-permute-start | bytes 1769480 | tf_op jit(solution)/shard_map/ppermute | solution.py:64
  77.6 16.2 %collective-permute-start.18 = (bf16[96,3072]{1,0:T(8,128)(2,1)S(1)}, bf16[96,3072]{1,0:T(8,128)(2,1)S(1)}, u32[]{:S(2)}, u32[]{:S(2)}) collective-permute-start(bf16[96,3072]{1,0:T(8,128)(2,1)S(1)} %get-tuple-element.58), channel_id=1, source_target_pairs={{16,0},{24,8},{0,16},{8,24},{17,1},{25,9},{1,17},{9,25},{18,2},{26... | collective-permute-start | bytes 1769480 | tf_op jit(solution)/shard_map/ppermute | solution.py:64
  82.6 17.7 %collective-permute-start.15 = (bf16[64,3072]{1,0:T(8,128)(2,1)S(1)}, bf16[64,3072]{1,0:T(8,128)(2,1)S(1)}, u32[]{:S(2)}, u32[]{:S(2)}) collective-permute-start(bf16[64,3072]{1,0:T(8,128)(2,1)S(1)} %get-tuple-element.53), channel_id=1, source_target_pairs={{8,0},{0,8},{24,16},{16,24},{9,1},{1,9},{25,17},{17,25},{10,2},{2,... | collective-permute-start | bytes 1179656 | tf_op jit(solution)/shard_map/ppermute | solution.py:64
  83.8 18.4 %collective-permute-start.16 = (bf16[64,3072]{1,0:T(8,128)(2,1)S(1)}, bf16[64,3072]{1,0:T(8,128)(2,1)S(1)}, u32[]{:S(2)}, u32[]{:S(2)}) collective-permute-start(bf16[64,3072]{1,0:T(8,128)(2,1)S(1)} %get-tuple-element.55), channel_id=1, source_target_pairs={{16,0},{24,8},{0,16},{8,24},{17,1},{25,9},{1,17},{9,25},{18,2},{26... | collective-permute-start | bytes 1179656 | tf_op jit(solution)/shard_map/ppermute | solution.py:64
  93.9 14.6 %collective-permute-start.21 = (bf16[48,3072]{1,0:T(8,128)(2,1)S(1)}, bf16[48,3072]{1,0:T(8,128)(2,1)S(1)}, u32[]{:S(2)}, u32[]{:S(2)}) collective-permute-start(bf16[48,3072]{1,0:T(8,128)(2,1)S(1)} %get-tuple-element.62), channel_id=1, source_target_pairs={{16,0},{24,8},{0,16},{8,24},{17,1},{25,9},{1,17},{9,25},{18,2},{26... | collective-permute-start | bytes 884744 | tf_op jit(solution)/shard_map/ppermute | solution.py:64
  94.0 14.5 %collective-permute-start.22 = (bf16[48,3072]{1,0:T(8,128)(2,1)S(1)}, bf16[48,3072]{1,0:T(8,128)(2,1)S(1)}, u32[]{:S(2)}, u32[]{:S(2)}) collective-permute-start(bf16[48,3072]{1,0:T(8,128)(2,1)S(1)} %get-tuple-element.59.refs_4_), channel_id=1, source_target_pairs={{8,0},{0,8},{24,16},{16,24},{9,1},{1,9},{25,17},{17,25},{10,2},{2,... | collective-permute-start | bytes 884744 | tf_op jit(solution)/shard_map/ppermute | solution.py:64
  102.3 9.3 %collective-permute-start.19 = (bf16[32,3072]{1,0:T(8,128)(2,1)S(1)}, bf16[32,3072]{1,0:T(8,128)(2,1)S(1)}, u32[]{:S(2)}, u32[]{:S(2)}) collective-permute-start(bf16[32,3072]{1,0:T(8,128)(2,1)S(1)} %get-tuple-element.60), channel_id=1, source_target_pairs={{16,0},{24,8},{0,16},{8,24},{17,1},{25,9},{1,17},{9,25},{18,2},{26... | collective-permute-start | bytes 589832 | tf_op jit(solution)/shard_map/ppermute | solution.py:64
  102.4 9.2 %collective-permute-start.20 = (bf16[32,3072]{1,0:T(8,128)(2,1)S(1)}, bf16[32,3072]{1,0:T(8,128)(2,1)S(1)}, u32[]{:S(2)}, u32[]{:S(2)}) collective-permute-start(bf16[32,3072]{1,0:T(8,128)(2,1)S(1)} %get-tuple-element.61.refs_9_), channel_id=1, source_target_pairs={{8,0},{0,8},{24,16},{16,24},{9,1},{1,9},{25,17},{17,25},{10,2},{2,... | collective-permute-start | bytes 589832 | tf_op jit(solution)/shard_map/ppermute | solution.py:64
  103.6 7.8 %collective-permute-start.23 = (bf16[16,3072]{1,0:T(8,128)(2,1)S(1)}, bf16[16,3072]{1,0:T(8,128)(2,1)S(1)}, u32[]{:S(2)}, u32[]{:S(2)}) collective-permute-start(bf16[16,3072]{1,0:T(8,128)(2,1)S(1)} %get-tuple-element.51.refs_5_), channel_id=1, source_target_pairs={{0,8},{8,16},{16,24},{1,9},{9,17},{17,25},{2,10},{10,18},{18,26},{... | collective-permute-start | bytes 294920 | tf_op jit(solution)/shard_map/ppermute | solution.py:311
  (3 other events, 16.4 us)

commit v4 on v3

--- a/solution.py
+++ b/solution.py
@@ -11,6 +11,7 @@
 RIM = 16
 STEP = 72
 LANES = 128
+LONG = 10 * 10**9
 VMEM = pl.BlockSpec(memory_space=pltpu.VMEM)
 HBM = pl.BlockSpec(memory_space=pl.ANY)
 BF16, F32 = jnp.bfloat16, jnp.float32
@@ -25,9 +26,9 @@
         self.last = None
         self.wait = []
 
-    def call(self, kernel, args, shapes, name, scratch=(), specs=None, after=(), shown=0):
+    def call(self, kernel, args, shapes, name, scratch=(), specs=None, shown=0, last=False):
         specs = [VMEM] * len(args) if specs is None else specs
-        extra = [*([] if self.last is None else [self.last]), *self.wait, *after]
+        extra = [*([] if self.last is None else [self.last]), *self.wait]
         self.wait = []
         count = len(args)
 
@@ -37,8 +38,8 @@
         outs = pl.pallas_call(
             body,
             in_specs=specs + [HBM] * len(extra),
-            out_specs=[VMEM] * len(shapes),
-            out_shape=[pltpu.VMEM(s, t) for s, t in shapes],
+            out_specs=[HBM if last else VMEM] * len(shapes),
+            out_shape=[jax.ShapeDtypeStruct(s, t) if last else pltpu.VMEM(s, t) for s, t in shapes],
             scratch_shapes=list(scratch),
             compiler_params=params(),
             cost_estimate=pl.CostEstimate(flops=shown, bytes_accessed=0, transcendentals=0),
@@ -64,23 +65,35 @@
     return lax.ppermute(block, "row", route)
 
 
-def widen_kernel(own, other, *outs):
+def widen_kernel(own, other, *refs):
+    *outs, sems = refs
     e = own.shape[1]
     core = lax.rem(lax.axis_index("col"), CORES)
-    row = own.shape[0]
-    for o in outs:
-        row -= o.shape[0]
-        for k in range(CORES):
-
-            @pl.when(core == k)
-            def _():
-                o[:, k * e : (k + 1) * e] = own[row : row + o.shape[0]]
+    for k in range(CORES):
+
+        @pl.when(core == k)
+        def _():
+            copies = []
+            row = own.shape[0]
+            for i, o in enumerate(outs):
+                row -= o.shape[0]
+                source = own.at[pl.ds(row, o.shape[0])]
+                copies.append(pltpu.make_async_copy(source, o.at[:, pl.ds(k * e, e)], sems.at[i]))
+            for c in copies:
+                c.start()
+            row = own.shape[0]
+            for o in outs:
+                row -= o.shape[0]
                 o[:, (1 - k) * e : (2 - k) * e] = other[row : row + o.shape[0]]
+            for c in copies:
+                c.wait()
 
 
 def widen(order, own, other, sizes):
     shapes = [((n, CORES * own.shape[1]), BF16) for n in sizes]
-    return order.call(widen_kernel, [own, other], shapes, "widen")
+    own = pltpu.with_memory_space_constraint(own, pltpu.HBM)
+    scratch = [pltpu.SemaphoreType.DMA((len(sizes),))]
+    return order.call(widen_kernel, [own, other], shapes, "widen", scratch, specs=[HBM, VMEM])
 
 
 def gather(piece):
@@ -148,35 +161,39 @@
     return order.call(fetch_kernel, [w], [(w.shape, BF16)], "fetch_w", scratch, specs=[HBM])[0]
 
 
-def project_kernel(tn, shape, *refs):
+def project_kernel(tn, shape, start, *refs):
     count = shape[0] * shape[1] // CORES
     mine, other, w_ref = refs[:count], refs[count : 2 * count], refs[2 * count]
     *outs, halves = refs[2 * count + 1 :]
     stack_halves(shape, mine, other, halves)
-    parts, h, e = halves.shape
+    h, e = halves.shape[1:]
+    rows = sum(o.shape[0] for o in outs)
     cols = w_ref.shape[2]
     for g in range(3):
         for c in range(0, cols, tn):
-            acc = jnp.dot(halves[...].reshape(parts * h, e), w_ref[g, :, c : c + tn], preferred_element_type=F32)
+            x = halves[start : start + rows // h].reshape(rows, e)
+            acc = jnp.dot(x, w_ref[g, :, c : c + tn], preferred_element_type=F32)
             at = 0
             for o in outs:
                 o[:, g * cols + c : g * cols + c + tn] = acc[at : at + o.shape[0]].astype(o.dtype)
                 at += o.shape[0]
 
 
-def project(order, mine, other, w, shape):
+def project(order, mine, other, w, shape, kept):
     ys, xs = shape
     n, e = mine[0].shape
     h = n // 2
     cols = w.shape[2]
-    counts = [ys] * (xs - 1) + [xs] * (ys - 1) + [ys, xs]
-    shapes = [((k * h, 3 * cols), BF16 if i < xs + ys - 2 else F32) for i, k in enumerate(counts)]
+    sent = [ys] * (xs - 1) + [xs] * (ys - 1)
+    shapes = [((k * h, 3 * cols), F32 if kept else BF16) for k in ([ys, xs] if kept else sent)]
     scratch = [pltpu.VMEM((2 * xs * ys, h, e), BF16)]
-    kernel = functools.partial(project_kernel, min(cols, 256), shape)
-    outs = order.call(kernel, [*mine, *other, w], shapes, "project", scratch)
+    kernel = functools.partial(project_kernel, min(cols, 256), shape, sum(sent) if kept else 0)
+    outs = order.call(kernel, [*mine, *other, w], shapes, "keep" if kept else "send", scratch, shown=LONG if kept else 0)
+    if kept:
+        return outs
     got_a = [shift_rows(s, shape, 0, -dx) for dx, s in enumerate(outs[: xs - 1], 1)]
-    got_c = [shift_rows(s, shape, -dy, 0) for dy, s in enumerate(outs[xs - 1 : -2], 1)]
-    return [outs[-2], *got_a], [outs[-1], *got_c]
+    got_c = [shift_rows(s, shape, -dy, 0) for dy, s in enumerate(outs[xs - 1 :], 1)]
+    return got_a, got_c
 
 
 def middle_kernel(count_a, count_c, *refs):
@@ -204,16 +221,26 @@
     return [*first, *last_a], [*second, *last_c]
 
 
-def finish_kernel(top, bottom, n, count_a, count_c, *refs):
+def finish_kernel(top, bottom, n, count_a, count_c, dones, *refs):
     refs = list(refs)
     terms = [refs[:count_a], refs[count_a : count_a + count_c]]
     del refs[: count_a + count_c]
     fin, fmix = refs.pop(0), refs.pop(0)
     follow = refs.pop(0) if not bottom else None
     rim = refs.pop(0) if top else None
+    done = [refs.pop(0) for _ in range(dones)]
     out = refs.pop(0)
     lead = refs.pop(0) if not top else None
     tail = refs.pop(0) if bottom else None
+    copies = []
+    if top:
+        whole, out, sems = out, refs.pop(), refs.pop()
+        row = whole.shape[0]
+        for i, o in enumerate([*done, out]):
+            row -= o.shape[0]
+            copies.append(pltpu.make_async_copy(o, whole.at[pl.ds(row, o.shape[0])], sems.at[i]))
+        for c in copies[:-1]:
+            c.start()
     ext, prod = refs
     h = n // 2
     for i, group in enumerate(terms):
@@ -254,25 +281,31 @@
         return 0
 
     lax.fori_loop(0, cols // LANES, column, 0)
-
-
-def finish(order, top, bottom, n, terms, fin, fmix, follow, rim):
+    for c in copies[-1:]:
+        c.start()
+    for c in copies:
+        c.wait()
+
+
+def finish(order, top, bottom, n, terms, fin, fmix, follow, rim, done):
     width = terms[0][0].shape[1]
     cols = fmix.shape[1]
     rows = n + (RIM if top else 0) - (RIM if bottom else 0)
     args = [*terms[0], *terms[1], fin, fmix]
     args += [follow] if not bottom else []
-    args += [rim] if top else []
-    shapes = [((rows, cols), BF16)]
+    args += [rim, *done] if top else []
+    height = rows + sum(o.shape[0] for o in done)
+    shapes = [((height if top else rows, cols), BF16)]
     shapes += [((RIM, width), F32)] if not top else []
     shapes += [((RIM, width), BF16)] if bottom else []
-    kernel = functools.partial(finish_kernel, top, bottom, n, len(terms[0]), len(terms[1]))
+    kernel = functools.partial(finish_kernel, top, bottom, n, len(terms[0]), len(terms[1]), len(done) if top else 0)
     scratch = [pltpu.VMEM((n + 2 * RIM, width), F32), pltpu.VMEM((STEP + 8, LANES), F32)]
-    return order.call(kernel, args, shapes, "finish", scratch, shown=50 * 10**9 if bottom else 0)
+    scratch += [pltpu.SemaphoreType.DMA((len(done) + 1,)), pltpu.VMEM((rows, cols), BF16)] if top else []
+    return order.call(kernel, args, shapes, "finish", scratch, shown=LONG if bottom else 0, last=top)
 
 
 CHUNKS = ((3,), (3, 2))
-PLAN = ("W", "K0", "C0", "J0", "K1", "C1", "C2", "M0", "J1", "F0", "J2", "M1", "M2", "F1", "F2")
+PLAN = ("W", "K0", "C0", "J0", "B0", "K1", "C1", "C2", "M0", "Y2", "J1", "B1", "F0", "J2", "B2", "M1", "M2", "F1", "F2")
 
 
 def per_device(tokens, w_in, filt_in, filt_mix):
@@ -288,28 +321,33 @@
     last = len(sizes) - 1
     wide = widen(order, tokens, lax.ppermute(tokens, "col", swap), [sum(p) for p in parts])
     blocks = [gather(piece) for piece in wide]
-    mine, other, terms, outs = [], {}, {}, {}
+    mine, outs, other, got, terms = [], [], {}, {}, {}
     follow, rim = None, None
     for step in PLAN:
         kind, i = step[0], int(step[1:] or 0)
         if kind == "W":
             w = fetch(order, w_in)
+        elif kind == "Y":
+            order.wait += other[i]
         elif kind == "K":
             mine += cut(order, blocks[i], parts[i])
         elif kind == "C":
             other[i] = [lax.ppermute(b, "col", swap) for b in mine[i]]
         elif kind == "J":
-            terms[i] = project(order, mine[i], other[i], w, shape)
+            got[i] = project(order, mine[i], other[i], w, shape, False)
+        elif kind == "B":
+            keep = project(order, mine[i], other[i], w, shape, True)
+            terms[i] = [[k, *g] for k, g in zip(keep, got[i])]
         elif kind == "M":
             terms[i] = middle(order, terms[i], sizes[i] // 2, shape)
         else:
-            got = finish(order, i == last, i == 0, sizes[i], terms[i], fin, filt_mix, follow, rim)
-            outs[i] = got.pop(0)
+            made = finish(order, i == last, i == 0, sizes[i], terms[i], fin, filt_mix, follow, rim, outs)
+            outs.append(made.pop(0))
             if i < last:
-                follow = got.pop(0)
+                follow = made.pop(0)
             if i == 0:
-                rim = lax.ppermute(got.pop(0), "row", [(r, r + 1) for r in range(count - 1)])
-    return jnp.concatenate([outs[i] for i in reversed(range(len(sizes)))], axis=0)
+                rim = lax.ppermute(made.pop(0), "row", [(r, r + 1) for r in range(count - 1)])
+    return outs[-1]
 
 
 def solution(mesh):

time: 114 us -> 114 us (level)
  starting transfers between devices: 37.5 us -> 34 us
  Pallas kernels: 23.5 us -> 26.3 us
  waiting for transfers between devices: 50.7 us -> 52.7 us
    ppermute x12, starting transfers between devices: 9.73 us -> 5.34 us  [shift_rows(): return lax.ppermute(block, 'row', route)]
    ppermute x12, waiting for transfers between devices: 29.3 us -> 33.2 us  [shift_rows(): return lax.ppermute(block, 'row', route)]
    pallas_call x13 -> x16, Pallas kernels: 23.5 us -> 26.3 us  [call(): pl.pallas_call(body, in_specs=specs + [HBM] * len(extra), out_specs=[HBM...]
    ppermute x4, waiting for transfers between devices: 18.4 us -> 16.8 us  [gather(): blocks.append(lax.ppermute(piece, ('row', 'col'), route))]
    ppermute x1, starting transfers between devices: 2.73 us -> 3.91 us  [per_device(): lax.ppermute(made.pop(0), 'row', [(r, r + 1) for r in range(count - 1)])]
  transfers between devices with their start and end apart: 24 -> 24, of which waited for: 11 -> 12; matrix products, arithmetic and copies ran while one was open for 0% -> 0% of each run, Pallas kernels for 19% -> 14%
where the time goes in v4:
time: 114 us; the launch traced here: 113 us
  waiting for transfers between devices  52.7 us (46%)
  starting transfers between devices  34 us (30%)
  Pallas kernels  26.3 us (23%)
    ppermute x12, waiting for transfers between devices, shift_rows(): return lax.ppermute(block, 'row', route)  33.2 us
    pallas_call x16, Pallas kernels, call(): pl.pallas_call(body, in_specs=specs + [HBM] * len(extra), out_specs=[HBM...  26.3 us
    ppermute x4, starting transfers between devices, gather(): blocks.append(lax.ppermute(piece, ('row', 'col'), route))  22.8 us
    ppermute x4, waiting for transfers between devices, gather(): blocks.append(lax.ppermute(piece, ('row', 'col'), route))  16.8 us
    ppermute x12, starting transfers between devices, shift_rows(): return lax.ppermute(block, 'row', route)  5.34 us
    ppermute x1, starting transfers between devices, per_device(): lax.ppermute(made.pop(0), 'row', [(r, r + 1) for r in range(count - 1)])  3.91 us
  transfers between devices with their start and end apart: 24, of which 12 were waited for; matrix products, arithmetic and copies ran while one was open for 0% of the time, Pallas kernels for 14%

profile of v4, /device:TPU:0, one launch (start us, length us, event | category | flops | bytes accessed | tf_op | source)
XLA Modules:
  0.0 113.4 jit_solution(7681686314687688287)
XLA Ops:
  0.5 1.7 %collective-permute-done.refs_1_ = bf16[256,1024]{1,0:T(8,128)(2,1)S(1)} collective-permute-done((bf16[256,1024]{1,0:T(8,128)(2,1)}, bf16[256,1024]{1,0:T(8,128)(2,1)S(1)}, u32[]{:S(2)}, u32[]{:S(2)}) %collective-permute-start) | collective-permute-done | bytes 524320 | tf_op jit(solution)/shard_map/ppermute | solution.py:322
  4.0 6.5 %collective-permute-start.4 = (bf16[96,2048]{1,0:T(8,128)(2,1)S(1)}, bf16[96,2048]{1,0:T(8,128)(2,1)S(1)}, u32[]{:S(2)}, u32[]{:S(2)}) collective-permute-start(bf16[96,2048]{1,0:T(8,128)(2,1)S(1)} %get-tuple-element.37), channel_id=1, source_target_pairs={{0,4},{1,7},{2,12},{3,15},{4,20},{5,23},{6,28},{7,31},{8,6},{9,5},... | collective-permute-start | bytes 1179656 | tf_op jit(solution)/shard_map/ppermute | solution.py:114
  10.5 4.7 %fetch_w.1.refs_2_.refs_4_ = bf16[3,2048,1024]{2,1,0:T(8,128)(2,1)S(1)} custom-call(bf16[3,2048,1024]{2,1,0:T(8,128)(2,1)} %bitcast.5, bf16[160,2048]{1,0:T(8,128)(2,1)S(1)} %get-tuple-element.36.refs_1_), custom_call_target="tpu_custom_call" | custom-call | tf_op jit(solution)/shard_map/fetch_w/pallas_call | solution.py:38
  15.2 5.4 %collective-permute-done.4.refs_1_ = bf16[96,2048]{1,0:T(8,128)(2,1)S(1)} collective-permute-done((bf16[96,2048]{1,0:T(8,128)(2,1)S(1)}, bf16[96,2048]{1,0:T(8,128)(2,1)S(1)}, u32[]{:S(2)}, u32[]{:S(2)}) %collective-permute-start.4) | collective-permute-done | bytes 393248 | tf_op jit(solution)/shard_map/ppermute | solution.py:114
  22.1 14.9 %collective-permute-start.2 = (bf16[160,2048]{1,0:T(8,128)(2,1)S(1)}, bf16[160,2048]{1,0:T(8,128)(2,1)S(1)}, u32[]{:S(2)}, u32[]{:S(2)}) collective-permute-start(bf16[160,2048]{1,0:T(8,128)(2,1)S(1)} %get-tuple-element.36.refs_1_), channel_id=1, source_target_pairs={{0,4},{1,7},{2,12},{3,15},{4,20},{5,23},{6,28},{7,31},{8,6},{9,5},... | collective-permute-start | bytes 1966088 | tf_op jit(solution)/shard_map/ppermute | solution.py:114
  37.0 2.7 %send.3 = (bf16[96,3072]{1,0:T(8,128)(2,1)S(1)}, bf16[96,3072]{1,0:T(8,128)(2,1)S(1)}) custom-call(bf16[96,2048]{1,0:T(8,128)(2,1)S(1)} %get-tuple-element.38.refs_0_, bf16[96,2048]{1,0:T(8,128)(2,1)S(1)} %get-tuple-element.39.refs_1_.refs_5_, bf16[96,2048]{1,0:T(8,128)(2,1)S(1)} %collective-permute-done.5.refs_2_, ...), custom_call_target="tpu_custom_call" | custom-call | tf_op jit(solution)/shard_map/send/pallas_call | solution.py:38
  39.9 2.7 %keep.3 = (f32[96,3072]{1,0:T(8,128)S(1)}, f32[96,3072]{1,0:T(8,128)S(1)}) custom-call(bf16[96,2048]{1,0:T(8,128)(2,1)S(1)} %get-tuple-element.38.refs_0_, bf16[96,2048]{1,0:T(8,128)(2,1)S(1)} %get-tuple-element.39.refs_1_.refs_5_, bf16[96,2048]{1,0:T(8,128)(2,1)S(1)} %collective-permute-done.5.refs_2_, bf16[96,2048]{1,0:T(8,128)(2,1)S(1)} %collective-permute-done.6.refs_3_, ...), custom_call_target="tpu_custom_call" | custom-call | flops 10000000000 | tf_op jit(solution)/shard_map/keep/pallas_call | solution.py:38
  42.7 11.3 %collective-permute-done.2.refs_1_ = bf16[160,2048]{1,0:T(8,128)(2,1)S(1)} collective-permute-done((bf16[160,2048]{1,0:T(8,128)(2,1)S(1)}, bf16[160,2048]{1,0:T(8,128)(2,1)S(1)}, u32[]{:S(2)}, u32[]{:S(2)}) %collective-permute-start.2) | collective-permute-done | bytes 655392 | tf_op jit(solution)/shard_map/ppermute | solution.py:114
  54.9 4.8 %collective-permute-done.9.refs_1_ = bf16[96,3072]{1,0:T(8,128)(2,1)S(1)} collective-permute-done((bf16[96,3072]{1,0:T(8,128)(2,1)S(1)}, bf16[96,3072]{1,0:T(8,128)(2,1)S(1)}, u32[]{:S(2)}, u32[]{:S(2)}) %collective-permute-start.9) | collective-permute-done | bytes 589856 | tf_op jit(solution)/shard_map/ppermute | solution.py:65
  59.8 7.6 %collective-permute-done.10.refs_3_.refs_4_ = bf16[96,3072]{1,0:T(8,128)(2,1)S(1)} collective-permute-done((bf16[96,3072]{1,0:T(8,128)(2,1)S(1)}, bf16[96,3072]{1,0:T(8,128)(2,1)S(1)}, u32[]{:S(2)}, u32[]{:S(2)}) %collective-permute-start.10) | collective-permute-done | bytes 589856 | tf_op jit(solution)/shard_map/ppermute | solution.py:65
  67.5 2.5 %collective-permute-start.11 = (bf16[48,3072]{1,0:T(8,128)(2,1)S(1)}, bf16[48,3072]{1,0:T(8,128)(2,1)S(1)}, u32[]{:S(2)}, u32[]{:S(2)}) collective-permute-start(bf16[48,3072]{1,0:T(8,128)(2,1)S(1)} %get-tuple-element.46), channel_id=1, source_target_pairs={{16,0},{24,8},{0,16},{8,24},{17,1},{25,9},{1,17},{9,25},{18,2},{26... | collective-permute-start | bytes 884744 | tf_op jit(solution)/shard_map/ppermute | solution.py:65
  70.1 2.7 %send.4 = (bf16[96,3072]{1,0:T(8,128)(2,1)S(1)}, bf16[96,3072]{1,0:T(8,128)(2,1)S(1)}) custom-call(bf16[96,2048]{1,0:T(8,128)(2,1)S(1)} %get-tuple-element.48.refs_0_, bf16[96,2048]{1,0:T(8,128)(2,1)S(1)} %get-tuple-element.49.refs_1_, bf16[96,2048]{1,0:T(8,128)(2,1)S(1)} %collective-permute-done.13.refs_2_, ...), custom_call_target="tpu_custom_call" | custom-call | tf_op jit(solution)/shard_map/send/pallas_call | solution.py:38
  72.8 2.1 %collective-permute-start.17 = (bf16[96,3072]{1,0:T(8,128)(2,1)S(1)}, bf16[96,3072]{1,0:T(8,128)(2,1)S(1)}, u32[]{:S(2)}, u32[]{:S(2)}) collective-permute-start(bf16[96,3072]{1,0:T(8,128)(2,1)S(1)} %get-tuple-element.58), channel_id=1, source_target_pairs={{8,0},{0,8},{24,16},{16,24},{9,1},{1,9},{25,17},{17,25},{10,2},{2,... | collective-permute-start | bytes 1769480 | tf_op jit(solution)/shard_map/ppermute | solution.py:65
  75.0 2.7 %keep.4 = (f32[96,3072]{1,0:T(8,128)S(1)}, f32[96,3072]{1,0:T(8,128)S(1)}) custom-call(bf16[96,2048]{1,0:T(8,128)(2,1)S(1)} %get-tuple-element.48.refs_0_, bf16[96,2048]{1,0:T(8,128)(2,1)S(1)} %get-tuple-element.49.refs_1_, bf16[96,2048]{1,0:T(8,128)(2,1)S(1)} %collective-permute-done.13.refs_2_, bf16[96,2048]{1,0:T(8,128)(2,1)S(1)} %collective-permute-done.14.refs_3_, ...), custom_call_target="tpu_custom_call" | custom-call | flops 10000000000 | tf_op jit(solution)/shard_map/keep/pallas_call | solution.py:38
  77.8 2.2 %collective-permute-done.12.refs_5_ = bf16[48,3072]{1,0:T(8,128)(2,1)S(1)} collective-permute-done((bf16[48,3072]{1,0:T(8,128)(2,1)S(1)}, bf16[48,3072]{1,0:T(8,128)(2,1)S(1)}, u32[]{:S(2)}, u32[]{:S(2)}) %collective-permute-start.12) | collective-permute-done | bytes 294944 | tf_op jit(solution)/shard_map/ppermute | solution.py:65
  80.0 1.7 %finish.3 = (bf16[80,1024]{1,0:T(8,128)(2,1)S(1)}, f32[16,3072]{1,0:T(8,128)S(1)}, bf16[16,3072]{1,0:T(8,128)(2,1)S(1)}) custom-call(f32[96,3072]{1,0:T(8,128)S(1)} %get-tuple-element.44.refs_0_, bf16[96,3072]{1,0:T(8,128)(2,1)S(1)} %collective-permute-done.9.refs_1_, bf16[48,3072]{1,0:T(8,128)(2,1)S(1)} %collective-permute-done.11.refs_2_, ...), custom_call_target="tpu_custom_call" | custom-call | flops 10000000000 | tf_op jit(solution)/shard_map/finish/pallas_call | solution.py:38
  81.6 1.9 %send.5 = (bf16[64,3072]{1,0:T(8,128)(2,1)S(1)}, bf16[64,3072]{1,0:T(8,128)(2,1)S(1)}) custom-call(bf16[64,2048]{1,0:T(8,128)(2,1)S(1)} %get-tuple-element.42.refs_0_, bf16[64,2048]{1,0:T(8,128)(2,1)S(1)} %get-tuple-element.43.refs_4_.refs_1_, bf16[64,2048]{1,0:T(8,128)(2,1)S(1)} %collective-permute-done.7.refs_6_.refs_2_, ...), custom_call_target="tpu_custom_call" | custom-call | tf_op jit(solution)/shard_map/send/pallas_call | solution.py:38
  83.7 1.9 %keep.5 = (f32[64,3072]{1,0:T(8,128)S(1)}, f32[64,3072]{1,0:T(8,128)S(1)}) custom-call(bf16[64,2048]{1,0:T(8,128)(2,1)S(1)} %get-tuple-element.42.refs_0_, bf16[64,2048]{1,0:T(8,128)(2,1)S(1)} %get-tuple-element.43.refs_4_.refs_1_, bf16[64,2048]{1,0:T(8,128)(2,1)S(1)} %collective-permute-done.7.refs_6_.refs_2_, ...), custom_call_target="tpu_custom_call" | custom-call | flops 10000000000 | tf_op jit(solution)/shard_map/keep/pallas_call | solution.py:38
  85.6 7.0 %collective-permute-done.17.refs_1_ = bf16[96,3072]{1,0:T(8,128)(2,1)S(1)} collective-permute-done((bf16[96,3072]{1,0:T(8,128)(2,1)S(1)}, bf16[96,3072]{1,0:T(8,128)(2,1)S(1)}, u32[]{:S(2)}, u32[]{:S(2)}) %collective-permute-start.17) | collective-permute-done | bytes 589856 | tf_op jit(solution)/shard_map/ppermute | solution.py:65
  92.9 8.2 %collective-permute-done.15.refs_1_ = bf16[64,3072]{1,0:T(8,128)(2,1)S(1)} collective-permute-done((bf16[64,3072]{1,0:T(8,128)(2,1)S(1)}, bf16[64,3072]{1,0:T(8,128)(2,1)S(1)}, u32[]{:S(2)}, u32[]{:S(2)}) %collective-permute-start.15) | collective-permute-done | bytes 393248 | tf_op jit(solution)/shard_map/ppermute | solution.py:65
  101.3 3.9 %collective-permute-start.23 = (bf16[16,3072]{1,0:T(8,128)(2,1)S(1)}, bf16[16,3072]{1,0:T(8,128)(2,1)S(1)}, u32[]{:S(2)}, u32[]{:S(2)}) collective-permute-start(bf16[16,3072]{1,0:T(8,128)(2,1)S(1)} %get-tuple-element.52.refs_5_), channel_id=1, source_target_pairs={{0,8},{8,16},{16,24},{1,9},{9,17},{17,25},{2,10},{10,18},{18,26},{... | collective-permute-start | bytes 294920 | tf_op jit(solution)/shard_map/ppermute | solution.py:349
  105.9 1.4 %collective-permute-done.22.refs_5_ = bf16[48,3072]{1,0:T(8,128)(2,1)S(1)} collective-permute-done((bf16[48,3072]{1,0:T(8,128)(2,1)S(1)}, bf16[48,3072]{1,0:T(8,128)(2,1)S(1)}, u32[]{:S(2)}, u32[]{:S(2)}) %collective-permute-start.22) | collective-permute-done | bytes 294944 | tf_op jit(solution)/shard_map/ppermute | solution.py:65
  107.4 1.7 %finish.4 = (bf16[96,1024]{1,0:T(8,128)(2,1)S(1)}, f32[16,3072]{1,0:T(8,128)S(1)}) custom-call(f32[96,3072]{1,0:T(8,128)S(1)} %get-tuple-element.57.refs_0_, bf16[96,3072]{1,0:T(8,128)(2,1)S(1)} %collective-permute-done.17.refs_1_, bf16[48,3072]{1,0:T(8,128)(2,1)S(1)} %collective-permute-done.21.refs_2_, ...), custom_call_target="tpu_custom_call" | custom-call | tf_op jit(solution)/shard_map/finish/pallas_call | solution.py:38
  111.2 2.0 %finish.5 = bf16[256,1024]{1,0:T(8,128)(2,1)} custom-call(f32[64,3072]{1,0:T(8,128)S(1)} %get-tuple-element.54.refs_0_, bf16[64,3072]{1,0:T(8,128)(2,1)S(1)} %collective-permute-done.15.refs_1_, bf16[32,3072]{1,0:T(8,128)(2,1)S(1)} %collective-permute-done.19.refs_2_, f32[64,3072]{1,0:T(8,128)S(1)} %get-tuple-element.56.refs_4_.refs_2_.refs_3_, ...), custom_call_target="tpu_custom_call" | custom-call | tf_op jit(solution)/shard_map/finish/pallas_call | solution.py:38
  (44 shorter events, 8.5 us)
Async XLA Ops:
  0.0 2.2 %collective-permute-start = (bf16[256,1024]{1,0:T(8,128)(2,1)}, bf16[256,1024]{1,0:T(8,128)(2,1)S(1)}, u32[]{:S(2)}, u32[]{:S(2)}) collective-permute-start(bf16[256,1024]{1,0:T(8,128)(2,1)} %refs_0_.1), channel_id=1, source_target_pairs={{0,1},{1,0},{2,3},{3,2},{4,5},{5,4},{6,7},{7,6},{8,9},{9,8},{10,11... | collective-permute-start | bytes 1572872 | tf_op jit(solution)/shard_map/ppermute | solution.py:322
  3.3 11.9 %collective-permute-start.3 = (bf16[96,2048]{1,0:T(8,128)(2,1)S(1)}, bf16[96,2048]{1,0:T(8,128)(2,1)S(1)}, u32[]{:S(2)}, u32[]{:S(2)}) collective-permute-start(bf16[96,2048]{1,0:T(8,128)(2,1)S(1)} %get-tuple-element.37), channel_id=1, source_target_pairs={{0,0},{1,3},{2,8},{3,11},{4,16},{5,19},{6,24},{7,27},{8,2},{9,1},{... | collective-permute-start | bytes 1179656 | tf_op jit(solution)/shard_map/ppermute | solution.py:114
  4.0 16.7 %collective-permute-start.4 = (bf16[96,2048]{1,0:T(8,128)(2,1)S(1)}, bf16[96,2048]{1,0:T(8,128)(2,1)S(1)}, u32[]{:S(2)}, u32[]{:S(2)}) collective-permute-start(bf16[96,2048]{1,0:T(8,128)(2,1)S(1)} %get-tuple-element.37), channel_id=1, source_target_pairs={{0,4},{1,7},{2,12},{3,15},{4,20},{5,23},{6,28},{7,31},{8,6},{9,5},... | collective-permute-start | bytes 1179656 | tf_op jit(solution)/shard_map/ppermute | solution.py:114
  20.7 16.3 %collective-permute-start.5 = (bf16[96,2048]{1,0:T(8,128)(2,1)S(1)}, bf16[96,2048]{1,0:T(8,128)(2,1)S(1)}, u32[]{:S(2)}, u32[]{:S(2)}) collective-permute-start(bf16[96,2048]{1,0:T(8,128)(2,1)S(1)} %get-tuple-element.38.refs_0_), channel_id=1, source_target_pairs={{0,1},{1,0},{2,3},{3,2},{4,5},{5,4},{6,7},{7,6},{8,9},{9,8},{10,11... | collective-permute-start | bytes 1179656 | tf_op jit(solution)/shard_map/ppermute | solution.py:335
  21.3 15.7 %collective-permute-start.6 = (bf16[96,2048]{1,0:T(8,128)(2,1)S(1)}, bf16[96,2048]{1,0:T(8,128)(2,1)S(1)}, u32[]{:S(2)}, u32[]{:S(2)}) collective-permute-start(bf16[96,2048]{1,0:T(8,128)(2,1)S(1)} %get-tuple-element.39.refs_1_.refs_5_), channel_id=1, source_target_pairs={{0,1},{1,0},{2,3},{3,2},{4,5},{5,4},{6,7},{7,6},{8,9},{9,8},{10,11... | collective-permute-start | bytes 1179656 | tf_op jit(solution)/shard_map/ppermute | solution.py:335
  21.4 21.3 %collective-permute-start.1 = (bf16[160,2048]{1,0:T(8,128)(2,1)S(1)}, bf16[160,2048]{1,0:T(8,128)(2,1)S(1)}, u32[]{:S(2)}, u32[]{:S(2)}) collective-permute-start(bf16[160,2048]{1,0:T(8,128)(2,1)S(1)} %get-tuple-element.36.refs_1_), channel_id=1, source_target_pairs={{0,0},{1,3},{2,8},{3,11},{4,16},{5,19},{6,24},{7,27},{8,2},{9,1},{... | collective-permute-start | bytes 1966088 | tf_op jit(solution)/shard_map/ppermute | solution.py:114
  22.1 31.9 %collective-permute-start.2 = (bf16[160,2048]{1,0:T(8,128)(2,1)S(1)}, bf16[160,2048]{1,0:T(8,128)(2,1)S(1)}, u32[]{:S(2)}, u32[]{:S(2)}) collective-permute-start(bf16[160,2048]{1,0:T(8,128)(2,1)S(1)} %get-tuple-element.36.refs_1_), channel_id=1, source_target_pairs={{0,4},{1,7},{2,12},{3,15},{4,20},{5,23},{6,28},{7,31},{8,6},{9,5},... | collective-permute-start | bytes 1966088 | tf_op jit(solution)/shard_map/ppermute | solution.py:114
  39.8 19.9 %collective-permute-start.9 = (bf16[96,3072]{1,0:T(8,128)(2,1)S(1)}, bf16[96,3072]{1,0:T(8,128)(2,1)S(1)}, u32[]{:S(2)}, u32[]{:S(2)}) collective-permute-start(bf16[96,3072]{1,0:T(8,128)(2,1)S(1)} %get-tuple-element.45), channel_id=1, source_target_pairs={{8,0},{0,8},{24,16},{16,24},{9,1},{1,9},{25,17},{17,25},{10,2},{2,... | collective-permute-start | bytes 1769480 | tf_op jit(solution)/shard_map/ppermute | solution.py:65
  39.9 27.5 %collective-permute-start.10 = (bf16[96,3072]{1,0:T(8,128)(2,1)S(1)}, bf16[96,3072]{1,0:T(8,128)(2,1)S(1)}, u32[]{:S(2)}, u32[]{:S(2)}) collective-permute-start(bf16[96,3072]{1,0:T(8,128)(2,1)S(1)} %get-tuple-element.40.refs_5_), channel_id=1, source_target_pairs={{16,0},{24,8},{0,16},{8,24},{17,1},{25,9},{1,17},{9,25},{18,2},{26... | collective-permute-start | bytes 1769480 | tf_op jit(solution)/shard_map/ppermute | solution.py:65
  54.1 15.9 %collective-permute-start.13 = (bf16[96,2048]{1,0:T(8,128)(2,1)S(1)}, bf16[96,2048]{1,0:T(8,128)(2,1)S(1)}, u32[]{:S(2)}, u32[]{:S(2)}) collective-permute-start(bf16[96,2048]{1,0:T(8,128)(2,1)S(1)} %get-tuple-element.48.refs_0_), channel_id=1, source_target_pairs={{0,1},{1,0},{2,3},{3,2},{4,5},{5,4},{6,7},{7,6},{8,9},{9,8},{10,11... | collective-permute-start | bytes 1179656 | tf_op jit(solution)/shard_map/ppermute | solution.py:335
  54.3 15.7 %collective-permute-start.14 = (bf16[96,2048]{1,0:T(8,128)(2,1)S(1)}, bf16[96,2048]{1,0:T(8,128)(2,1)S(1)}, u32[]{:S(2)}, u32[]{:S(2)}) collective-permute-start(bf16[96,2048]{1,0:T(8,128)(2,1)S(1)} %get-tuple-element.49.refs_1_), channel_id=1, source_target_pairs={{0,1},{1,0},{2,3},{3,2},{4,5},{5,4},{6,7},{7,6},{8,9},{9,8},{10,11... | collective-permute-start | bytes 1179656 | tf_op jit(solution)/shard_map/ppermute | solution.py:335
  54.7 15.3 %collective-permute-start.7 = (bf16[64,2048]{1,0:T(8,128)(2,1)S(1)}, bf16[64,2048]{1,0:T(8,128)(2,1)S(1)}, u32[]{:S(2)}, u32[]{:S(2)}) collective-permute-start(bf16[64,2048]{1,0:T(8,128)(2,1)S(1)} %get-tuple-element.42.refs_0_), channel_id=1, source_target_pairs={{0,1},{1,0},{2,3},{3,2},{4,5},{5,4},{6,7},{7,6},{8,9},{9,8},{10,11... | collective-permute-start | bytes 786440 | tf_op jit(solution)/shard_map/ppermute | solution.py:335
  59.7 10.4 %collective-permute-start.8 = (bf16[64,2048]{1,0:T(8,128)(2,1)S(1)}, bf16[64,2048]{1,0:T(8,128)(2,1)S(1)}, u32[]{:S(2)}, u32[]{:S(2)}) collective-permute-start(bf16[64,2048]{1,0:T(8,128)(2,1)S(1)} %get-tuple-element.43.refs_4_.refs_1_), channel_id=1, source_target_pairs={{0,1},{1,0},{2,3},{3,2},{4,5},{5,4},{6,7},{7,6},{8,9},{9,8},{10,11... | collective-permute-start | bytes 786440 | tf_op jit(solution)/shard_map/ppermute | solution.py:335
  67.5 10.3 %collective-permute-start.11 = (bf16[48,3072]{1,0:T(8,128)(2,1)S(1)}, bf16[48,3072]{1,0:T(8,128)(2,1)S(1)}, u32[]{:S(2)}, u32[]{:S(2)}) collective-permute-start(bf16[48,3072]{1,0:T(8,128)(2,1)S(1)} %get-tuple-element.46), channel_id=1, source_target_pairs={{16,0},{24,8},{0,16},{8,24},{17,1},{25,9},{1,17},{9,25},{18,2},{26... | collective-permute-start | bytes 884744 | tf_op jit(solution)/shard_map/ppermute | solution.py:65
  70.0 9.9 %collective-permute-start.12 = (bf16[48,3072]{1,0:T(8,128)(2,1)S(1)}, bf16[48,3072]{1,0:T(8,128)(2,1)S(1)}, u32[]{:S(2)}, u32[]{:S(2)}) collective-permute-start(bf16[48,3072]{1,0:T(8,128)(2,1)S(1)} %get-tuple-element.47.refs_5_), channel_id=1, source_target_pairs={{8,0},{0,8},{24,16},{16,24},{9,1},{1,9},{25,17},{17,25},{10,2},{2,... | collective-permute-start | bytes 884744 | tf_op jit(solution)/shard_map/ppermute | solution.py:65
  72.8 19.8 %collective-permute-start.17 = (bf16[96,3072]{1,0:T(8,128)(2,1)S(1)}, bf16[96,3072]{1,0:T(8,128)(2,1)S(1)}, u32[]{:S(2)}, u32[]{:S(2)}) collective-permute-start(bf16[96,3072]{1,0:T(8,128)(2,1)S(1)} %get-tuple-element.58), channel_id=1, source_target_pairs={{8,0},{0,8},{24,16},{16,24},{9,1},{1,9},{25,17},{17,25},{10,2},{2,... | collective-permute-start | bytes 1769480 | tf_op jit(solution)/shard_map/ppermute | solution.py:65
  74.9 17.7 %collective-permute-start.18 = (bf16[96,3072]{1,0:T(8,128)(2,1)S(1)}, bf16[96,3072]{1,0:T(8,128)(2,1)S(1)}, u32[]{:S(2)}, u32[]{:S(2)}) collective-permute-start(bf16[96,3072]{1,0:T(8,128)(2,1)S(1)} %get-tuple-element.50.refs_5_), channel_id=1, source_target_pairs={{16,0},{24,8},{0,16},{8,24},{17,1},{25,9},{1,17},{9,25},{18,2},{26... | collective-permute-start | bytes 1769480 | tf_op jit(solution)/shard_map/ppermute | solution.py:65
  83.5 17.5 %collective-permute-start.15 = (bf16[64,3072]{1,0:T(8,128)(2,1)S(1)}, bf16[64,3072]{1,0:T(8,128)(2,1)S(1)}, u32[]{:S(2)}, u32[]{:S(2)}) collective-permute-start(bf16[64,3072]{1,0:T(8,128)(2,1)S(1)} %get-tuple-element.55), channel_id=1, source_target_pairs={{8,0},{0,8},{24,16},{16,24},{9,1},{1,9},{25,17},{17,25},{10,2},{2,... | collective-permute-start | bytes 1179656 | tf_op jit(solution)/shard_map/ppermute | solution.py:65
  83.6 17.4 %collective-permute-start.16 = (bf16[64,3072]{1,0:T(8,128)(2,1)S(1)}, bf16[64,3072]{1,0:T(8,128)(2,1)S(1)}, u32[]{:S(2)}, u32[]{:S(2)}) collective-permute-start(bf16[64,3072]{1,0:T(8,128)(2,1)S(1)} %get-tuple-element.53.refs_5_), channel_id=1, source_target_pairs={{16,0},{24,8},{0,16},{8,24},{17,1},{25,9},{1,17},{9,25},{18,2},{26... | collective-permute-start | bytes 1179656 | tf_op jit(solution)/shard_map/ppermute | solution.py:65
  92.7 13.2 %collective-permute-start.21 = (bf16[48,3072]{1,0:T(8,128)(2,1)S(1)}, bf16[48,3072]{1,0:T(8,128)(2,1)S(1)}, u32[]{:S(2)}, u32[]{:S(2)}) collective-permute-start(bf16[48,3072]{1,0:T(8,128)(2,1)S(1)} %get-tuple-element.62), channel_id=1, source_target_pairs={{16,0},{24,8},{0,16},{8,24},{17,1},{25,9},{1,17},{9,25},{18,2},{26... | collective-permute-start | bytes 884744 | tf_op jit(solution)/shard_map/ppermute | solution.py:65
  92.8 14.5 %collective-permute-start.22 = (bf16[48,3072]{1,0:T(8,128)(2,1)S(1)}, bf16[48,3072]{1,0:T(8,128)(2,1)S(1)}, u32[]{:S(2)}, u32[]{:S(2)}) collective-permute-start(bf16[48,3072]{1,0:T(8,128)(2,1)S(1)} %get-tuple-element.59.refs_4_), channel_id=1, source_target_pairs={{8,0},{0,8},{24,16},{16,24},{9,1},{1,9},{25,17},{17,25},{10,2},{2,... | collective-permute-start | bytes 884744 | tf_op jit(solution)/shard_map/ppermute | solution.py:65
  101.1 9.0 %collective-permute-start.19 = (bf16[32,3072]{1,0:T(8,128)(2,1)S(1)}, bf16[32,3072]{1,0:T(8,128)(2,1)S(1)}, u32[]{:S(2)}, u32[]{:S(2)}) collective-permute-start(bf16[32,3072]{1,0:T(8,128)(2,1)S(1)} %get-tuple-element.60), channel_id=1, source_target_pairs={{16,0},{24,8},{0,16},{8,24},{17,1},{25,9},{1,17},{9,25},{18,2},{26... | collective-permute-start | bytes 589832 | tf_op jit(solution)/shard_map/ppermute | solution.py:65
  101.2 10.0 %collective-permute-start.20 = (bf16[32,3072]{1,0:T(8,128)(2,1)S(1)}, bf16[32,3072]{1,0:T(8,128)(2,1)S(1)}, u32[]{:S(2)}, u32[]{:S(2)}) collective-permute-start(bf16[32,3072]{1,0:T(8,128)(2,1)S(1)} %get-tuple-element.61.refs_9_), channel_id=1, source_target_pairs={{8,0},{0,8},{24,16},{16,24},{9,1},{1,9},{25,17},{17,25},{10,2},{2,... | collective-permute-start | bytes 589832 | tf_op jit(solution)/shard_map/ppermute | solution.py:65
  101.3 8.8 %collective-permute-start.23 = (bf16[16,3072]{1,0:T(8,128)(2,1)S(1)}, bf16[16,3072]{1,0:T(8,128)(2,1)S(1)}, u32[]{:S(2)}, u32[]{:S(2)}) collective-permute-start(bf16[16,3072]{1,0:T(8,128)(2,1)S(1)} %get-tuple-element.52.refs_5_), channel_id=1, source_target_pairs={{0,8},{8,16},{16,24},{1,9},{9,17},{17,25},{2,10},{10,18},{18,26},{... | collective-permute-start | bytes 294920 | tf_op jit(solution)/shard_map/ppermute | solution.py:349
  (2 other events, 10.1 us)

commit v5 on v4

--- a/solution.py
+++ b/solution.py
@@ -110,7 +110,7 @@
         for row in range(count):
             for plane in range(planes):
                 for core in range(CORES):
-                    route.append((place(row, plane, core), place(plane, row ^ (a * CORES + core), core)))
+                    route.append((place(row, plane, core), place(plane, row ^ (core * (count // CORES) + a), core)))
         blocks.append(lax.ppermute(piece, ("row", "col"), route))
     return blocks
 
@@ -139,7 +139,7 @@
     core = lax.rem(lax.axis_index("col"), CORES)
     sent = (xs - 1) * ys + (ys - 1) * xs
     for a in range(len(mine)):
-        for blocks, j in ((mine, a * CORES + core), (other, a * CORES + 1 - core)):
+        for blocks, j in ((mine, core * len(mine) + a), (other, (1 - core) * len(mine) + a)):
             row = lax.bitwise_xor(plane, j)
             dy = lax.rem(row // xs - me // xs + ys, ys)
             dx = lax.rem(lax.rem(row, xs) - lax.rem(me, xs) + xs, xs)

time: 114 us -> 112 us (0.982)
  waiting for transfers between devices: 52.7 us -> 34.9 us
  starting transfers between devices: 34 us -> 49.8 us
    ppermute x12, starting transfers between devices: 5.34 us -> 20.4 us  [shift_rows(): return lax.ppermute(block, 'row', route)]
    ppermute x4, waiting for transfers between devices: 16.8 us -> 4.85 us  [gather(): blocks.append(lax.ppermute(piece, ('row', 'col'), route))]
    ppermute x6, starting transfers between devices: 1.5 us -> 11.2 us  [per_device(): other[i] = [lax.ppermute(b, 'col', swap) for b in mine[i]]]
    ppermute x4, starting transfers between devices: 22.8 us -> 13.9 us  [gather(): blocks.append(lax.ppermute(piece, ('row', 'col'), route))]
    ppermute x12, waiting for transfers between devices: 33.2 us -> 27 us  [shift_rows(): return lax.ppermute(block, 'row', route)]
  transfers between devices with their start and end apart: 24 -> 24, of which waited for: 12 -> 10; matrix products, arithmetic and copies ran while one was open for 0% -> 0% of each run, Pallas kernels for 14% -> 14%
where the time goes in v5:
time: 112 us; the launch traced here: 111 us
  starting transfers between devices  49.8 us (44%)
  waiting for transfers between devices  34.9 us (31%)
  Pallas kernels  26.3 us (23%)
    ppermute x12, waiting for transfers between devices, shift_rows(): return lax.ppermute(block, 'row', route)  27 us
    pallas_call x16, Pallas kernels, call(): pl.pallas_call(body, in_specs=specs + [HBM] * len(extra), out_specs=[HBM...  26.3 us
    ppermute x12, starting transfers between devices, shift_rows(): return lax.ppermute(block, 'row', route)  20.4 us
    ppermute x4, starting transfers between devices, gather(): blocks.append(lax.ppermute(piece, ('row', 'col'), route))  13.9 us
    ppermute x6, starting transfers between devices, per_device(): other[i] = [lax.ppermute(b, 'col', swap) for b in mine[i]]  11.2 us
    ppermute x4, waiting for transfers between devices, gather(): blocks.append(lax.ppermute(piece, ('row', 'col'), route))  4.85 us
    ppermute x1, starting transfers between devices, per_device(): lax.ppermute(made.pop(0), 'row', [(r, r + 1) for r in range(count - 1)])  3.92 us
  transfers between devices with their start and end apart: 24, of which 10 were waited for; matrix products, arithmetic and copies ran while one was open for 0% of the time, Pallas kernels for 14%

profile of v5, /device:TPU:0, one launch (start us, length us, event | category | flops | bytes accessed | tf_op | source)
XLA Modules:
  0.0 111.3 jit_solution(2436230867520217809)
XLA Ops:
  0.5 1.7 %collective-permute-done.refs_1_ = bf16[256,1024]{1,0:T(8,128)(2,1)S(1)} collective-permute-done((bf16[256,1024]{1,0:T(8,128)(2,1)}, bf16[256,1024]{1,0:T(8,128)(2,1)S(1)}, u32[]{:S(2)}, u32[]{:S(2)}) %collective-permute-start) | collective-permute-done | bytes 524320 | tf_op jit(solution)/shard_map/ppermute | solution.py:322
  4.0 5.6 %collective-permute-start.4 = (bf16[96,2048]{1,0:T(8,128)(2,1)S(1)}, bf16[96,2048]{1,0:T(8,128)(2,1)S(1)}, u32[]{:S(2)}, u32[]{:S(2)}) collective-permute-start(bf16[96,2048]{1,0:T(8,128)(2,1)S(1)} %get-tuple-element.37), channel_id=1, source_target_pairs={{0,2},{1,7},{2,10},{3,15},{4,18},{5,23},{6,26},{7,31},{8,0},{9,5},... | collective-permute-start | bytes 1179656 | tf_op jit(solution)/shard_map/ppermute | solution.py:114
  9.6 4.7 %fetch_w.1.refs_2_.refs_4_ = bf16[3,2048,1024]{2,1,0:T(8,128)(2,1)S(1)} custom-call(bf16[3,2048,1024]{2,1,0:T(8,128)(2,1)} %bitcast.5, bf16[160,2048]{1,0:T(8,128)(2,1)S(1)} %get-tuple-element.36.refs_1_), custom_call_target="tpu_custom_call" | custom-call | tf_op jit(solution)/shard_map/fetch_w/pallas_call | solution.py:38
  14.3 4.8 %collective-permute-done.4.refs_1_ = bf16[96,2048]{1,0:T(8,128)(2,1)S(1)} collective-permute-done((bf16[96,2048]{1,0:T(8,128)(2,1)S(1)}, bf16[96,2048]{1,0:T(8,128)(2,1)S(1)}, u32[]{:S(2)}, u32[]{:S(2)}) %collective-permute-start.4) | collective-permute-done | bytes 393248 | tf_op jit(solution)/shard_map/ppermute | solution.py:114
  19.2 3.1 %collective-permute-start.5 = (bf16[96,2048]{1,0:T(8,128)(2,1)S(1)}, bf16[96,2048]{1,0:T(8,128)(2,1)S(1)}, u32[]{:S(2)}, u32[]{:S(2)}) collective-permute-start(bf16[96,2048]{1,0:T(8,128)(2,1)S(1)} %get-tuple-element.38.refs_0_), channel_id=1, source_target_pairs={{0,1},{1,0},{2,3},{3,2},{4,5},{5,4},{6,7},{7,6},{8,9},{9,8},{10,11... | collective-permute-start | bytes 1179656 | tf_op jit(solution)/shard_map/ppermute | solution.py:335
  23.1 6.9 %collective-permute-start.2 = (bf16[160,2048]{1,0:T(8,128)(2,1)S(1)}, bf16[160,2048]{1,0:T(8,128)(2,1)S(1)}, u32[]{:S(2)}, u32[]{:S(2)}) collective-permute-start(bf16[160,2048]{1,0:T(8,128)(2,1)S(1)} %get-tuple-element.36.refs_1_), channel_id=1, source_target_pairs={{0,2},{1,7},{2,10},{3,15},{4,18},{5,23},{6,26},{7,31},{8,0},{9,5},... | collective-permute-start | bytes 1966088 | tf_op jit(solution)/shard_map/ppermute | solution.py:114
  30.0 2.8 %send.3 = (bf16[96,3072]{1,0:T(8,128)(2,1)S(1)}, bf16[96,3072]{1,0:T(8,128)(2,1)S(1)}) custom-call(bf16[96,2048]{1,0:T(8,128)(2,1)S(1)} %get-tuple-element.38.refs_0_, bf16[96,2048]{1,0:T(8,128)(2,1)S(1)} %get-tuple-element.39.refs_1_.refs_5_, bf16[96,2048]{1,0:T(8,128)(2,1)S(1)} %collective-permute-done.5.refs_2_, ...), custom_call_target="tpu_custom_call" | custom-call | tf_op jit(solution)/shard_map/send/pallas_call | solution.py:38
  34.3 8.3 %collective-permute-start.10 = (bf16[96,3072]{1,0:T(8,128)(2,1)S(1)}, bf16[96,3072]{1,0:T(8,128)(2,1)S(1)}, u32[]{:S(2)}, u32[]{:S(2)}) collective-permute-start(bf16[96,3072]{1,0:T(8,128)(2,1)S(1)} %get-tuple-element.40.refs_5_), channel_id=1, source_target_pairs={{16,0},{24,8},{0,16},{8,24},{17,1},{25,9},{1,17},{9,25},{18,2},{26... | collective-permute-start | bytes 1769480 | tf_op jit(solution)/shard_map/ppermute | solution.py:65
  42.6 2.7 %keep.3 = (f32[96,3072]{1,0:T(8,128)S(1)}, f32[96,3072]{1,0:T(8,128)S(1)}) custom-call(bf16[96,2048]{1,0:T(8,128)(2,1)S(1)} %get-tuple-element.38.refs_0_, bf16[96,2048]{1,0:T(8,128)(2,1)S(1)} %get-tuple-element.39.refs_1_.refs_5_, bf16[96,2048]{1,0:T(8,128)(2,1)S(1)} %collective-permute-done.5.refs_2_, bf16[96,2048]{1,0:T(8,128)(2,1)S(1)} %collective-permute-done.6.refs_3_, ...), custom_call_target="tpu_custom_call" | custom-call | flops 10000000000 | tf_op jit(solution)/shard_map/keep/pallas_call | solution.py:38
  45.4 7.4 %collective-permute-start.13 = (bf16[96,2048]{1,0:T(8,128)(2,1)S(1)}, bf16[96,2048]{1,0:T(8,128)(2,1)S(1)}, u32[]{:S(2)}, u32[]{:S(2)}) collective-permute-start(bf16[96,2048]{1,0:T(8,128)(2,1)S(1)} %get-tuple-element.48.refs_0_), channel_id=1, source_target_pairs={{0,1},{1,0},{2,3},{3,2},{4,5},{5,4},{6,7},{7,6},{8,9},{9,8},{10,11... | collective-permute-start | bytes 1179656 | tf_op jit(solution)/shard_map/ppermute | solution.py:335
  53.3 3.8 %collective-permute-done.9.refs_1_ = bf16[96,3072]{1,0:T(8,128)(2,1)S(1)} collective-permute-done((bf16[96,3072]{1,0:T(8,128)(2,1)S(1)}, bf16[96,3072]{1,0:T(8,128)(2,1)S(1)}, u32[]{:S(2)}, u32[]{:S(2)}) %collective-permute-start.9) | collective-permute-done | bytes 589856 | tf_op jit(solution)/shard_map/ppermute | solution.py:65
  57.3 7.9 %collective-permute-done.10.refs_3_.refs_4_ = bf16[96,3072]{1,0:T(8,128)(2,1)S(1)} collective-permute-done((bf16[96,3072]{1,0:T(8,128)(2,1)S(1)}, bf16[96,3072]{1,0:T(8,128)(2,1)S(1)}, u32[]{:S(2)}, u32[]{:S(2)}) %collective-permute-start.10) | collective-permute-done | bytes 589856 | tf_op jit(solution)/shard_map/ppermute | solution.py:65
  65.2 2.5 %collective-permute-start.11 = (bf16[48,3072]{1,0:T(8,128)(2,1)S(1)}, bf16[48,3072]{1,0:T(8,128)(2,1)S(1)}, u32[]{:S(2)}, u32[]{:S(2)}) collective-permute-start(bf16[48,3072]{1,0:T(8,128)(2,1)S(1)} %get-tuple-element.46), channel_id=1, source_target_pairs={{16,0},{24,8},{0,16},{8,24},{17,1},{25,9},{1,17},{9,25},{18,2},{26... | collective-permute-start | bytes 884744 | tf_op jit(solution)/shard_map/ppermute | solution.py:65
  68.0 2.7 %send.4 = (bf16[96,3072]{1,0:T(8,128)(2,1)S(1)}, bf16[96,3072]{1,0:T(8,128)(2,1)S(1)}) custom-call(bf16[96,2048]{1,0:T(8,128)(2,1)S(1)} %get-tuple-element.48.refs_0_, bf16[96,2048]{1,0:T(8,128)(2,1)S(1)} %get-tuple-element.49.refs_1_, bf16[96,2048]{1,0:T(8,128)(2,1)S(1)} %collective-permute-done.13.refs_2_, ...), custom_call_target="tpu_custom_call" | custom-call | tf_op jit(solution)/shard_map/send/pallas_call | solution.py:38
  70.7 1.9 %collective-permute-start.17 = (bf16[96,3072]{1,0:T(8,128)(2,1)S(1)}, bf16[96,3072]{1,0:T(8,128)(2,1)S(1)}, u32[]{:S(2)}, u32[]{:S(2)}) collective-permute-start(bf16[96,3072]{1,0:T(8,128)(2,1)S(1)} %get-tuple-element.58), channel_id=1, source_target_pairs={{8,0},{0,8},{24,16},{16,24},{9,1},{1,9},{25,17},{17,25},{10,2},{2,... | collective-permute-start | bytes 1769480 | tf_op jit(solution)/shard_map/ppermute | solution.py:65
  74.1 2.7 %keep.4 = (f32[96,3072]{1,0:T(8,128)S(1)}, f32[96,3072]{1,0:T(8,128)S(1)}) custom-call(bf16[96,2048]{1,0:T(8,128)(2,1)S(1)} %get-tuple-element.48.refs_0_, bf16[96,2048]{1,0:T(8,128)(2,1)S(1)} %get-tuple-element.49.refs_1_, bf16[96,2048]{1,0:T(8,128)(2,1)S(1)} %collective-permute-done.13.refs_2_, bf16[96,2048]{1,0:T(8,128)(2,1)S(1)} %collective-permute-done.14.refs_3_, ...), custom_call_target="tpu_custom_call" | custom-call | flops 10000000000 | tf_op jit(solution)/shard_map/keep/pallas_call | solution.py:38
  77.7 1.7 %finish.3 = (bf16[80,1024]{1,0:T(8,128)(2,1)S(1)}, f32[16,3072]{1,0:T(8,128)S(1)}, bf16[16,3072]{1,0:T(8,128)(2,1)S(1)}) custom-call(f32[96,3072]{1,0:T(8,128)S(1)} %get-tuple-element.44.refs_0_, bf16[96,3072]{1,0:T(8,128)(2,1)S(1)} %collective-permute-done.9.refs_1_, bf16[48,3072]{1,0:T(8,128)(2,1)S(1)} %collective-permute-done.11.refs_2_, ...), custom_call_target="tpu_custom_call" | custom-call | flops 10000000000 | tf_op jit(solution)/shard_map/finish/pallas_call | solution.py:38
  79.3 1.9 %send.5 = (bf16[64,3072]{1,0:T(8,128)(2,1)S(1)}, bf16[64,3072]{1,0:T(8,128)(2,1)S(1)}) custom-call(bf16[64,2048]{1,0:T(8,128)(2,1)S(1)} %get-tuple-element.42.refs_0_, bf16[64,2048]{1,0:T(8,128)(2,1)S(1)} %get-tuple-element.43.refs_4_.refs_1_, bf16[64,2048]{1,0:T(8,128)(2,1)S(1)} %collective-permute-done.7.refs_6_.refs_2_, ...), custom_call_target="tpu_custom_call" | custom-call | tf_op jit(solution)/shard_map/send/pallas_call | solution.py:38
  82.8 1.9 %keep.5 = (f32[64,3072]{1,0:T(8,128)S(1)}, f32[64,3072]{1,0:T(8,128)S(1)}) custom-call(bf16[64,2048]{1,0:T(8,128)(2,1)S(1)} %get-tuple-element.42.refs_0_, bf16[64,2048]{1,0:T(8,128)(2,1)S(1)} %get-tuple-element.43.refs_4_.refs_1_, bf16[64,2048]{1,0:T(8,128)(2,1)S(1)} %collective-permute-done.7.refs_6_.refs_2_, ...), custom_call_target="tpu_custom_call" | custom-call | flops 10000000000 | tf_op jit(solution)/shard_map/keep/pallas_call | solution.py:38
  84.7 5.7 %collective-permute-done.17.refs_1_ = bf16[96,3072]{1,0:T(8,128)(2,1)S(1)} collective-permute-done((bf16[96,3072]{1,0:T(8,128)(2,1)S(1)}, bf16[96,3072]{1,0:T(8,128)(2,1)S(1)}, u32[]{:S(2)}, u32[]{:S(2)}) %collective-permute-start.17) | collective-permute-done | bytes 589856 | tf_op jit(solution)/shard_map/ppermute | solution.py:65
  91.9 6.8 %collective-permute-done.15.refs_1_ = bf16[64,3072]{1,0:T(8,128)(2,1)S(1)} collective-permute-done((bf16[64,3072]{1,0:T(8,128)(2,1)S(1)}, bf16[64,3072]{1,0:T(8,128)(2,1)S(1)}, u32[]{:S(2)}, u32[]{:S(2)}) %collective-permute-start.15) | collective-permute-done | bytes 393248 | tf_op jit(solution)/shard_map/ppermute | solution.py:65
  100.3 3.9 %collective-permute-start.23 = (bf16[16,3072]{1,0:T(8,128)(2,1)S(1)}, bf16[16,3072]{1,0:T(8,128)(2,1)S(1)}, u32[]{:S(2)}, u32[]{:S(2)}) collective-permute-start(bf16[16,3072]{1,0:T(8,128)(2,1)S(1)} %get-tuple-element.52.refs_5_), channel_id=1, source_target_pairs={{0,8},{8,16},{16,24},{1,9},{9,17},{17,25},{2,10},{10,18},{18,26},{... | collective-permute-start | bytes 294920 | tf_op jit(solution)/shard_map/ppermute | solution.py:349
  105.1 1.7 %finish.4 = (bf16[96,1024]{1,0:T(8,128)(2,1)S(1)}, f32[16,3072]{1,0:T(8,128)S(1)}) custom-call(f32[96,3072]{1,0:T(8,128)S(1)} %get-tuple-element.57.refs_0_, bf16[96,3072]{1,0:T(8,128)(2,1)S(1)} %collective-permute-done.17.refs_1_, bf16[48,3072]{1,0:T(8,128)(2,1)S(1)} %collective-permute-done.21.refs_2_, ...), custom_call_target="tpu_custom_call" | custom-call | tf_op jit(solution)/shard_map/finish/pallas_call | solution.py:38
  109.1 2.0 %finish.5 = bf16[256,1024]{1,0:T(8,128)(2,1)} custom-call(f32[64,3072]{1,0:T(8,128)S(1)} %get-tuple-element.54.refs_0_, bf16[64,3072]{1,0:T(8,128)(2,1)S(1)} %collective-permute-done.15.refs_1_, bf16[32,3072]{1,0:T(8,128)(2,1)S(1)} %collective-permute-done.19.refs_2_, f32[64,3072]{1,0:T(8,128)S(1)} %get-tuple-element.56.refs_4_.refs_2_.refs_3_, ...), custom_call_target="tpu_custom_call" | custom-call | tf_op jit(solution)/shard_map/finish/pallas_call | solution.py:38
  (44 shorter events, 15.8 us)
Async XLA Ops:
  0.0 2.2 %collective-permute-start = (bf16[256,1024]{1,0:T(8,128)(2,1)}, bf16[256,1024]{1,0:T(8,128)(2,1)S(1)}, u32[]{:S(2)}, u32[]{:S(2)}) collective-permute-start(bf16[256,1024]{1,0:T(8,128)(2,1)} %refs_0_.1), channel_id=1, source_target_pairs={{0,1},{1,0},{2,3},{3,2},{4,5},{5,4},{6,7},{7,6},{8,9},{9,8},{10,11... | collective-permute-start | bytes 1572872 | tf_op jit(solution)/shard_map/ppermute | solution.py:322
  3.3 11.0 %collective-permute-start.3 = (bf16[96,2048]{1,0:T(8,128)(2,1)S(1)}, bf16[96,2048]{1,0:T(8,128)(2,1)S(1)}, u32[]{:S(2)}, u32[]{:S(2)}) collective-permute-start(bf16[96,2048]{1,0:T(8,128)(2,1)S(1)} %get-tuple-element.37), channel_id=1, source_target_pairs={{0,0},{1,5},{2,8},{3,13},{4,16},{5,21},{6,24},{7,29},{8,2},{9,7},{... | collective-permute-start | bytes 1179656 | tf_op jit(solution)/shard_map/ppermute | solution.py:114
  4.0 15.1 %collective-permute-start.4 = (bf16[96,2048]{1,0:T(8,128)(2,1)S(1)}, bf16[96,2048]{1,0:T(8,128)(2,1)S(1)}, u32[]{:S(2)}, u32[]{:S(2)}) collective-permute-start(bf16[96,2048]{1,0:T(8,128)(2,1)S(1)} %get-tuple-element.37), channel_id=1, source_target_pairs={{0,2},{1,7},{2,10},{3,15},{4,18},{5,23},{6,26},{7,31},{8,0},{9,5},... | collective-permute-start | bytes 1179656 | tf_op jit(solution)/shard_map/ppermute | solution.py:114
  19.2 10.8 %collective-permute-start.5 = (bf16[96,2048]{1,0:T(8,128)(2,1)S(1)}, bf16[96,2048]{1,0:T(8,128)(2,1)S(1)}, u32[]{:S(2)}, u32[]{:S(2)}) collective-permute-start(bf16[96,2048]{1,0:T(8,128)(2,1)S(1)} %get-tuple-element.38.refs_0_), channel_id=1, source_target_pairs={{0,1},{1,0},{2,3},{3,2},{4,5},{5,4},{6,7},{7,6},{8,9},{9,8},{10,11... | collective-permute-start | bytes 1179656 | tf_op jit(solution)/shard_map/ppermute | solution.py:335
  22.3 7.7 %collective-permute-start.6 = (bf16[96,2048]{1,0:T(8,128)(2,1)S(1)}, bf16[96,2048]{1,0:T(8,128)(2,1)S(1)}, u32[]{:S(2)}, u32[]{:S(2)}) collective-permute-start(bf16[96,2048]{1,0:T(8,128)(2,1)S(1)} %get-tuple-element.39.refs_1_.refs_5_), channel_id=1, source_target_pairs={{0,1},{1,0},{2,3},{3,2},{4,5},{5,4},{6,7},{7,6},{8,9},{9,8},{10,11... | collective-permute-start | bytes 1179656 | tf_op jit(solution)/shard_map/ppermute | solution.py:335
  22.4 23.0 %collective-permute-start.1 = (bf16[160,2048]{1,0:T(8,128)(2,1)S(1)}, bf16[160,2048]{1,0:T(8,128)(2,1)S(1)}, u32[]{:S(2)}, u32[]{:S(2)}) collective-permute-start(bf16[160,2048]{1,0:T(8,128)(2,1)S(1)} %get-tuple-element.36.refs_1_), channel_id=1, source_target_pairs={{0,0},{1,5},{2,8},{3,13},{4,16},{5,21},{6,24},{7,29},{8,2},{9,7},{... | collective-permute-start | bytes 1966088 | tf_op jit(solution)/shard_map/ppermute | solution.py:114
  23.1 22.3 %collective-permute-start.2 = (bf16[160,2048]{1,0:T(8,128)(2,1)S(1)}, bf16[160,2048]{1,0:T(8,128)(2,1)S(1)}, u32[]{:S(2)}, u32[]{:S(2)}) collective-permute-start(bf16[160,2048]{1,0:T(8,128)(2,1)S(1)} %get-tuple-element.36.refs_1_), channel_id=1, source_target_pairs={{0,2},{1,7},{2,10},{3,15},{4,18},{5,23},{6,26},{7,31},{8,0},{9,5},... | collective-permute-start | bytes 1966088 | tf_op jit(solution)/shard_map/ppermute | solution.py:114
  32.8 24.4 %collective-permute-start.9 = (bf16[96,3072]{1,0:T(8,128)(2,1)S(1)}, bf16[96,3072]{1,0:T(8,128)(2,1)S(1)}, u32[]{:S(2)}, u32[]{:S(2)}) collective-permute-start(bf16[96,3072]{1,0:T(8,128)(2,1)S(1)} %get-tuple-element.45), channel_id=1, source_target_pairs={{8,0},{0,8},{24,16},{16,24},{9,1},{1,9},{25,17},{17,25},{10,2},{2,... | collective-permute-start | bytes 1769480 | tf_op jit(solution)/shard_map/ppermute | solution.py:65
  34.3 30.8 %collective-permute-start.10 = (bf16[96,3072]{1,0:T(8,128)(2,1)S(1)}, bf16[96,3072]{1,0:T(8,128)(2,1)S(1)}, u32[]{:S(2)}, u32[]{:S(2)}) collective-permute-start(bf16[96,3072]{1,0:T(8,128)(2,1)S(1)} %get-tuple-element.40.refs_5_), channel_id=1, source_target_pairs={{16,0},{24,8},{0,16},{8,24},{17,1},{25,9},{1,17},{9,25},{18,2},{26... | collective-permute-start | bytes 1769480 | tf_op jit(solution)/shard_map/ppermute | solution.py:65
  45.4 22.5 %collective-permute-start.13 = (bf16[96,2048]{1,0:T(8,128)(2,1)S(1)}, bf16[96,2048]{1,0:T(8,128)(2,1)S(1)}, u32[]{:S(2)}, u32[]{:S(2)}) collective-permute-start(bf16[96,2048]{1,0:T(8,128)(2,1)S(1)} %get-tuple-element.48.refs_0_), channel_id=1, source_target_pairs={{0,1},{1,0},{2,3},{3,2},{4,5},{5,4},{6,7},{7,6},{8,9},{9,8},{10,11... | collective-permute-start | bytes 1179656 | tf_op jit(solution)/shard_map/ppermute | solution.py:335
  52.8 15.2 %collective-permute-start.14 = (bf16[96,2048]{1,0:T(8,128)(2,1)S(1)}, bf16[96,2048]{1,0:T(8,128)(2,1)S(1)}, u32[]{:S(2)}, u32[]{:S(2)}) collective-permute-start(bf16[96,2048]{1,0:T(8,128)(2,1)S(1)} %get-tuple-element.49.refs_1_), channel_id=1, source_target_pairs={{0,1},{1,0},{2,3},{3,2},{4,5},{5,4},{6,7},{7,6},{8,9},{9,8},{10,11... | collective-permute-start | bytes 1179656 | tf_op jit(solution)/shard_map/ppermute | solution.py:335
  52.9 14.9 %collective-permute-start.7 = (bf16[64,2048]{1,0:T(8,128)(2,1)S(1)}, bf16[64,2048]{1,0:T(8,128)(2,1)S(1)}, u32[]{:S(2)}, u32[]{:S(2)}) collective-permute-start(bf16[64,2048]{1,0:T(8,128)(2,1)S(1)} %get-tuple-element.42.refs_0_), channel_id=1, source_target_pairs={{0,1},{1,0},{2,3},{3,2},{4,5},{5,4},{6,7},{7,6},{8,9},{9,8},{10,11... | collective-permute-start | bytes 786440 | tf_op jit(solution)/shard_map/ppermute | solution.py:335
  57.1 10.8 %collective-permute-start.8 = (bf16[64,2048]{1,0:T(8,128)(2,1)S(1)}, bf16[64,2048]{1,0:T(8,128)(2,1)S(1)}, u32[]{:S(2)}, u32[]{:S(2)}) collective-permute-start(bf16[64,2048]{1,0:T(8,128)(2,1)S(1)} %get-tuple-element.43.refs_4_.refs_1_), channel_id=1, source_target_pairs={{0,1},{1,0},{2,3},{3,2},{4,5},{5,4},{6,7},{7,6},{8,9},{9,8},{10,11... | collective-permute-start | bytes 786440 | tf_op jit(solution)/shard_map/ppermute | solution.py:335
  65.2 11.6 %collective-permute-start.11 = (bf16[48,3072]{1,0:T(8,128)(2,1)S(1)}, bf16[48,3072]{1,0:T(8,128)(2,1)S(1)}, u32[]{:S(2)}, u32[]{:S(2)}) collective-permute-start(bf16[48,3072]{1,0:T(8,128)(2,1)S(1)} %get-tuple-element.46), channel_id=1, source_target_pairs={{16,0},{24,8},{0,16},{8,24},{17,1},{25,9},{1,17},{9,25},{18,2},{26... | collective-permute-start | bytes 884744 | tf_op jit(solution)/shard_map/ppermute | solution.py:65
  67.8 9.9 %collective-permute-start.12 = (bf16[48,3072]{1,0:T(8,128)(2,1)S(1)}, bf16[48,3072]{1,0:T(8,128)(2,1)S(1)}, u32[]{:S(2)}, u32[]{:S(2)}) collective-permute-start(bf16[48,3072]{1,0:T(8,128)(2,1)S(1)} %get-tuple-element.47.refs_5_), channel_id=1, source_target_pairs={{8,0},{0,8},{24,16},{16,24},{9,1},{1,9},{25,17},{17,25},{10,2},{2,... | collective-permute-start | bytes 884744 | tf_op jit(solution)/shard_map/ppermute | solution.py:65
  70.7 19.6 %collective-permute-start.17 = (bf16[96,3072]{1,0:T(8,128)(2,1)S(1)}, bf16[96,3072]{1,0:T(8,128)(2,1)S(1)}, u32[]{:S(2)}, u32[]{:S(2)}) collective-permute-start(bf16[96,3072]{1,0:T(8,128)(2,1)S(1)} %get-tuple-element.58), channel_id=1, source_target_pairs={{8,0},{0,8},{24,16},{16,24},{9,1},{1,9},{25,17},{17,25},{10,2},{2,... | collective-permute-start | bytes 1769480 | tf_op jit(solution)/shard_map/ppermute | solution.py:65
  72.6 17.7 %collective-permute-start.18 = (bf16[96,3072]{1,0:T(8,128)(2,1)S(1)}, bf16[96,3072]{1,0:T(8,128)(2,1)S(1)}, u32[]{:S(2)}, u32[]{:S(2)}) collective-permute-start(bf16[96,3072]{1,0:T(8,128)(2,1)S(1)} %get-tuple-element.50.refs_5_), channel_id=1, source_target_pairs={{16,0},{24,8},{0,16},{8,24},{17,1},{25,9},{1,17},{9,25},{18,2},{26... | collective-permute-start | bytes 1769480 | tf_op jit(solution)/shard_map/ppermute | solution.py:65
  81.2 17.5 %collective-permute-start.15 = (bf16[64,3072]{1,0:T(8,128)(2,1)S(1)}, bf16[64,3072]{1,0:T(8,128)(2,1)S(1)}, u32[]{:S(2)}, u32[]{:S(2)}) collective-permute-start(bf16[64,3072]{1,0:T(8,128)(2,1)S(1)} %get-tuple-element.55), channel_id=1, source_target_pairs={{8,0},{0,8},{24,16},{16,24},{9,1},{1,9},{25,17},{17,25},{10,2},{2,... | collective-permute-start | bytes 1179656 | tf_op jit(solution)/shard_map/ppermute | solution.py:65
  81.5 17.3 %collective-permute-start.16 = (bf16[64,3072]{1,0:T(8,128)(2,1)S(1)}, bf16[64,3072]{1,0:T(8,128)(2,1)S(1)}, u32[]{:S(2)}, u32[]{:S(2)}) collective-permute-start(bf16[64,3072]{1,0:T(8,128)(2,1)S(1)} %get-tuple-element.53.refs_5_), channel_id=1, source_target_pairs={{16,0},{24,8},{0,16},{8,24},{17,1},{25,9},{1,17},{9,25},{18,2},{26... | collective-permute-start | bytes 1179656 | tf_op jit(solution)/shard_map/ppermute | solution.py:65
  90.4 13.8 %collective-permute-start.21 = (bf16[48,3072]{1,0:T(8,128)(2,1)S(1)}, bf16[48,3072]{1,0:T(8,128)(2,1)S(1)}, u32[]{:S(2)}, u32[]{:S(2)}) collective-permute-start(bf16[48,3072]{1,0:T(8,128)(2,1)S(1)} %get-tuple-element.62), channel_id=1, source_target_pairs={{16,0},{24,8},{0,16},{8,24},{17,1},{25,9},{1,17},{9,25},{18,2},{26... | collective-permute-start | bytes 884744 | tf_op jit(solution)/shard_map/ppermute | solution.py:65
  91.9 13.2 %collective-permute-start.22 = (bf16[48,3072]{1,0:T(8,128)(2,1)S(1)}, bf16[48,3072]{1,0:T(8,128)(2,1)S(1)}, u32[]{:S(2)}, u32[]{:S(2)}) collective-permute-start(bf16[48,3072]{1,0:T(8,128)(2,1)S(1)} %get-tuple-element.59.refs_4_), channel_id=1, source_target_pairs={{8,0},{0,8},{24,16},{16,24},{9,1},{1,9},{25,17},{17,25},{10,2},{2,... | collective-permute-start | bytes 884744 | tf_op jit(solution)/shard_map/ppermute | solution.py:65
  98.8 9.2 %collective-permute-start.19 = (bf16[32,3072]{1,0:T(8,128)(2,1)S(1)}, bf16[32,3072]{1,0:T(8,128)(2,1)S(1)}, u32[]{:S(2)}, u32[]{:S(2)}) collective-permute-start(bf16[32,3072]{1,0:T(8,128)(2,1)S(1)} %get-tuple-element.60), channel_id=1, source_target_pairs={{16,0},{24,8},{0,16},{8,24},{17,1},{25,9},{1,17},{9,25},{18,2},{26... | collective-permute-start | bytes 589832 | tf_op jit(solution)/shard_map/ppermute | solution.py:65
  100.3 8.8 %collective-permute-start.20 = (bf16[32,3072]{1,0:T(8,128)(2,1)S(1)}, bf16[32,3072]{1,0:T(8,128)(2,1)S(1)}, u32[]{:S(2)}, u32[]{:S(2)}) collective-permute-start(bf16[32,3072]{1,0:T(8,128)(2,1)S(1)} %get-tuple-element.61.refs_9_), channel_id=1, source_target_pairs={{8,0},{0,8},{24,16},{16,24},{9,1},{1,9},{25,17},{17,25},{10,2},{2,... | collective-permute-start | bytes 589832 | tf_op jit(solution)/shard_map/ppermute | solution.py:65
  100.3 7.7 %collective-permute-start.23 = (bf16[16,3072]{1,0:T(8,128)(2,1)S(1)}, bf16[16,3072]{1,0:T(8,128)(2,1)S(1)}, u32[]{:S(2)}, u32[]{:S(2)}) collective-permute-start(bf16[16,3072]{1,0:T(8,128)(2,1)S(1)} %get-tuple-element.52.refs_5_), channel_id=1, source_target_pairs={{0,8},{8,16},{16,24},{1,9},{9,17},{17,25},{2,10},{10,18},{18,26},{... | collective-permute-start | bytes 294920 | tf_op jit(solution)/shard_map/ppermute | solution.py:349
  (2 other events, 10.1 us)

commit v6 on v5

--- a/solution.py
+++ b/solution.py
@@ -105,14 +105,14 @@
         return row * cols + plane * CORES + core
 
     blocks = []
-    for a in range(count // CORES):
+    for a in reversed(range(count // CORES)):
         route = []
         for row in range(count):
             for plane in range(planes):
                 for core in range(CORES):
                     route.append((place(row, plane, core), place(plane, row ^ (core * (count // CORES) + a), core)))
         blocks.append(lax.ppermute(piece, ("row", "col"), route))
-    return blocks
+    return blocks[::-1]
 
 
 def cut_kernel(sizes, count, *refs):

time: 112 us -> 112 us (level)
  no operation moved by 1% of the time
where the time goes in v6:
time: 112 us; the launch traced here: 111 us
  starting transfers between devices  49.8 us (44%)
  waiting for transfers between devices  34.9 us (31%)
  Pallas kernels  26.3 us (23%)
    ppermute x12, waiting for transfers between devices, shift_rows(): return lax.ppermute(block, 'row', route)  27 us
    pallas_call x16, Pallas kernels, call(): pl.pallas_call(body, in_specs=specs + [HBM] * len(extra), out_specs=[HBM...  26.3 us
    ppermute x12, starting transfers between devices, shift_rows(): return lax.ppermute(block, 'row', route)  20.4 us
    ppermute x4, starting transfers between devices, gather(): blocks.append(lax.ppermute(piece, ('row', 'col'), route))  13.9 us
    ppermute x6, starting transfers between devices, per_device(): other[i] = [lax.ppermute(b, 'col', swap) for b in mine[i]]  11.2 us
    ppermute x4, waiting for transfers between devices, gather(): blocks.append(lax.ppermute(piece, ('row', 'col'), route))  4.85 us
    ppermute x1, starting transfers between devices, per_device(): lax.ppermute(made.pop(0), 'row', [(r, r + 1) for r in range(count - 1)])  3.92 us
  transfers between devices with their start and end apart: 24, of which 10 were waited for; matrix products, arithmetic and copies ran while one was open for 0% of the time, Pallas kernels for 14%

profile of v6, /device:TPU:0, one launch (start us, length us, event | category | flops | bytes accessed | tf_op | source)
XLA Modules:
  0.0 111.3 jit_solution(2436230867520217809)
XLA Ops:
  0.5 1.7 %collective-permute-done.refs_1_ = bf16[256,1024]{1,0:T(8,128)(2,1)S(1)} collective-permute-done((bf16[256,1024]{1,0:T(8,128)(2,1)}, bf16[256,1024]{1,0:T(8,128)(2,1)S(1)}, u32[]{:S(2)}, u32[]{:S(2)}) %collective-permute-start) | collective-permute-done | bytes 524320 | tf_op jit(solution)/shard_map/ppermute | solution.py:322
  4.0 5.6 %collective-permute-start.4 = (bf16[96,2048]{1,0:T(8,128)(2,1)S(1)}, bf16[96,2048]{1,0:T(8,128)(2,1)S(1)}, u32[]{:S(2)}, u32[]{:S(2)}) collective-permute-start(bf16[96,2048]{1,0:T(8,128)(2,1)S(1)} %get-tuple-element.37), channel_id=1, source_target_pairs={{0,2},{1,7},{2,10},{3,15},{4,18},{5,23},{6,26},{7,31},{8,0},{9,5},... | collective-permute-start | bytes 1179656 | tf_op jit(solution)/shard_map/ppermute | solution.py:114
  9.6 4.7 %fetch_w.1.refs_2_.refs_4_ = bf16[3,2048,1024]{2,1,0:T(8,128)(2,1)S(1)} custom-call(bf16[3,2048,1024]{2,1,0:T(8,128)(2,1)} %bitcast.5, bf16[160,2048]{1,0:T(8,128)(2,1)S(1)} %get-tuple-element.36.refs_1_), custom_call_target="tpu_custom_call" | custom-call | tf_op jit(solution)/shard_map/fetch_w/pallas_call | solution.py:38
  14.3 4.8 %collective-permute-done.4.refs_1_ = bf16[96,2048]{1,0:T(8,128)(2,1)S(1)} collective-permute-done((bf16[96,2048]{1,0:T(8,128)(2,1)S(1)}, bf16[96,2048]{1,0:T(8,128)(2,1)S(1)}, u32[]{:S(2)}, u32[]{:S(2)}) %collective-permute-start.4) | collective-permute-done | bytes 393248 | tf_op jit(solution)/shard_map/ppermute | solution.py:114
  19.2 3.1 %collective-permute-start.5 = (bf16[96,2048]{1,0:T(8,128)(2,1)S(1)}, bf16[96,2048]{1,0:T(8,128)(2,1)S(1)}, u32[]{:S(2)}, u32[]{:S(2)}) collective-permute-start(bf16[96,2048]{1,0:T(8,128)(2,1)S(1)} %get-tuple-element.38.refs_0_), channel_id=1, source_target_pairs={{0,1},{1,0},{2,3},{3,2},{4,5},{5,4},{6,7},{7,6},{8,9},{9,8},{10,11... | collective-permute-start | bytes 1179656 | tf_op jit(solution)/shard_map/ppermute | solution.py:335
  23.1 6.9 %collective-permute-start.2 = (bf16[160,2048]{1,0:T(8,128)(2,1)S(1)}, bf16[160,2048]{1,0:T(8,128)(2,1)S(1)}, u32[]{:S(2)}, u32[]{:S(2)}) collective-permute-start(bf16[160,2048]{1,0:T(8,128)(2,1)S(1)} %get-tuple-element.36.refs_1_), channel_id=1, source_target_pairs={{0,2},{1,7},{2,10},{3,15},{4,18},{5,23},{6,26},{7,31},{8,0},{9,5},... | collective-permute-start | bytes 1966088 | tf_op jit(solution)/shard_map/ppermute | solution.py:114
  30.0 2.8 %send.3 = (bf16[96,3072]{1,0:T(8,128)(2,1)S(1)}, bf16[96,3072]{1,0:T(8,128)(2,1)S(1)}) custom-call(bf16[96,2048]{1,0:T(8,128)(2,1)S(1)} %get-tuple-element.38.refs_0_, bf16[96,2048]{1,0:T(8,128)(2,1)S(1)} %get-tuple-element.39.refs_1_.refs_5_, bf16[96,2048]{1,0:T(8,128)(2,1)S(1)} %collective-permute-done.5.refs_2_, ...), custom_call_target="tpu_custom_call" | custom-call | tf_op jit(solution)/shard_map/send/pallas_call | solution.py:38
  34.3 8.3 %collective-permute-start.10 = (bf16[96,3072]{1,0:T(8,128)(2,1)S(1)}, bf16[96,3072]{1,0:T(8,128)(2,1)S(1)}, u32[]{:S(2)}, u32[]{:S(2)}) collective-permute-start(bf16[96,3072]{1,0:T(8,128)(2,1)S(1)} %get-tuple-element.40.refs_5_), channel_id=1, source_target_pairs={{16,0},{24,8},{0,16},{8,24},{17,1},{25,9},{1,17},{9,25},{18,2},{26... | collective-permute-start | bytes 1769480 | tf_op jit(solution)/shard_map/ppermute | solution.py:65
  42.6 2.7 %keep.3 = (f32[96,3072]{1,0:T(8,128)S(1)}, f32[96,3072]{1,0:T(8,128)S(1)}) custom-call(bf16[96,2048]{1,0:T(8,128)(2,1)S(1)} %get-tuple-element.38.refs_0_, bf16[96,2048]{1,0:T(8,128)(2,1)S(1)} %get-tuple-element.39.refs_1_.refs_5_, bf16[96,2048]{1,0:T(8,128)(2,1)S(1)} %collective-permute-done.5.refs_2_, bf16[96,2048]{1,0:T(8,128)(2,1)S(1)} %collective-permute-done.6.refs_3_, ...), custom_call_target="tpu_custom_call" | custom-call | flops 10000000000 | tf_op jit(solution)/shard_map/keep/pallas_call | solution.py:38
  45.4 7.4 %collective-permute-start.13 = (bf16[96,2048]{1,0:T(8,128)(2,1)S(1)}, bf16[96,2048]{1,0:T(8,128)(2,1)S(1)}, u32[]{:S(2)}, u32[]{:S(2)}) collective-permute-start(bf16[96,2048]{1,0:T(8,128)(2,1)S(1)} %get-tuple-element.48.refs_0_), channel_id=1, source_target_pairs={{0,1},{1,0},{2,3},{3,2},{4,5},{5,4},{6,7},{7,6},{8,9},{9,8},{10,11... | collective-permute-start | bytes 1179656 | tf_op jit(solution)/shard_map/ppermute | solution.py:335
  53.3 3.8 %collective-permute-done.9.refs_1_ = bf16[96,3072]{1,0:T(8,128)(2,1)S(1)} collective-permute-done((bf16[96,3072]{1,0:T(8,128)(2,1)S(1)}, bf16[96,3072]{1,0:T(8,128)(2,1)S(1)}, u32[]{:S(2)}, u32[]{:S(2)}) %collective-permute-start.9) | collective-permute-done | bytes 589856 | tf_op jit(solution)/shard_map/ppermute | solution.py:65
  57.3 7.9 %collective-permute-done.10.refs_3_.refs_4_ = bf16[96,3072]{1,0:T(8,128)(2,1)S(1)} collective-permute-done((bf16[96,3072]{1,0:T(8,128)(2,1)S(1)}, bf16[96,3072]{1,0:T(8,128)(2,1)S(1)}, u32[]{:S(2)}, u32[]{:S(2)}) %collective-permute-start.10) | collective-permute-done | bytes 589856 | tf_op jit(solution)/shard_map/ppermute | solution.py:65
  65.2 2.5 %collective-permute-start.11 = (bf16[48,3072]{1,0:T(8,128)(2,1)S(1)}, bf16[48,3072]{1,0:T(8,128)(2,1)S(1)}, u32[]{:S(2)}, u32[]{:S(2)}) collective-permute-start(bf16[48,3072]{1,0:T(8,128)(2,1)S(1)} %get-tuple-element.46), channel_id=1, source_target_pairs={{16,0},{24,8},{0,16},{8,24},{17,1},{25,9},{1,17},{9,25},{18,2},{26... | collective-permute-start | bytes 884744 | tf_op jit(solution)/shard_map/ppermute | solution.py:65
  68.0 2.7 %send.4 = (bf16[96,3072]{1,0:T(8,128)(2,1)S(1)}, bf16[96,3072]{1,0:T(8,128)(2,1)S(1)}) custom-call(bf16[96,2048]{1,0:T(8,128)(2,1)S(1)} %get-tuple-element.48.refs_0_, bf16[96,2048]{1,0:T(8,128)(2,1)S(1)} %get-tuple-element.49.refs_1_, bf16[96,2048]{1,0:T(8,128)(2,1)S(1)} %collective-permute-done.13.refs_2_, ...), custom_call_target="tpu_custom_call" | custom-call | tf_op jit(solution)/shard_map/send/pallas_call | solution.py:38
  70.7 1.9 %collective-permute-start.17 = (bf16[96,3072]{1,0:T(8,128)(2,1)S(1)}, bf16[96,3072]{1,0:T(8,128)(2,1)S(1)}, u32[]{:S(2)}, u32[]{:S(2)}) collective-permute-start(bf16[96,3072]{1,0:T(8,128)(2,1)S(1)} %get-tuple-element.58), channel_id=1, source_target_pairs={{8,0},{0,8},{24,16},{16,24},{9,1},{1,9},{25,17},{17,25},{10,2},{2,... | collective-permute-start | bytes 1769480 | tf_op jit(solution)/shard_map/ppermute | solution.py:65
  74.1 2.7 %keep.4 = (f32[96,3072]{1,0:T(8,128)S(1)}, f32[96,3072]{1,0:T(8,128)S(1)}) custom-call(bf16[96,2048]{1,0:T(8,128)(2,1)S(1)} %get-tuple-element.48.refs_0_, bf16[96,2048]{1,0:T(8,128)(2,1)S(1)} %get-tuple-element.49.refs_1_, bf16[96,2048]{1,0:T(8,128)(2,1)S(1)} %collective-permute-done.13.refs_2_, bf16[96,2048]{1,0:T(8,128)(2,1)S(1)} %collective-permute-done.14.refs_3_, ...), custom_call_target="tpu_custom_call" | custom-call | flops 10000000000 | tf_op jit(solution)/shard_map/keep/pallas_call | solution.py:38
  77.7 1.7 %finish.3 = (bf16[80,1024]{1,0:T(8,128)(2,1)S(1)}, f32[16,3072]{1,0:T(8,128)S(1)}, bf16[16,3072]{1,0:T(8,128)(2,1)S(1)}) custom-call(f32[96,3072]{1,0:T(8,128)S(1)} %get-tuple-element.44.refs_0_, bf16[96,3072]{1,0:T(8,128)(2,1)S(1)} %collective-permute-done.9.refs_1_, bf16[48,3072]{1,0:T(8,128)(2,1)S(1)} %collective-permute-done.11.refs_2_, ...), custom_call_target="tpu_custom_call" | custom-call | flops 10000000000 | tf_op jit(solution)/shard_map/finish/pallas_call | solution.py:38
  79.3 1.9 %send.5 = (bf16[64,3072]{1,0:T(8,128)(2,1)S(1)}, bf16[64,3072]{1,0:T(8,128)(2,1)S(1)}) custom-call(bf16[64,2048]{1,0:T(8,128)(2,1)S(1)} %get-tuple-element.42.refs_0_, bf16[64,2048]{1,0:T(8,128)(2,1)S(1)} %get-tuple-element.43.refs_4_.refs_1_, bf16[64,2048]{1,0:T(8,128)(2,1)S(1)} %collective-permute-done.7.refs_6_.refs_2_, ...), custom_call_target="tpu_custom_call" | custom-call | tf_op jit(solution)/shard_map/send/pallas_call | solution.py:38
  82.8 1.9 %keep.5 = (f32[64,3072]{1,0:T(8,128)S(1)}, f32[64,3072]{1,0:T(8,128)S(1)}) custom-call(bf16[64,2048]{1,0:T(8,128)(2,1)S(1)} %get-tuple-element.42.refs_0_, bf16[64,2048]{1,0:T(8,128)(2,1)S(1)} %get-tuple-element.43.refs_4_.refs_1_, bf16[64,2048]{1,0:T(8,128)(2,1)S(1)} %collective-permute-done.7.refs_6_.refs_2_, ...), custom_call_target="tpu_custom_call" | custom-call | flops 10000000000 | tf_op jit(solution)/shard_map/keep/pallas_call | solution.py:38
  84.7 5.7 %collective-permute-done.17.refs_1_ = bf16[96,3072]{1,0:T(8,128)(2,1)S(1)} collective-permute-done((bf16[96,3072]{1,0:T(8,128)(2,1)S(1)}, bf16[96,3072]{1,0:T(8,128)(2,1)S(1)}, u32[]{:S(2)}, u32[]{:S(2)}) %collective-permute-start.17) | collective-permute-done | bytes 589856 | tf_op jit(solution)/shard_map/ppermute | solution.py:65
  91.9 6.8 %collective-permute-done.15.refs_1_ = bf16[64,3072]{1,0:T(8,128)(2,1)S(1)} collective-permute-done((bf16[64,3072]{1,0:T(8,128)(2,1)S(1)}, bf16[64,3072]{1,0:T(8,128)(2,1)S(1)}, u32[]{:S(2)}, u32[]{:S(2)}) %collective-permute-start.15) | collective-permute-done | bytes 393248 | tf_op jit(solution)/shard_map/ppermute | solution.py:65
  100.3 3.9 %collective-permute-start.23 = (bf16[16,3072]{1,0:T(8,128)(2,1)S(1)}, bf16[16,3072]{1,0:T(8,128)(2,1)S(1)}, u32[]{:S(2)}, u32[]{:S(2)}) collective-permute-start(bf16[16,3072]{1,0:T(8,128)(2,1)S(1)} %get-tuple-element.52.refs_5_), channel_id=1, source_target_pairs={{0,8},{8,16},{16,24},{1,9},{9,17},{17,25},{2,10},{10,18},{18,26},{... | collective-permute-start | bytes 294920 | tf_op jit(solution)/shard_map/ppermute | solution.py:349
  105.1 1.7 %finish.4 = (bf16[96,1024]{1,0:T(8,128)(2,1)S(1)}, f32[16,3072]{1,0:T(8,128)S(1)}) custom-call(f32[96,3072]{1,0:T(8,128)S(1)} %get-tuple-element.57.refs_0_, bf16[96,3072]{1,0:T(8,128)(2,1)S(1)} %collective-permute-done.17.refs_1_, bf16[48,3072]{1,0:T(8,128)(2,1)S(1)} %collective-permute-done.21.refs_2_, ...), custom_call_target="tpu_custom_call" | custom-call | tf_op jit(solution)/shard_map/finish/pallas_call | solution.py:38
  109.1 2.0 %finish.5 = bf16[256,1024]{1,0:T(8,128)(2,1)} custom-call(f32[64,3072]{1,0:T(8,128)S(1)} %get-tuple-element.54.refs_0_, bf16[64,3072]{1,0:T(8,128)(2,1)S(1)} %collective-permute-done.15.refs_1_, bf16[32,3072]{1,0:T(8,128)(2,1)S(1)} %collective-permute-done.19.refs_2_, f32[64,3072]{1,0:T(8,128)S(1)} %get-tuple-element.56.refs_4_.refs_2_.refs_3_, ...), custom_call_target="tpu_custom_call" | custom-call | tf_op jit(solution)/shard_map/finish/pallas_call | solution.py:38
  (44 shorter events, 15.8 us)
Async XLA Ops:
  0.0 2.2 %collective-permute-start = (bf16[256,1024]{1,0:T(8,128)(2,1)}, bf16[256,1024]{1,0:T(8,128)(2,1)S(1)}, u32[]{:S(2)}, u32[]{:S(2)}) collective-permute-start(bf16[256,1024]{1,0:T(8,128)(2,1)} %refs_0_.1), channel_id=1, source_target_pairs={{0,1},{1,0},{2,3},{3,2},{4,5},{5,4},{6,7},{7,6},{8,9},{9,8},{10,11... | collective-permute-start | bytes 1572872 | tf_op jit(solution)/shard_map/ppermute | solution.py:322
  3.3 11.0 %collective-permute-start.3 = (bf16[96,2048]{1,0:T(8,128)(2,1)S(1)}, bf16[96,2048]{1,0:T(8,128)(2,1)S(1)}, u32[]{:S(2)}, u32[]{:S(2)}) collective-permute-start(bf16[96,2048]{1,0:T(8,128)(2,1)S(1)} %get-tuple-element.37), channel_id=1, source_target_pairs={{0,0},{1,5},{2,8},{3,13},{4,16},{5,21},{6,24},{7,29},{8,2},{9,7},{... | collective-permute-start | bytes 1179656 | tf_op jit(solution)/shard_map/ppermute | solution.py:114
  4.0 15.1 %collective-permute-start.4 = (bf16[96,2048]{1,0:T(8,128)(2,1)S(1)}, bf16[96,2048]{1,0:T(8,128)(2,1)S(1)}, u32[]{:S(2)}, u32[]{:S(2)}) collective-permute-start(bf16[96,2048]{1,0:T(8,128)(2,1)S(1)} %get-tuple-element.37), channel_id=1, source_target_pairs={{0,2},{1,7},{2,10},{3,15},{4,18},{5,23},{6,26},{7,31},{8,0},{9,5},... | collective-permute-start | bytes 1179656 | tf_op jit(solution)/shard_map/ppermute | solution.py:114
  19.2 10.8 %collective-permute-start.5 = (bf16[96,2048]{1,0:T(8,128)(2,1)S(1)}, bf16[96,2048]{1,0:T(8,128)(2,1)S(1)}, u32[]{:S(2)}, u32[]{:S(2)}) collective-permute-start(bf16[96,2048]{1,0:T(8,128)(2,1)S(1)} %get-tuple-element.38.refs_0_), channel_id=1, source_target_pairs={{0,1},{1,0},{2,3},{3,2},{4,5},{5,4},{6,7},{7,6},{8,9},{9,8},{10,11... | collective-permute-start | bytes 1179656 | tf_op jit(solution)/shard_map/ppermute | solution.py:335
  22.3 7.7 %collective-permute-start.6 = (bf16[96,2048]{1,0:T(8,128)(2,1)S(1)}, bf16[96,2048]{1,0:T(8,128)(2,1)S(1)}, u32[]{:S(2)}, u32[]{:S(2)}) collective-permute-start(bf16[96,2048]{1,0:T(8,128)(2,1)S(1)} %get-tuple-element.39.refs_1_.refs_5_), channel_id=1, source_target_pairs={{0,1},{1,0},{2,3},{3,2},{4,5},{5,4},{6,7},{7,6},{8,9},{9,8},{10,11... | collective-permute-start | bytes 1179656 | tf_op jit(solution)/shard_map/ppermute | solution.py:335
  22.4 23.0 %collective-permute-start.1 = (bf16[160,2048]{1,0:T(8,128)(2,1)S(1)}, bf16[160,2048]{1,0:T(8,128)(2,1)S(1)}, u32[]{:S(2)}, u32[]{:S(2)}) collective-permute-start(bf16[160,2048]{1,0:T(8,128)(2,1)S(1)} %get-tuple-element.36.refs_1_), channel_id=1, source_target_pairs={{0,0},{1,5},{2,8},{3,13},{4,16},{5,21},{6,24},{7,29},{8,2},{9,7},{... | collective-permute-start | bytes 1966088 | tf_op jit(solution)/shard_map/ppermute | solution.py:114
  23.1 22.3 %collective-permute-start.2 = (bf16[160,2048]{1,0:T(8,128)(2,1)S(1)}, bf16[160,2048]{1,0:T(8,128)(2,1)S(1)}, u32[]{:S(2)}, u32[]{:S(2)}) collective-permute-start(bf16[160,2048]{1,0:T(8,128)(2,1)S(1)} %get-tuple-element.36.refs_1_), channel_id=1, source_target_pairs={{0,2},{1,7},{2,10},{3,15},{4,18},{5,23},{6,26},{7,31},{8,0},{9,5},... | collective-permute-start | bytes 1966088 | tf_op jit(solution)/shard_map/ppermute | solution.py:114
  32.8 24.4 %collective-permute-start.9 = (bf16[96,3072]{1,0:T(8,128)(2,1)S(1)}, bf16[96,3072]{1,0:T(8,128)(2,1)S(1)}, u32[]{:S(2)}, u32[]{:S(2)}) collective-permute-start(bf16[96,3072]{1,0:T(8,128)(2,1)S(1)} %get-tuple-element.45), channel_id=1, source_target_pairs={{8,0},{0,8},{24,16},{16,24},{9,1},{1,9},{25,17},{17,25},{10,2},{2,... | collective-permute-start | bytes 1769480 | tf_op jit(solution)/shard_map/ppermute | solution.py:65
  34.3 30.8 %collective-permute-start.10 = (bf16[96,3072]{1,0:T(8,128)(2,1)S(1)}, bf16[96,3072]{1,0:T(8,128)(2,1)S(1)}, u32[]{:S(2)}, u32[]{:S(2)}) collective-permute-start(bf16[96,3072]{1,0:T(8,128)(2,1)S(1)} %get-tuple-element.40.refs_5_), channel_id=1, source_target_pairs={{16,0},{24,8},{0,16},{8,24},{17,1},{25,9},{1,17},{9,25},{18,2},{26... | collective-permute-start | bytes 1769480 | tf_op jit(solution)/shard_map/ppermute | solution.py:65
  45.4 22.5 %collective-permute-start.13 = (bf16[96,2048]{1,0:T(8,128)(2,1)S(1)}, bf16[96,2048]{1,0:T(8,128)(2,1)S(1)}, u32[]{:S(2)}, u32[]{:S(2)}) collective-permute-start(bf16[96,2048]{1,0:T(8,128)(2,1)S(1)} %get-tuple-element.48.refs_0_), channel_id=1, source_target_pairs={{0,1},{1,0},{2,3},{3,2},{4,5},{5,4},{6,7},{7,6},{8,9},{9,8},{10,11... | collective-permute-start | bytes 1179656 | tf_op jit(solution)/shard_map/ppermute | solution.py:335
  52.8 15.2 %collective-permute-start.14 = (bf16[96,2048]{1,0:T(8,128)(2,1)S(1)}, bf16[96,2048]{1,0:T(8,128)(2,1)S(1)}, u32[]{:S(2)}, u32[]{:S(2)}) collective-permute-start(bf16[96,2048]{1,0:T(8,128)(2,1)S(1)} %get-tuple-element.49.refs_1_), channel_id=1, source_target_pairs={{0,1},{1,0},{2,3},{3,2},{4,5},{5,4},{6,7},{7,6},{8,9},{9,8},{10,11... | collective-permute-start | bytes 1179656 | tf_op jit(solution)/shard_map/ppermute | solution.py:335
  52.9 14.9 %collective-permute-start.7 = (bf16[64,2048]{1,0:T(8,128)(2,1)S(1)}, bf16[64,2048]{1,0:T(8,128)(2,1)S(1)}, u32[]{:S(2)}, u32[]{:S(2)}) collective-permute-start(bf16[64,2048]{1,0:T(8,128)(2,1)S(1)} %get-tuple-element.42.refs_0_), channel_id=1, source_target_pairs={{0,1},{1,0},{2,3},{3,2},{4,5},{5,4},{6,7},{7,6},{8,9},{9,8},{10,11... | collective-permute-start | bytes 786440 | tf_op jit(solution)/shard_map/ppermute | solution.py:335
  57.1 10.8 %collective-permute-start.8 = (bf16[64,2048]{1,0:T(8,128)(2,1)S(1)}, bf16[64,2048]{1,0:T(8,128)(2,1)S(1)}, u32[]{:S(2)}, u32[]{:S(2)}) collective-permute-start(bf16[64,2048]{1,0:T(8,128)(2,1)S(1)} %get-tuple-element.43.refs_4_.refs_1_), channel_id=1, source_target_pairs={{0,1},{1,0},{2,3},{3,2},{4,5},{5,4},{6,7},{7,6},{8,9},{9,8},{10,11... | collective-permute-start | bytes 786440 | tf_op jit(solution)/shard_map/ppermute | solution.py:335
  65.2 11.6 %collective-permute-start.11 = (bf16[48,3072]{1,0:T(8,128)(2,1)S(1)}, bf16[48,3072]{1,0:T(8,128)(2,1)S(1)}, u32[]{:S(2)}, u32[]{:S(2)}) collective-permute-start(bf16[48,3072]{1,0:T(8,128)(2,1)S(1)} %get-tuple-element.46), channel_id=1, source_target_pairs={{16,0},{24,8},{0,16},{8,24},{17,1},{25,9},{1,17},{9,25},{18,2},{26... | collective-permute-start | bytes 884744 | tf_op jit(solution)/shard_map/ppermute | solution.py:65
  67.8 9.9 %collective-permute-start.12 = (bf16[48,3072]{1,0:T(8,128)(2,1)S(1)}, bf16[48,3072]{1,0:T(8,128)(2,1)S(1)}, u32[]{:S(2)}, u32[]{:S(2)}) collective-permute-start(bf16[48,3072]{1,0:T(8,128)(2,1)S(1)} %get-tuple-element.47.refs_5_), channel_id=1, source_target_pairs={{8,0},{0,8},{24,16},{16,24},{9,1},{1,9},{25,17},{17,25},{10,2},{2,... | collective-permute-start | bytes 884744 | tf_op jit(solution)/shard_map/ppermute | solution.py:65
  70.7 19.6 %collective-permute-start.17 = (bf16[96,3072]{1,0:T(8,128)(2,1)S(1)}, bf16[96,3072]{1,0:T(8,128)(2,1)S(1)}, u32[]{:S(2)}, u32[]{:S(2)}) collective-permute-start(bf16[96,3072]{1,0:T(8,128)(2,1)S(1)} %get-tuple-element.58), channel_id=1, source_target_pairs={{8,0},{0,8},{24,16},{16,24},{9,1},{1,9},{25,17},{17,25},{10,2},{2,... | collective-permute-start | bytes 1769480 | tf_op jit(solution)/shard_map/ppermute | solution.py:65
  72.6 17.7 %collective-permute-start.18 = (bf16[96,3072]{1,0:T(8,128)(2,1)S(1)}, bf16[96,3072]{1,0:T(8,128)(2,1)S(1)}, u32[]{:S(2)}, u32[]{:S(2)}) collective-permute-start(bf16[96,3072]{1,0:T(8,128)(2,1)S(1)} %get-tuple-element.50.refs_5_), channel_id=1, source_target_pairs={{16,0},{24,8},{0,16},{8,24},{17,1},{25,9},{1,17},{9,25},{18,2},{26... | collective-permute-start | bytes 1769480 | tf_op jit(solution)/shard_map/ppermute | solution.py:65
  81.2 17.5 %collective-permute-start.15 = (bf16[64,3072]{1,0:T(8,128)(2,1)S(1)}, bf16[64,3072]{1,0:T(8,128)(2,1)S(1)}, u32[]{:S(2)}, u32[]{:S(2)}) collective-permute-start(bf16[64,3072]{1,0:T(8,128)(2,1)S(1)} %get-tuple-element.55), channel_id=1, source_target_pairs={{8,0},{0,8},{24,16},{16,24},{9,1},{1,9},{25,17},{17,25},{10,2},{2,... | collective-permute-start | bytes 1179656 | tf_op jit(solution)/shard_map/ppermute | solution.py:65
  81.5 17.3 %collective-permute-start.16 = (bf16[64,3072]{1,0:T(8,128)(2,1)S(1)}, bf16[64,3072]{1,0:T(8,128)(2,1)S(1)}, u32[]{:S(2)}, u32[]{:S(2)}) collective-permute-start(bf16[64,3072]{1,0:T(8,128)(2,1)S(1)} %get-tuple-element.53.refs_5_), channel_id=1, source_target_pairs={{16,0},{24,8},{0,16},{8,24},{17,1},{25,9},{1,17},{9,25},{18,2},{26... | collective-permute-start | bytes 1179656 | tf_op jit(solution)/shard_map/ppermute | solution.py:65
  90.4 13.8 %collective-permute-start.21 = (bf16[48,3072]{1,0:T(8,128)(2,1)S(1)}, bf16[48,3072]{1,0:T(8,128)(2,1)S(1)}, u32[]{:S(2)}, u32[]{:S(2)}) collective-permute-start(bf16[48,3072]{1,0:T(8,128)(2,1)S(1)} %get-tuple-element.62), channel_id=1, source_target_pairs={{16,0},{24,8},{0,16},{8,24},{17,1},{25,9},{1,17},{9,25},{18,2},{26... | collective-permute-start | bytes 884744 | tf_op jit(solution)/shard_map/ppermute | solution.py:65
  91.9 13.2 %collective-permute-start.22 = (bf16[48,3072]{1,0:T(8,128)(2,1)S(1)}, bf16[48,3072]{1,0:T(8,128)(2,1)S(1)}, u32[]{:S(2)}, u32[]{:S(2)}) collective-permute-start(bf16[48,3072]{1,0:T(8,128)(2,1)S(1)} %get-tuple-element.59.refs_4_), channel_id=1, source_target_pairs={{8,0},{0,8},{24,16},{16,24},{9,1},{1,9},{25,17},{17,25},{10,2},{2,... | collective-permute-start | bytes 884744 | tf_op jit(solution)/shard_map/ppermute | solution.py:65
  98.8 9.2 %collective-permute-start.19 = (bf16[32,3072]{1,0:T(8,128)(2,1)S(1)}, bf16[32,3072]{1,0:T(8,128)(2,1)S(1)}, u32[]{:S(2)}, u32[]{:S(2)}) collective-permute-start(bf16[32,3072]{1,0:T(8,128)(2,1)S(1)} %get-tuple-element.60), channel_id=1, source_target_pairs={{16,0},{24,8},{0,16},{8,24},{17,1},{25,9},{1,17},{9,25},{18,2},{26... | collective-permute-start | bytes 589832 | tf_op jit(solution)/shard_map/ppermute | solution.py:65
  100.3 8.8 %collective-permute-start.20 = (bf16[32,3072]{1,0:T(8,128)(2,1)S(1)}, bf16[32,3072]{1,0:T(8,128)(2,1)S(1)}, u32[]{:S(2)}, u32[]{:S(2)}) collective-permute-start(bf16[32,3072]{1,0:T(8,128)(2,1)S(1)} %get-tuple-element.61.refs_9_), channel_id=1, source_target_pairs={{8,0},{0,8},{24,16},{16,24},{9,1},{1,9},{25,17},{17,25},{10,2},{2,... | collective-permute-start | bytes 589832 | tf_op jit(solution)/shard_map/ppermute | solution.py:65
  100.3 7.7 %collective-permute-start.23 = (bf16[16,3072]{1,0:T(8,128)(2,1)S(1)}, bf16[16,3072]{1,0:T(8,128)(2,1)S(1)}, u32[]{:S(2)}, u32[]{:S(2)}) collective-permute-start(bf16[16,3072]{1,0:T(8,128)(2,1)S(1)} %get-tuple-element.52.refs_5_), channel_id=1, source_target_pairs={{0,8},{8,16},{16,24},{1,9},{9,17},{17,25},{2,10},{10,18},{18,26},{... | collective-permute-start | bytes 294920 | tf_op jit(solution)/shard_map/ppermute | solution.py:349
  (2 other events, 10.1 us)
